TPU v7x, 256 devices: a whole 4x4x8 slice. The times are simulated.
256 devices in a mesh: section: 16 (over x_hi, z), dp: 16 (over x_lo, y, core).
Axes of the slice: x: 4 (x_hi: 2, x_lo: 2; x = x_hi * 2 + x_lo), y: 4, z: 8, core: 2. Of those that a mesh axis runs over, the one named last changes fastest.
Arguments:
- saved_inputs: bfloat16 [16, 32, 256, 2560], P('section', 'dp'), may hold values from -20 to 20
- query_gains: float32 [16, 2560], P('section'), may hold values from 0.5 to 1.5
- cache_slots: bfloat16 [16, 32, 256, 1024], P('section', 'dp'), may hold values from -4 to 4
- segment_ids: int32 [32, 256], P('dp'), may hold values from 0 to 4, as said below
- output_grad: bfloat16 [32, 256, 2560], P('dp'), may hold values from -6 to 6
Outputs:
- layer_grads: bfloat16 [16, 32, 256, 2560], P('section', 'dp')
- cache_grad: bfloat16 [32, 256, 1024], P('dp')
- gain_grads: float32 [16, 2560], P('section')
Inputs may be any that keep to these rules, and one draw needn't show every extreme that they name: `segment_ids`: along each row the ids start at 0, never fall, rise by at most one and end at 4; every segment begins at an even position.
All inputs are finite; a program needn't handle non-finite values.
Results may differ from a plain program's by a relative error of at most 0.0092.
Values may be sent and summed in bfloat16 or wider, within the bound.
No kernel may reach another device: no remote copies, remote signals or barrier semaphores. Data moves between devices by JAX's collectives and lax.ppermute only.
A program may use at most 128 MiB of HBM per device.

v0:
```python
import jax
import jax.numpy as jnp
from jax import lax
from jax.sharding import PartitionSpec as P

HEADS = 20
KV_HEADS = 4
HEAD = 128


def spread(array, axis, root):
    mine = lax.axis_index(axis) == root
    return lax.psum(jnp.where(mine, array, jnp.zeros_like(array)), axis)


def passed_along(array, axis, by):
    peers = lax.axis_size(axis)
    pairs = [(i, i + by) for i in range(peers) if 0 <= i + by < peers]
    return lax.ppermute(array, axis, pairs)


def rows_backward(saved_rows, gain_row, cache_rows, grad_rows, segment_row, row_start):
    row_count, feature_width = saved_rows.shape
    length = cache_rows.shape[0]
    key_width = cache_rows.shape[1] // 2
    group = HEADS // KV_HEADS
    score_scale = HEAD ** (-0.5)
    queries = (saved_rows.astype(jnp.float32) * gain_row).astype(jnp.bfloat16)
    query_heads = queries.reshape(row_count, KV_HEADS, group, HEAD)
    key_heads = cache_rows[:, :key_width].reshape(length, KV_HEADS, HEAD)
    value_heads = cache_rows[:, key_width:].reshape(length, KV_HEADS, HEAD)
    grad_heads = grad_rows.reshape(row_count, KV_HEADS, group, HEAD)
    scores = (
        jnp.einsum("qkgd,tkd->kgqt", query_heads, key_heads, preferred_element_type=jnp.float32)
        * score_scale
    )
    query_pos = row_start + jnp.arange(row_count)
    key_pos = jnp.arange(length)
    allowed = (query_pos[:, None] >= key_pos[None, :]) & (
        segment_row[:, None] == segment_row[None, :]
    )
    scores = jnp.where(allowed, scores, -jnp.inf)
    row_max = jnp.max(scores, axis=-1, keepdims=True)
    exp_terms = jnp.exp(scores - row_max)
    attn_probs = exp_terms / jnp.sum(exp_terms, axis=-1, keepdims=True)
    dprob = jnp.einsum(
        "qkgd,tkd->kgqt", grad_heads, value_heads, preferred_element_type=jnp.float32
    )
    row_delta = jnp.sum(attn_probs * dprob, axis=-1, keepdims=True)
    dscore_round = (attn_probs * (dprob - row_delta)).astype(jnp.bfloat16)
    probs_round = attn_probs.astype(jnp.bfloat16)
    dvalues = jnp.einsum(
        "kgqt,qkgd->tkd", probs_round, grad_heads, preferred_element_type=jnp.float32
    )
    dquery = (
        jnp.einsum("kgqt,tkd->qkgd", dscore_round, key_heads, preferred_element_type=jnp.float32)
        * score_scale
    )
    dkeys = (
        jnp.einsum("kgqt,qkgd->tkd", dscore_round, query_heads, preferred_element_type=jnp.float32)
        * score_scale
    )
    dquery_flat = dquery.reshape(row_count, feature_width)
    grad_next = (grad_rows.astype(jnp.float32) + gain_row * dquery_flat).astype(jnp.bfloat16)
    gain_part = jnp.sum(dquery_flat * saved_rows.astype(jnp.float32), axis=0)
    cache_part = jnp.concatenate(
        [dkeys.reshape(length, key_width), dvalues.reshape(length, key_width)], axis=1
    )
    return (grad_next, cache_part, gain_part)


def on_device(saved_inputs, query_gains, cache_slots, segment_ids, output_grad):
    section_count = lax.axis_size("section")
    section_index = lax.axis_index("section")
    saved_local = saved_inputs[0]
    gain_row = query_gains[0]
    shared_cache = spread(cache_slots[0], "section", 0)
    micro_count, length, feature_width = saved_local.shape
    cache_width = shared_cache.shape[2]
    pieces = 1
    row_count = length // pieces
    unit_count = micro_count * pieces
    tick_count = section_count + unit_count - 1

    def tick(carry, tick_index):
        incoming, grads_done, cache_total, gain_total = carry
        work_unit = tick_index - (section_count - 1 - section_index)
        active = (work_unit >= 0) & (work_unit < unit_count)
        safe_unit = jnp.clip(work_unit, 0, unit_count - 1)
        micro_index = safe_unit // pieces
        row_start = safe_unit % pieces * row_count
        zero_index = jnp.int32(0)
        top_rows = lax.dynamic_slice(
            output_grad, (micro_index, row_start, zero_index), (1, row_count, feature_width)
        )[0]
        grad_rows = jnp.where(section_index == section_count - 1, top_rows, incoming)

        def run_rows(unused):
            saved_rows = lax.dynamic_slice(
                saved_local, (micro_index, row_start, zero_index), (1, row_count, feature_width)
            )[0]
            cache_rows = lax.dynamic_index_in_dim(shared_cache, micro_index, 0, keepdims=False)
            segment_row = lax.dynamic_index_in_dim(segment_ids, micro_index, 0, keepdims=False)
            return rows_backward(
                saved_rows, gain_row, cache_rows, grad_rows, segment_row, row_start
            )

        def skip_rows(unused):
            return (
                jnp.zeros((row_count, feature_width), jnp.bfloat16),
                jnp.zeros((length, cache_width), jnp.float32),
                jnp.zeros((feature_width,), jnp.float32),
            )

        grad_next, cache_part, gain_part = lax.cond(active, run_rows, skip_rows, None)
        previous = lax.dynamic_slice(
            grads_done, (micro_index, row_start, zero_index), (1, row_count, feature_width)
        )
        grads_done = lax.dynamic_update_slice(
            grads_done,
            jnp.where(active, grad_next[None], previous),
            (micro_index, row_start, zero_index),
        )
        cache_old = lax.dynamic_slice(
            cache_total, (micro_index, zero_index, zero_index), (1, length, cache_width)
        )
        cache_total = lax.dynamic_update_slice(
            cache_total, cache_old + cache_part[None], (micro_index, zero_index, zero_index)
        )
        gain_total = gain_total + gain_part
        sent_down = passed_along(grad_next, "section", -1)
        return ((sent_down, grads_done, cache_total, gain_total), None)

    start_carry = (
        jnp.zeros((row_count, feature_width), jnp.bfloat16),
        jnp.zeros((micro_count, length, feature_width), jnp.bfloat16),
        jnp.zeros((micro_count, length, cache_width), jnp.float32),
        jnp.zeros((feature_width,), jnp.float32),
    )
    final_carry, unused_out = lax.scan(tick, start_carry, jnp.arange(tick_count, dtype=jnp.int32))
    layer_out = final_carry[1][None]
    cache_total = final_carry[2]
    gain_total = final_carry[3]
    cache_grad = lax.psum(cache_total, "section").astype(jnp.bfloat16)
    gain_grads = lax.psum(gain_total, "dp")
    return (layer_out, cache_grad, gain_grads[None])


def solution(mesh):
    return jax.shard_map(
        on_device,
        mesh=mesh,
        in_specs=(
            P("section", "dp", None, None),
            P("section", None),
            P("section", "dp", None, None),
            P("dp", None),
            P("dp", None, None),
        ),
        out_specs=(P("section", "dp", None, None), P("dp", None, None), P("section", None)),
        check_vma=False,
    )
```

profile of v0, /device:TPU:8, one launch (start us, length us, event | category | flops | bytes accessed | tf_op | source)
XLA Modules:
  0.0 1048.0 jit_solution(5711696078965415812)
XLA Ops:
  7.2 1.5 copy.25
  9.8 4.5 copy.27
  14.4 2.6 copy.26
  17.0 155.6 %all-reduce.3.cloned.1.call-done = bf16[2,256,1024]{1,2,0:T(8,128)(2,1)} async-done(((bf16[2,256,1024]{1,2,0:T(8,128)(2,1)}), bf16[2,256,1024]{1,2,0:T(8,128)(2,1)}) %all-reduce.3.cloned.1.call-update) | async-done | bytes 1048592 | tf_op jit(solution)/shard_map/psum | solution.py:13
  173.8 1.7 broadcast_in_dim.50.clone
  175.4 1.6 broadcast_in_dim.51.clone
  177.0 726.4 %while.19 = (s32[]{:T(128)}, bf16[256,2560]{0,1:T(8,128)(2,1)}, bf16[2,256,2560]{2,1,0:T(8,128)(2,1)}, f32[2,256,1024]{2,1,0:T(8,128)}, f32[2560]{0:T(1024)S(1)}...) while((s32[]{:T(128)}, bf16[256,2560]{0,1:T(8,128)(2,1)}, ...), condition=%wide.region_8.9_spmd.clone, body=%wide.region_1.8_spmd.clone.sunk | while | flops 1708717824 | bytes 168688256 | solution.py:140
  178.2 3.4 conditional.3
  182.9 1.4 constant_dynamic-slice_fusion.6
  191.4 14.5 %collective-permute-done = bf16[256,2560]{0,1:T(8,128)(2,1)} collective-permute-done((bf16[256,2560]{0,1:T(8,128)(2,1)}, bf16[256,2560]{0,1:T(8,128)(2,1)}, u32[]{:S(2)}, u32[]{:S(2)}) %collective-permute-start) | collective-permute-done | bytes 1310752 | tf_op jit(solution)/shard_map/while/body/eval_jaxpr/ppermute | solution.py:19
  207.2 3.4 conditional.3
  220.3 14.5 %collective-permute-done = bf16[256,2560]{0,1:T(8,128)(2,1)} collective-permute-done((bf16[256,2560]{0,1:T(8,128)(2,1)}, bf16[256,2560]{0,1:T(8,128)(2,1)}, u32[]{:S(2)}, u32[]{:S(2)}) %collective-permute-start) | collective-permute-done | bytes 1310752 | tf_op jit(solution)/shard_map/while/body/eval_jaxpr/ppermute | solution.py:19
  236.1 3.4 conditional.3
  240.8 1.4 constant_dynamic-slice_fusion.6
  249.3 14.5 %collective-permute-done = bf16[256,2560]{0,1:T(8,128)(2,1)} collective-permute-done((bf16[256,2560]{0,1:T(8,128)(2,1)}, bf16[256,2560]{0,1:T(8,128)(2,1)}, u32[]{:S(2)}, u32[]{:S(2)}) %collective-permute-start) | collective-permute-done | bytes 1310752 | tf_op jit(solution)/shard_map/while/body/eval_jaxpr/ppermute | solution.py:19
  265.0 3.4 conditional.3
  278.2 14.5 %collective-permute-done = bf16[256,2560]{0,1:T(8,128)(2,1)} collective-permute-done((bf16[256,2560]{0,1:T(8,128)(2,1)}, bf16[256,2560]{0,1:T(8,128)(2,1)}, u32[]{:S(2)}, u32[]{:S(2)}) %collective-permute-start) | collective-permute-done | bytes 1310752 | tf_op jit(solution)/shard_map/while/body/eval_jaxpr/ppermute | solution.py:19
  294.0 3.4 conditional.3
  307.2 15.3 %collective-permute-done = bf16[256,2560]{0,1:T(8,128)(2,1)} collective-permute-done((bf16[256,2560]{0,1:T(8,128)(2,1)}, bf16[256,2560]{0,1:T(8,128)(2,1)}, u32[]{:S(2)}, u32[]{:S(2)}) %collective-permute-start) | collective-permute-done | bytes 1310752 | tf_op jit(solution)/shard_map/while/body/eval_jaxpr/ppermute | solution.py:19
  323.7 3.4 conditional.3
  328.4 1.4 constant_dynamic-slice_fusion.6
  336.9 16.4 %collective-permute-done = bf16[256,2560]{0,1:T(8,128)(2,1)} collective-permute-done((bf16[256,2560]{0,1:T(8,128)(2,1)}, bf16[256,2560]{0,1:T(8,128)(2,1)}, u32[]{:S(2)}, u32[]{:S(2)}) %collective-permute-start) | collective-permute-done | bytes 1310752 | tf_op jit(solution)/shard_map/while/body/eval_jaxpr/ppermute | solution.py:19
  354.5 3.4 conditional.3
  367.7 17.5 %collective-permute-done = bf16[256,2560]{0,1:T(8,128)(2,1)} collective-permute-done((bf16[256,2560]{0,1:T(8,128)(2,1)}, bf16[256,2560]{0,1:T(8,128)(2,1)}, u32[]{:S(2)}, u32[]{:S(2)}) %collective-permute-start) | collective-permute-done | bytes 1310752 | tf_op jit(solution)/shard_map/while/body/eval_jaxpr/ppermute | solution.py:19
  386.4 3.4 conditional.3
  399.6 18.5 %collective-permute-done = bf16[256,2560]{0,1:T(8,128)(2,1)} collective-permute-done((bf16[256,2560]{0,1:T(8,128)(2,1)}, bf16[256,2560]{0,1:T(8,128)(2,1)}, u32[]{:S(2)}, u32[]{:S(2)}) %collective-permute-start) | collective-permute-done | bytes 1310752 | tf_op jit(solution)/shard_map/while/body/eval_jaxpr/ppermute | solution.py:19
  419.4 3.4 conditional.3
  424.1 1.4 constant_dynamic-slice_fusion.6
  432.6 19.6 %collective-permute-done = bf16[256,2560]{0,1:T(8,128)(2,1)} collective-permute-done((bf16[256,2560]{0,1:T(8,128)(2,1)}, bf16[256,2560]{0,1:T(8,128)(2,1)}, u32[]{:S(2)}, u32[]{:S(2)}) %collective-permute-start) | collective-permute-done | bytes 1310752 | tf_op jit(solution)/shard_map/while/body/eval_jaxpr/ppermute | solution.py:19
  453.4 3.4 conditional.3
  466.6 20.7 %collective-permute-done = bf16[256,2560]{0,1:T(8,128)(2,1)} collective-permute-done((bf16[256,2560]{0,1:T(8,128)(2,1)}, bf16[256,2560]{0,1:T(8,128)(2,1)}, u32[]{:S(2)}, u32[]{:S(2)}) %collective-permute-start) | collective-permute-done | bytes 1310752 | tf_op jit(solution)/shard_map/while/body/eval_jaxpr/ppermute | solution.py:19
  488.6 3.4 conditional.3
  493.3 1.4 constant_dynamic-slice_fusion.6
  501.8 21.8 %collective-permute-done = bf16[256,2560]{0,1:T(8,128)(2,1)} collective-permute-done((bf16[256,2560]{0,1:T(8,128)(2,1)}, bf16[256,2560]{0,1:T(8,128)(2,1)}, u32[]{:S(2)}, u32[]{:S(2)}) %collective-permute-start) | collective-permute-done | bytes 1310752 | tf_op jit(solution)/shard_map/while/body/eval_jaxpr/ppermute | solution.py:19
  524.8 3.4 conditional.3
  538.0 23.2 %collective-permute-done = bf16[256,2560]{0,1:T(8,128)(2,1)} collective-permute-done((bf16[256,2560]{0,1:T(8,128)(2,1)}, bf16[256,2560]{0,1:T(8,128)(2,1)}, u32[]{:S(2)}, u32[]{:S(2)}) %collective-permute-start) | collective-permute-done | bytes 1310752 | tf_op jit(solution)/shard_map/while/body/eval_jaxpr/ppermute | solution.py:19
  562.5 3.4 conditional.3
  575.7 24.3 %collective-permute-done = bf16[256,2560]{0,1:T(8,128)(2,1)} collective-permute-done((bf16[256,2560]{0,1:T(8,128)(2,1)}, bf16[256,2560]{0,1:T(8,128)(2,1)}, u32[]{:S(2)}, u32[]{:S(2)}) %collective-permute-start) | collective-permute-done | bytes 1310752 | tf_op jit(solution)/shard_map/while/body/eval_jaxpr/ppermute | solution.py:19
  601.2 3.4 conditional.3
  614.4 10.0 collective-permute-done
  625.7 3.4 conditional.3
  638.8 169.7 %collective-permute-done = bf16[256,2560]{0,1:T(8,128)(2,1)} collective-permute-done((bf16[256,2560]{0,1:T(8,128)(2,1)}, bf16[256,2560]{0,1:T(8,128)(2,1)}, u32[]{:S(2)}, u32[]{:S(2)}) %collective-permute-start) | collective-permute-done | bytes 1310752 | tf_op jit(solution)/shard_map/while/body/eval_jaxpr/ppermute | solution.py:19
  809.8 21.5 %conditional.3 = (bf16[256,2560]{0,1:T(8,128)(2,1)}, f32[2560]{0:T(1024)S(1)}, bf16[1,256,2560]{1,2,0:T(8,128)(2,1)}, f32[1,256,1024]{1,2,0:T(8,128)}) conditional(s32[]{:T(128)} %convert_element_type.53, () %tuple.60, (pred[]{:T(512)}, bf16[2,256,2560]{1,2,0:T(8,128)(2,1)}, s32[]{:T(128)}, bf16[256,2560]{0,1:T(8,128)(2,1)}, f32[1,2560]{1,0:T(1,128)S(1)}, ...), branch_computations={%region_2.2_spmd, %region_3.7_spmd} | conditional | flops 1707795200 | bytes 137461024 | solution.py:115
  809.9 1.4 constant_dynamic-slice_fusion
  811.3 1.5 dynamic-slice_bitcast_fusion
  814.2 1.5 fusion.22
  816.0 2.5 bitcast_select_fusion.4
  821.4 1.5 fusion.8
  822.9 2.6 copy.64
  825.5 3.6 fusion.9
  834.7 1.5 broadcast_select_fusion.2
  842.5 12.3 %collective-permute-done = bf16[256,2560]{0,1:T(8,128)(2,1)} collective-permute-done((bf16[256,2560]{0,1:T(8,128)(2,1)}, bf16[256,2560]{0,1:T(8,128)(2,1)}, u32[]{:S(2)}, u32[]{:S(2)}) %collective-permute-start) | collective-permute-done | bytes 1310752 | tf_op jit(solution)/shard_map/while/body/eval_jaxpr/ppermute | solution.py:19
  856.0 21.5 %conditional.3 = (bf16[256,2560]{0,1:T(8,128)(2,1)}, f32[2560]{0:T(1024)S(1)}, bf16[1,256,2560]{1,2,0:T(8,128)(2,1)}, f32[1,256,1024]{1,2,0:T(8,128)}) conditional(s32[]{:T(128)} %convert_element_type.53, () %tuple.60, (pred[]{:T(512)}, bf16[2,256,2560]{1,2,0:T(8,128)(2,1)}, s32[]{:T(128)}, bf16[256,2560]{0,1:T(8,128)(2,1)}, f32[1,2560]{1,0:T(1,128)S(1)}, ...), branch_computations={%region_2.2_spmd, %region_3.7_spmd} | conditional | flops 1707795200 | bytes 137461024 | solution.py:115
  856.1 1.4 constant_dynamic-slice_fusion
  857.5 1.5 dynamic-slice_bitcast_fusion
  860.4 1.5 fusion.22
  862.2 2.5 bitcast_select_fusion.4
  867.6 1.5 fusion.8
  869.1 2.6 copy.64
  871.7 3.6 fusion.9
  880.9 1.5 broadcast_select_fusion.2
  888.7 14.7 %collective-permute-done = bf16[256,2560]{0,1:T(8,128)(2,1)} collective-permute-done((bf16[256,2560]{0,1:T(8,128)(2,1)}, bf16[256,2560]{0,1:T(8,128)(2,1)}, u32[]{:S(2)}, u32[]{:S(2)}) %collective-permute-start) | collective-permute-done | bytes 1310752 | tf_op jit(solution)/shard_map/while/body/eval_jaxpr/ppermute | solution.py:19
  903.4 88.6 %all-reduce.4 = bf16[2,256,1024]{2,1,0:T(8,128)(2,1)} all-reduce(f32[2,256,1024]{2,1,0:T(8,128)} %get-tuple-element.227), channel_id=1, replica_groups=mesh['section'=16,'dp'=16] {'section'}, use_global_device_ids=true, to_apply=%region_9.10 | all-reduce | flops 524288 | bytes 3145728 | tf_op jit(solution)/shard_map/psum | solution.py:144
  992.0 49.1 %psum.23 = f32[1,2560]{1,0:T(1,128)} all-reduce(f32[1,2560]{1,0:T(1,128)S(1)} %broadcast_in_dim.54), channel_id=1, replica_groups=mesh['section'=16,'dp'=16] {'dp'}, use_global_device_ids=true, to_apply=%region_10.11 | all-reduce | flops 2560 | bytes 20480 | tf_op jit(solution)/shard_map/psum | solution.py:145
  (339 shorter events, 234.7 us)
Async XLA Ops:
  7.2 165.4 %all-reduce.3.cloned.1.call-start = ((), (), s32[]{:S(2)}) async-start(), calls=%async_computation | async-start | bytes 2097152 | tf_op jit(solution)/shard_map/psum | solution.py:13
  9.8 4.6 copy-start.7
  173.7 3.2 copy-start.8
  173.7 3.2 copy-start.9
  181.6 24.3 %collective-permute-start = (bf16[256,2560]{0,1:T(8,128)(2,1)}, bf16[256,2560]{0,1:T(8,128)(2,1)}, u32[]{:S(2)}, u32[]{:S(2)}) collective-permute-start(bf16[256,2560]{0,1:T(8,128)(2,1)} %get-tuple-element.418), channel_id=1, source_target_pairs={{16,0},{32,16},{48,32},{64,48},{80,64},{96,80},{112,96},{128,112},... | collective-permute-start | bytes 3932168 | tf_op jit(solution)/shard_map/while/body/eval_jaxpr/ppermute | solution.py:19
  210.6 24.3 %collective-permute-start = (bf16[256,2560]{0,1:T(8,128)(2,1)}, bf16[256,2560]{0,1:T(8,128)(2,1)}, u32[]{:S(2)}, u32[]{:S(2)}) collective-permute-start(bf16[256,2560]{0,1:T(8,128)(2,1)} %get-tuple-element.418), channel_id=1, source_target_pairs={{16,0},{32,16},{48,32},{64,48},{80,64},{96,80},{112,96},{128,112},... | collective-permute-start | bytes 3932168 | tf_op jit(solution)/shard_map/while/body/eval_jaxpr/ppermute | solution.py:19
  239.5 24.3 %collective-permute-start = (bf16[256,2560]{0,1:T(8,128)(2,1)}, bf16[256,2560]{0,1:T(8,128)(2,1)}, u32[]{:S(2)}, u32[]{:S(2)}) collective-permute-start(bf16[256,2560]{0,1:T(8,128)(2,1)} %get-tuple-element.418), channel_id=1, source_target_pairs={{16,0},{32,16},{48,32},{64,48},{80,64},{96,80},{112,96},{128,112},... | collective-permute-start | bytes 3932168 | tf_op jit(solution)/shard_map/while/body/eval_jaxpr/ppermute | solution.py:19
  268.4 24.3 %collective-permute-start = (bf16[256,2560]{0,1:T(8,128)(2,1)}, bf16[256,2560]{0,1:T(8,128)(2,1)}, u32[]{:S(2)}, u32[]{:S(2)}) collective-permute-start(bf16[256,2560]{0,1:T(8,128)(2,1)} %get-tuple-element.418), channel_id=1, source_target_pairs={{16,0},{32,16},{48,32},{64,48},{80,64},{96,80},{112,96},{128,112},... | collective-permute-start | bytes 3932168 | tf_op jit(solution)/shard_map/while/body/eval_jaxpr/ppermute | solution.py:19
  297.4 25.1 %collective-permute-start = (bf16[256,2560]{0,1:T(8,128)(2,1)}, bf16[256,2560]{0,1:T(8,128)(2,1)}, u32[]{:S(2)}, u32[]{:S(2)}) collective-permute-start(bf16[256,2560]{0,1:T(8,128)(2,1)} %get-tuple-element.418), channel_id=1, source_target_pairs={{16,0},{32,16},{48,32},{64,48},{80,64},{96,80},{112,96},{128,112},... | collective-permute-start | bytes 3932168 | tf_op jit(solution)/shard_map/while/body/eval_jaxpr/ppermute | solution.py:19
  327.1 26.2 %collective-permute-start = (bf16[256,2560]{0,1:T(8,128)(2,1)}, bf16[256,2560]{0,1:T(8,128)(2,1)}, u32[]{:S(2)}, u32[]{:S(2)}) collective-permute-start(bf16[256,2560]{0,1:T(8,128)(2,1)} %get-tuple-element.418), channel_id=1, source_target_pairs={{16,0},{32,16},{48,32},{64,48},{80,64},{96,80},{112,96},{128,112},... | collective-permute-start | bytes 3932168 | tf_op jit(solution)/shard_map/while/body/eval_jaxpr/ppermute | solution.py:19
  357.9 27.3 %collective-permute-start = (bf16[256,2560]{0,1:T(8,128)(2,1)}, bf16[256,2560]{0,1:T(8,128)(2,1)}, u32[]{:S(2)}, u32[]{:S(2)}) collective-permute-start(bf16[256,2560]{0,1:T(8,128)(2,1)} %get-tuple-element.418), channel_id=1, source_target_pairs={{16,0},{32,16},{48,32},{64,48},{80,64},{96,80},{112,96},{128,112},... | collective-permute-start | bytes 3932168 | tf_op jit(solution)/shard_map/while/body/eval_jaxpr/ppermute | solution.py:19
  389.8 28.3 %collective-permute-start = (bf16[256,2560]{0,1:T(8,128)(2,1)}, bf16[256,2560]{0,1:T(8,128)(2,1)}, u32[]{:S(2)}, u32[]{:S(2)}) collective-permute-start(bf16[256,2560]{0,1:T(8,128)(2,1)} %get-tuple-element.418), channel_id=1, source_target_pairs={{16,0},{32,16},{48,32},{64,48},{80,64},{96,80},{112,96},{128,112},... | collective-permute-start | bytes 3932168 | tf_op jit(solution)/shard_map/while/body/eval_jaxpr/ppermute | solution.py:19
  422.8 29.4 %collective-permute-start = (bf16[256,2560]{0,1:T(8,128)(2,1)}, bf16[256,2560]{0,1:T(8,128)(2,1)}, u32[]{:S(2)}, u32[]{:S(2)}) collective-permute-start(bf16[256,2560]{0,1:T(8,128)(2,1)} %get-tuple-element.418), channel_id=1, source_target_pairs={{16,0},{32,16},{48,32},{64,48},{80,64},{96,80},{112,96},{128,112},... | collective-permute-start | bytes 3932168 | tf_op jit(solution)/shard_map/while/body/eval_jaxpr/ppermute | solution.py:19
  456.8 30.5 %collective-permute-start = (bf16[256,2560]{0,1:T(8,128)(2,1)}, bf16[256,2560]{0,1:T(8,128)(2,1)}, u32[]{:S(2)}, u32[]{:S(2)}) collective-permute-start(bf16[256,2560]{0,1:T(8,128)(2,1)} %get-tuple-element.418), channel_id=1, source_target_pairs={{16,0},{32,16},{48,32},{64,48},{80,64},{96,80},{112,96},{128,112},... | collective-permute-start | bytes 3932168 | tf_op jit(solution)/shard_map/while/body/eval_jaxpr/ppermute | solution.py:19
  492.0 31.6 %collective-permute-start = (bf16[256,2560]{0,1:T(8,128)(2,1)}, bf16[256,2560]{0,1:T(8,128)(2,1)}, u32[]{:S(2)}, u32[]{:S(2)}) collective-permute-start(bf16[256,2560]{0,1:T(8,128)(2,1)} %get-tuple-element.418), channel_id=1, source_target_pairs={{16,0},{32,16},{48,32},{64,48},{80,64},{96,80},{112,96},{128,112},... | collective-permute-start | bytes 3932168 | tf_op jit(solution)/shard_map/while/body/eval_jaxpr/ppermute | solution.py:19
  528.2 33.0 %collective-permute-start = (bf16[256,2560]{0,1:T(8,128)(2,1)}, bf16[256,2560]{0,1:T(8,128)(2,1)}, u32[]{:S(2)}, u32[]{:S(2)}) collective-permute-start(bf16[256,2560]{0,1:T(8,128)(2,1)} %get-tuple-element.418), channel_id=1, source_target_pairs={{16,0},{32,16},{48,32},{64,48},{80,64},{96,80},{112,96},{128,112},... | collective-permute-start | bytes 3932168 | tf_op jit(solution)/shard_map/while/body/eval_jaxpr/ppermute | solution.py:19
  565.9 34.1 %collective-permute-start = (bf16[256,2560]{0,1:T(8,128)(2,1)}, bf16[256,2560]{0,1:T(8,128)(2,1)}, u32[]{:S(2)}, u32[]{:S(2)}) collective-permute-start(bf16[256,2560]{0,1:T(8,128)(2,1)} %get-tuple-element.418), channel_id=1, source_target_pairs={{16,0},{32,16},{48,32},{64,48},{80,64},{96,80},{112,96},{128,112},... | collective-permute-start | bytes 3932168 | tf_op jit(solution)/shard_map/while/body/eval_jaxpr/ppermute | solution.py:19
  604.6 19.8 %collective-permute-start = (bf16[256,2560]{0,1:T(8,128)(2,1)}, bf16[256,2560]{0,1:T(8,128)(2,1)}, u32[]{:S(2)}, u32[]{:S(2)}) collective-permute-start(bf16[256,2560]{0,1:T(8,128)(2,1)} %get-tuple-element.418), channel_id=1, source_target_pairs={{16,0},{32,16},{48,32},{64,48},{80,64},{96,80},{112,96},{128,112},... | collective-permute-start | bytes 3932168 | tf_op jit(solution)/shard_map/while/body/eval_jaxpr/ppermute | solution.py:19
  629.0 179.5 %collective-permute-start = (bf16[256,2560]{0,1:T(8,128)(2,1)}, bf16[256,2560]{0,1:T(8,128)(2,1)}, u32[]{:S(2)}, u32[]{:S(2)}) collective-permute-start(bf16[256,2560]{0,1:T(8,128)(2,1)} %get-tuple-element.418), channel_id=1, source_target_pairs={{16,0},{32,16},{48,32},{64,48},{80,64},{96,80},{112,96},{128,112},... | collective-permute-start | bytes 3932168 | tf_op jit(solution)/shard_map/while/body/eval_jaxpr/ppermute | solution.py:19
  811.3 2.8 copy-start
  814.2 1.7 copy-start.6
  815.7 3.7 copy-start.3
  818.5 3.0 copy-start.4
  819.4 1.3 copy-start.1
  822.9 2.6 copy-start.5
  825.5 3.6 copy-start.2
  831.4 23.4 %collective-permute-start = (bf16[256,2560]{0,1:T(8,128)(2,1)}, bf16[256,2560]{0,1:T(8,128)(2,1)}, u32[]{:S(2)}, u32[]{:S(2)}) collective-permute-start(bf16[256,2560]{0,1:T(8,128)(2,1)} %get-tuple-element.418), channel_id=1, source_target_pairs={{16,0},{32,16},{48,32},{64,48},{80,64},{96,80},{112,96},{128,112},... | collective-permute-start | bytes 3932168 | tf_op jit(solution)/shard_map/while/body/eval_jaxpr/ppermute | solution.py:19
  857.5 2.8 copy-start
  860.4 1.7 copy-start.6
  861.9 3.7 copy-start.3
  864.7 3.0 copy-start.4
  865.6 1.3 copy-start.1
  869.1 2.6 copy-start.5
  871.7 3.6 copy-start.2
  877.6 25.8 %collective-permute-start = (bf16[256,2560]{0,1:T(8,128)(2,1)}, bf16[256,2560]{0,1:T(8,128)(2,1)}, u32[]{:S(2)}, u32[]{:S(2)}) collective-permute-start(bf16[256,2560]{0,1:T(8,128)(2,1)} %get-tuple-element.418), channel_id=1, source_target_pairs={{16,0},{32,16},{48,32},{64,48},{80,64},{96,80},{112,96},{128,112},... | collective-permute-start | bytes 3932168 | tf_op jit(solution)/shard_map/while/body/eval_jaxpr/ppermute | solution.py:19
Sparse Core Ops, SparseCore 0:
  11.2 161.3 all-reduce.2
where the time goes:
time: 1050 us
  waiting for transfers between devices  598 us (57%)
  local copies, waits for them, and re-layouts  203 us (19%)
  blocking collectives  138 us (13%)
  other arithmetic  45.2 us (4%)
  starting transfers between devices  21.8 us (2%)
  matrix products  15.3 us (1%)
  between operations  14.1 us (1%)
  loops' own time  12.9 us (1%)
    ppermute x17, waiting for transfers between devices, passed_along(): return lax.ppermute(array, axis, pairs)  442 us
    psum x1, waiting for transfers between devices, spread(): return lax.psum(jnp.where(mine, array, jnp.zeros_like(array)), axis)  156 us
    psum x1, blocking collectives, on_device(): cache_grad = lax.psum(cache_total, 'section').astype(jnp.bfloat16)  88.6 us
    psum x1, blocking collectives, on_device(): gain_grads = lax.psum(gain_total, 'dp')  49.1 us
    dynamic_slice x34, local copies, waits for them, and re-layouts, tick(): lax.dynamic_slice(grads_done, (micro_index, row_start, zero_index), (1, r...  34.3 us
    dynamic_update_slice x34, local copies, waits for them, and re-layouts, tick(): lax.dynamic_update_slice(grads_done, jnp.where(active, grad_next[None], p...  32.3 us
    dynamic_slice x34, local copies, waits for them, and re-layouts, tick(): lax.dynamic_slice(cache_total, (micro_index, zero_index, zero_index), (1,...  27.7 us
    dynamic_update_slice x34, local copies, waits for them, and re-layouts, tick(): lax.dynamic_update_slice(cache_total, cache_old + cache_part[None], (micr...  23.5 us
  transfers between devices with their start and end apart: 18, of which 18 were waited for; matrix products, arithmetic and copies ran while one was open for 15% of the time, Pallas kernels for 0%

commit v1 on v0

v1 whole, which is shorter than its diff:
```python
import functools

import jax
import jax.numpy as jnp
from jax import lax
from jax.experimental import pallas as pl
from jax.experimental.pallas import tpu as pltpu
from jax.sharding import PartitionSpec as P

HEADS = 20
KV_HEADS = 4
HEAD = 128
GROUP = HEADS // KV_HEADS
WIDE = GROUP * HEAD
SECTIONS = 16
MICROS = 2
LENGTH = 256
BLOCK = 64
LOG2E = 1.4426950408889634
SCALE = HEAD ** -0.5
MASKED = -1e30


def stack_heads(rows):
    return jnp.concatenate([rows[:, h * HEAD : (h + 1) * HEAD] for h in range(GROUP)], axis=0)


def unstack_heads(rows):
    return jnp.concatenate([rows[h * BLOCK : (h + 1) * BLOCK] for h in range(GROUP)], axis=1)


def chain_kernel(saved_ref, gain_ref, kv_ref, bias_ref, top_ref, before_cache, before_gain,
                 grads_ref, cache_ref, gain_part_ref):
    keys_seen = bias_ref.shape[0]
    contract_last = (((1,), (1,)), ((), ()))
    contract_first = (((0,), (0,)), ((), ()))
    cache_ref[...] = before_cache[...]

    def layer(step, incoming):
        s = SECTIONS - 1 - step
        keys = kv_ref[:keys_seen, :HEAD]
        values = kv_ref[:keys_seen, HEAD:]
        gain = gain_ref[pl.ds(s, 1), :]
        saved = saved_ref[s].astype(jnp.float32)
        queries = stack_heads((saved * gain).astype(jnp.bfloat16))
        scores = lax.dot_general(keys, queries, contract_last, preferred_element_type=jnp.float32)
        scores = scores * (SCALE * LOG2E) + bias_ref[...]
        exp_terms = jnp.exp2(scores - jnp.max(scores, axis=0, keepdims=True))
        probs = exp_terms * (1.0 / jnp.sum(exp_terms, axis=0, keepdims=True))
        dprob = lax.dot_general(values, incoming, contract_last, preferred_element_type=jnp.float32)
        delta = jnp.sum(probs * dprob, axis=0, keepdims=True)
        dscore = (probs * (dprob - delta)).astype(jnp.bfloat16)
        dquery = unstack_heads(
            lax.dot_general(dscore, keys, contract_first, preferred_element_type=jnp.float32) * SCALE
        )
        cache_ref[:keys_seen, :HEAD] += SCALE * jnp.dot(dscore, queries, preferred_element_type=jnp.float32)
        cache_ref[:keys_seen, HEAD:] += jnp.dot(
            probs.astype(jnp.bfloat16), incoming, preferred_element_type=jnp.float32
        )
        gain_part_ref[pl.ds(s, 1), :] = before_gain[pl.ds(s, 1), :] + jnp.sum(
            dquery * saved, axis=0, keepdims=True
        )
        grads = (unstack_heads(incoming).astype(jnp.float32) + gain * dquery).astype(jnp.bfloat16)
        grads_ref[s] = grads
        return stack_heads(grads)

    lax.fori_loop(0, SECTIONS, layer, stack_heads(top_ref[...]), unroll=2)


def chain(saved, gains, kv_unit, bias, top, cache_part, gain_part):
    columns = GROUP * BLOCK
    keys_seen = bias.shape[0]
    vmem = pl.BlockSpec(memory_space=pltpu.VMEM)
    return pl.pallas_call(
        chain_kernel,
        out_shape=(
            jax.ShapeDtypeStruct((SECTIONS, BLOCK, WIDE), jnp.bfloat16),
            jax.ShapeDtypeStruct((LENGTH, 2 * HEAD), jnp.float32),
            jax.ShapeDtypeStruct((SECTIONS, WIDE), jnp.float32),
        ),
        in_specs=[vmem] * 7,
        out_specs=(vmem, vmem, vmem),
        compiler_params=pltpu.CompilerParams(vmem_limit_bytes=32 * 1024 * 1024),
        cost_estimate=pl.CostEstimate(
            flops=SECTIONS * 10 * columns * keys_seen * HEAD,
            bytes_accessed=6 * 1024 * 1024,
            transcendentals=SECTIONS * columns * keys_seen,
        ),
    )(saved, gains, kv_unit, bias, top, cache_part, gain_part)


def sent_to(array, axis, pairs):
    return lax.ppermute(array, axis, pairs)


def unit_of_cache(cache, me):
    keys = cache[:, :, : KV_HEADS * HEAD].reshape(MICROS, LENGTH, KV_HEADS, HEAD)
    values = cache[:, :, KV_HEADS * HEAD :].reshape(MICROS, LENGTH, KV_HEADS, HEAD)
    units = jnp.concatenate([keys, values], axis=-1).transpose(0, 2, 1, 3)
    quads = units.reshape(4, 2, LENGTH, 2 * HEAD)
    came = [sent_to(quads[j], "section", [(0, 4 * j)]) for j in (1, 2, 3)]
    pair = jnp.where(me == 0, quads[0], came[0] + came[1] + came[2])
    came = [
        sent_to(pair[j // 2], "section", [(4 * a, 4 * a + j) for a in range(4)]) for j in (1, 2, 3)
    ]
    return jnp.where(me % 4 == 0, pair[0], came[0] + came[1] + came[2])


def bias_of(segments, block, keys_seen):
    rows = lax.dynamic_slice(segments, (block * BLOCK,), (BLOCK,))
    key_pos = jnp.arange(keys_seen)
    query_pos = block * BLOCK + jnp.arange(BLOCK)
    allowed = (key_pos[:, None] <= query_pos[None, :]) & (
        segments[:keys_seen, None] == rows[None, :]
    )
    bias = jnp.where(allowed, 0.0, MASKED).astype(jnp.float32)
    return jnp.tile(bias, (1, GROUP))


def on_device(saved_inputs, query_gains, cache_slots, segment_ids, output_grad):
    me = lax.axis_index("section")
    micro, head, half = me // 8, (me % 8) // 2, me % 2
    exchange = functools.partial(
        lax.all_to_all, axis_name="section", split_axis=0, concat_axis=0, tiled=True
    )
    kv_unit = unit_of_cache(cache_slots[0], me)
    gain_spread = jnp.broadcast_to(
        jnp.pad(query_gains.reshape(1, KV_HEADS, 1, WIDE), ((0, 0), (0, 0), (0, 0), (0, 384))),
        (MICROS, KV_HEADS, 2, WIDE + 384),
    )
    gains = exchange(gain_spread.reshape(SECTIONS, 8, 128)).reshape(SECTIONS, WIDE + 384)[:, :WIDE]
    tiles = saved_inputs.reshape(MICROS, 4, BLOCK, KV_HEADS, WIDE).transpose(0, 3, 1, 2, 4)
    late = jnp.stack([tiles[:, :, 3], tiles[:, :, 2]], axis=2).reshape(SECTIONS, BLOCK, WIDE)
    early = tiles[:, :, :2].reshape(SECTIONS, BLOCK, WIDE)
    late_saved = exchange(late)
    early_saved = exchange(early)

    segments = lax.dynamic_index_in_dim(segment_ids, micro, 0, keepdims=False)
    late_block, early_block = 3 - half, half

    def top_of(block):
        start = (micro, block * BLOCK, head * WIDE)
        return lax.dynamic_slice(output_grad, start, (1, BLOCK, WIDE))[0]

    late_grads, cache_part, gain_part = chain(
        late_saved, gains, kv_unit, bias_of(segments, late_block, LENGTH), top_of(late_block),
        jnp.zeros((LENGTH, 2 * HEAD), jnp.float32), jnp.zeros((SECTIONS, WIDE), jnp.float32),
    )
    late_home = exchange(late_grads)
    early_grads, cache_part, gain_part = chain(
        early_saved, gains, kv_unit, bias_of(segments, early_block, LENGTH // 2), top_of(early_block),
        cache_part, gain_part,
    )
    gain_home = exchange(jnp.pad(gain_part, ((0, 0), (0, 384))).reshape(SECTIONS, 8, 128))
    early_home = exchange(early_grads)

    halves = cache_part.reshape(2, LENGTH // 2, 2 * HEAD)
    theirs = sent_to(
        lax.dynamic_index_in_dim(halves, 1 - half, 0, keepdims=False),
        "section", [(i, i ^ 1) for i in range(SECTIONS)],
    )
    mine = (lax.dynamic_index_in_dim(halves, half, 0, keepdims=False) + theirs).astype(jnp.bfloat16)
    whole = exchange(jnp.broadcast_to(mine[None], (SECTIONS, LENGTH // 2, 2 * HEAD)))
    whole = whole.reshape(MICROS, KV_HEADS, LENGTH, 2, HEAD).transpose(0, 2, 3, 1, 4)
    cache_grad = whole.reshape(MICROS, LENGTH, 2 * KV_HEADS * HEAD)

    gain_sum = gain_home.reshape(MICROS, KV_HEADS, 2, WIDE + 384)[..., :WIDE].sum((0, 2))
    gain_sum = gain_sum.reshape(20, 128)
    for bit in (8, 4, 2, 1):
        gain_sum = gain_sum + sent_to(gain_sum, "dp", [(i, i ^ bit) for i in range(16)])

    late_home = late_home.reshape(MICROS, KV_HEADS, 2, BLOCK, WIDE)
    early_home = early_home.reshape(MICROS, KV_HEADS, 2, BLOCK, WIDE)
    blocks = jnp.stack(
        [early_home[:, :, 0], early_home[:, :, 1], late_home[:, :, 1], late_home[:, :, 0]], axis=1
    )
    layer_out = blocks.transpose(0, 1, 3, 2, 4).reshape(1, MICROS, LENGTH, HEADS * HEAD)
    return (layer_out, cache_grad, gain_sum.reshape(1, HEADS * HEAD))


def solution(mesh):
    return jax.shard_map(
        on_device,
        mesh=mesh,
        in_specs=(
            P("section", "dp", None, None),
            P("section", None),
            P("section", "dp", None, None),
            P("dp", None),
            P("dp", None, None),
        ),
        out_specs=(P("section", "dp", None, None), P("dp", None, None), P("section", None)),
        check_vma=False,
    )
```

time: 1050 us -> 273 us (0.26)
  waiting for transfers between devices: 598 us -> 83.4 us
  local copies, waits for them, and re-layouts: 203 us -> 35.8 us
  blocking collectives: 138 us -> 66.3 us
  other arithmetic: 45.2 us -> 7.58 us
  starting transfers between devices: 21.8 us -> 59.2 us
  Pallas kernels: 0 us -> 18.5 us
  matrix products: 15.3 us -> 0 us
  between operations: 14.1 us -> 1.07 us
  loops' own time: 12.9 us -> 0 us
    ppermute x17 -> x11, waiting for transfers between devices: 442 us -> 33.4 us  [sent_to(): return lax.ppermute(array, axis, pairs)]
    psum x1 -> x0, waiting for transfers between devices: 156 us -> none  [spread(): return lax.psum(jnp.where(mine, array, jnp.zeros_like(array)), axis)]
    psum x2 -> x0, blocking collectives: 138 us -> none  [the longest x1 88.6 us: on_device(): cache_grad = lax.psum(cache_total, 'section').astype(jnp.bfloat16)]
    dynamic_slice x89 -> x1, local copies, waits for them, and re-layouts: 74.8 us -> 0.01 us  [on_device(): segments = lax.dynamic_index_in_dim(segment_ids, micro, 0, keepdims=False)]
    all_to_all x0 -> x2, blocking collectives: none -> 66.3 us  [the longest x1 36.8 us: on_device(): early_home = exchange(early_grads)]
    dynamic_update_slice x68 -> x0, local copies, waits for them, and re-layouts: 55.8 us -> none  [the longest x34 32.3 us: tick(): lax.dynamic_update_slice(grads_done, jnp.where(active, grad_next[None], p...]
    all_to_all x0 -> x5, waiting for transfers between devices: none -> 50 us  [the longest x1 30.1 us: on_device(): late_saved = exchange(late)]
    broadcast_in_dim x33 -> x5, local copies, waits for them, and re-layouts: 36.5 us -> 0.14 us  [the longest x1 0.09 us: on_device(): jnp.broadcast_to(mine[None], (SECTIONS, LENGTH // 2, 2 * HEAD))]
  transfers between devices with their start and end apart: 18 -> 16, of which waited for: 18 -> 12; matrix products, arithmetic and copies ran while one was open for 15% -> 12% of each run, Pallas kernels for 0% -> 4%
where the time goes in v1:
time: 273 us; the launch traced here: 272 us
  waiting for transfers between devices  83.4 us (31%)
  blocking collectives  66.3 us (24%)
  starting transfers between devices  59.2 us (22%)
  local copies, waits for them, and re-layouts  35.8 us (13%)
  Pallas kernels  18.5 us (7%)
  other arithmetic  7.58 us (3%)
    all_to_all x1, blocking collectives, on_device(): early_home = exchange(early_grads)  36.8 us
    ppermute x11, waiting for transfers between devices, sent_to(): return lax.ppermute(array, axis, pairs)  33.4 us
    all_to_all x1, waiting for transfers between devices, on_device(): late_saved = exchange(late)  30.1 us
    all_to_all x1, blocking collectives, on_device(): exchange(jnp.broadcast_to(mine[None], (SECTIONS, LENGTH // 2, 2 * HEAD)))  29.5 us
    ppermute x11, starting transfers between devices, sent_to(): return lax.ppermute(array, axis, pairs)  23.9 us
    pallas_call x2, Pallas kernels, chain(): pl.pallas_call(chain_kernel, out_shape=(jax.ShapeDtypeStruct((SECTIONS, B...  18.5 us
    all_to_all x1, starting transfers between devices, on_device(): exchange(gain_spread.reshape(SECTIONS, 8, 128))  11 us
    all_to_all x1, waiting for transfers between devices, on_device(): exchange(jnp.pad(gain_part, ((0, 0), (0, 384))).reshape(SECTIONS, 8, 128))  9.99 us
  transfers between devices with their start and end apart: 16, of which 12 were waited for; matrix products, arithmetic and copies ran while one was open for 12% of the time, Pallas kernels for 4%

profile of v1, /device:TPU:8, one launch (start us, length us, event | category | flops | bytes accessed | tf_op | source)
XLA Modules:
  0.0 271.9 jit_solution(12970727290031232082)
XLA Ops:
  0.6 0.7 reduce
  1.4 0.7 reshape.190
  2.1 11.0 %all-to-all-start.1 = ((f32[16,8,128]{2,1,0:T(8,128)}), f32[16,8,128]{2,1,0:T(8,128)S(1)}, u32[]{:S(2)}, u32[]{:S(2)}) async-start(f32[16,8,128]{2,1,0:T(8,128)} %reshape.190), calls=%async_computation.1 | async-start | bytes 131072 | tf_op jit(solution)/shard_map/all_to_all | solution.py:131
  13.1 4.5 %reshape.187 = bf16[2,4,64,4,640]{4,3,2,1,0:T(4,128)(2,1)S(1)} reshape(bf16[1,2,256,2560]{3,2,1,0:T(8,128)(2,1)} %param.5) | data formatting | bytes 5242880 | tf_op jit(solution)/shard_map/reshape | solution.py:132
  17.7 0.5 copy.48
  18.2 1.5 copy-done.2
  19.8 1.2 pad_maximum_fusion
  21.0 2.2 all-to-all-done.1
  23.2 7.6 %all-to-all-start.2 = ((bf16[16,64,640]{2,1,0:T(8,128)(2,1)}), bf16[16,64,640]{2,1,0:T(8,128)(2,1)S(1)}, u32[]{:S(2)}, u32[]{:S(2)}) async-start(bf16[16,64,640]{2,1,0:T(8,128)(2,1)} %bitcast.17), calls=%async_computation.2 | async-start | bytes 2621440 | tf_op jit(solution)/shard_map/all_to_all | solution.py:135
  30.7 2.5 slice.75
  33.3 0.9 slice_bitcast_fusion.5
  34.1 30.1 %all-to-all-done.2.saved_ref = bf16[16,64,640]{2,1,0:T(8,128)(2,1)S(1)} async-done(((bf16[16,64,640]{2,1,0:T(8,128)(2,1)}), bf16[16,64,640]{2,1,0:T(8,128)(2,1)S(1)}, u32[]{:S(2)}, u32[]{:S(2)}) %all-to-all-start.2) | async-done | bytes 1310752 | tf_op jit(solution)/shard_map/all_to_all | solution.py:135
  64.2 4.5 %all-to-all-start = ((bf16[16,64,640]{2,1,0:T(8,128)(2,1)}), bf16[16,64,640]{2,1,0:T(8,128)(2,1)S(1)}, u32[]{:S(2)}, u32[]{:S(2)}) async-start(bf16[16,64,640]{2,1,0:T(8,128)(2,1)} %bitcast.94), calls=%async_computation | async-start | bytes 2621440 | tf_op jit(solution)/shard_map/all_to_all | solution.py:136
  68.8 1.3 copy_bitcast_fusion.1
  70.1 1.1 pad_maximum_fusion.1
  71.2 2.0 slice_bitcast_fusion.7
  73.2 5.3 %collective-permute-start.1 = (bf16[2,256,256]{2,1,0:T(8,128)(2,1)}, bf16[2,256,256]{2,1,0:T(8,128)(2,1)S(1)}, u32[]{:S(2)}, u32[]{:S(2)}) collective-permute-start(bf16[2,256,256]{2,1,0:T(8,128)(2,1)} %get-tuple-element.26), channel_id=1, source_target_pairs={{0,128},{1,129},{2,130},{3,131},{4,132},{5,133},{6,134},{7,135},{8... | collective-permute-start | bytes 786440 | tf_op jit(solution)/shard_map/ppermute | solution.py:93
  78.6 5.5 %collective-permute-start.2 = (bf16[2,256,256]{2,1,0:T(8,128)(2,1)}, bf16[2,256,256]{2,1,0:T(8,128)(2,1)S(1)}, u32[]{:S(2)}, u32[]{:S(2)}) collective-permute-start(bf16[2,256,256]{2,1,0:T(8,128)(2,1)} %get-tuple-element.27), channel_id=1, source_target_pairs={{0,192},{1,193},{2,194},{3,195},{4,196},{5,197},{6,198},{7,199},{8... | collective-permute-start | bytes 786440 | tf_op jit(solution)/shard_map/ppermute | solution.py:93
  84.1 1.3 collective-permute-start
  85.4 0.5 iota_add_fusion
  86.0 0.5 fusion.6
  86.6 0.7 fusion.3
  87.3 0.9 collective-permute-done.1
  88.2 15.7 %collective-permute-done.2 = bf16[2,256,256]{2,1,0:T(8,128)(2,1)S(1)} collective-permute-done((bf16[2,256,256]{2,1,0:T(8,128)(2,1)}, bf16[2,256,256]{2,1,0:T(8,128)(2,1)S(1)}, u32[]{:S(2)}, u32[]{:S(2)}) %collective-permute-start.2) | collective-permute-done | bytes 262176 | tf_op jit(solution)/shard_map/ppermute | solution.py:93
  103.9 4.7 %collective-permute-done = bf16[2,256,256]{2,1,0:T(8,128)(2,1)S(1)} collective-permute-done((bf16[2,256,256]{2,1,0:T(8,128)(2,1)}, bf16[2,256,256]{2,1,0:T(8,128)(2,1)S(1)}, u32[]{:S(2)}, u32[]{:S(2)}) %collective-permute-start) | collective-permute-done | bytes 262176 | tf_op jit(solution)/shard_map/ppermute | solution.py:93
  108.5 1.0 fusion
  109.6 0.7 copy-done.4
  110.2 0.7 slice_bitcast_fusion.11
  111.0 1.9 collective-permute-start.5
  112.9 1.9 collective-permute-start.4
  114.8 1.9 collective-permute-start.3
  116.8 0.7 fusion.5
  117.6 0.1 copy.28.bias_ref
  117.7 0.8 tile.20
  118.5 1.1 copy.27.bias_ref
  119.6 1.0 dynamic-slice_bitcast_fusion.2
  120.7 1.1 add_select_fusion.kv_ref
  121.8 11.1 %shard_map.76 = (bf16[16,64,640]{2,1,0:T(8,128)(2,1)}, f32[256,256]{1,0:T(8,128)S(1)}, f32[16,640]{1,0:T(8,128)S(1)}) custom-call(bf16[16,64,640]{2,1,0:T(8,128)(2,1)S(1)} %all-to-all-done.2.saved_ref, f32[16,640]{1,0:T(8,128)S(1)} %slice.76.gain_ref, bf16[256,256]{1,0:T(8,128)(2,1)S(1)} %add_select_fusion.kv_ref, f32[256,320]{1,0:T(8,128)S(1)} %copy.27.bias_ref, ...), custom_call_target="tpu_custom_call" | custom-call | flops 1677721600 | bytes 6291456 | tf_op jit(solution)/shard_map/pallas_call | solution.py:74
  132.9 0.7 copy-done
  133.6 0.9 copy-done.1
  134.5 7.4 %shard_map.77 = (bf16[16,64,640]{2,1,0:T(8,128)(2,1)S(1)}, f32[256,256]{1,0:T(8,128)S(1)}, f32[16,640]{1,0:T(8,128)S(1)}) custom-call(bf16[16,64,640]{2,1,0:T(8,128)(2,1)S(1)} %all-to-all-done.saved_ref, f32[16,640]{1,0:T(8,128)S(1)} %slice.76.gain_ref, bf16[256,256]{1,0:T(8,128)(2,1)S(1)} %add_select_fusion.kv_ref, f32[128,320]{1,0:T(8,128)S(1)} %copy.28.bias_ref, ...), custom_call_target="tpu_custom_call" | custom-call | flops 838860800 | bytes 6291456 | tf_op jit(solution)/shard_map/pallas_call | solution.py:74
  142.0 2.6 collective-permute-start.6
  144.6 0.6 copy.41
  145.2 7.7 %all-to-all-start.6 = ((f32[16,8,128]{2,1,0:T(8,128)}), f32[16,8,128]{2,1,0:T(8,128)S(1)}, u32[]{:S(2)}, u32[]{:S(2)}) async-start(f32[16,8,128]{2,1,0:T(8,128)} %bitcast.48), calls=%async_computation.6 | async-start | bytes 131072 | tf_op jit(solution)/shard_map/all_to_all | solution.py:154
  152.9 10.0 %all-to-all-done.6 = f32[16,8,128]{2,1,0:T(8,128)S(1)} async-done(((f32[16,8,128]{2,1,0:T(8,128)}), f32[16,8,128]{2,1,0:T(8,128)S(1)}, u32[]{:S(2)}, u32[]{:S(2)}) %all-to-all-start.6) | async-done | bytes 65568 | tf_op jit(solution)/shard_map/all_to_all | solution.py:154
  163.0 29.5 %all_to_all.35 = bf16[16,128,256]{2,1,0:T(8,128)(2,1)} all-to-all(bf16[16,128,256]{2,1,0:T(8,128)(2,1)S(1)} %broadcast_in_dim.51), channel_id=1, replica_groups=mesh['section'=16,'dp'=16] {'section'}, dimensions={0} | all-to-all | bytes 2097152 | tf_op jit(solution)/shard_map/all_to_all | solution.py:163
  192.5 36.8 %all_to_all.36 = bf16[16,64,640]{2,1,0:T(8,128)(2,1)S(1)} all-to-all(bf16[16,64,640]{2,1,0:T(8,128)(2,1)S(1)} %get-tuple-element.11), channel_id=1, replica_groups=mesh['section'=16,'dp'=16] {'section'}, dimensions={0} | all-to-all | bytes 2621440 | tf_op jit(solution)/shard_map/all_to_all | solution.py:155
  229.3 4.5 %all-to-all-start.4 = ((bf16[16,64,640]{2,1,0:T(8,128)(2,1)}), bf16[16,64,640]{2,1,0:T(8,128)(2,1)S(1)}, u32[]{:S(2)}, u32[]{:S(2)}) async-start(bf16[16,64,640]{2,1,0:T(8,128)(2,1)} %get-tuple-element.12), calls=%async_computation.4 | async-start | bytes 2621440 | tf_op jit(solution)/shard_map/all_to_all | solution.py:149
  233.9 0.7 collective-permute-start.7
  234.6 4.8 %collective-permute-done.7 = f32[20,128]{1,0:T(8,128)S(1)} collective-permute-done((f32[20,128]{1,0:T(8,128)S(1)}, f32[20,128]{1,0:T(8,128)S(1)}, u32[]{:S(2)}, u32[]{:S(2)}) %collective-permute-start.7) | collective-permute-done | bytes 10272 | tf_op jit(solution)/shard_map/ppermute | solution.py:93
  239.4 2.3 collective-permute-start.8
  241.7 2.9 %collective-permute-done.8 = f32[20,128]{1,0:T(8,128)S(1)} collective-permute-done((f32[20,128]{1,0:T(8,128)S(1)}, f32[20,128]{1,0:T(8,128)S(1)}, u32[]{:S(2)}, u32[]{:S(2)}) %collective-permute-start.8) | collective-permute-done | bytes 10272 | tf_op jit(solution)/shard_map/ppermute | solution.py:93
  244.7 0.4 collective-permute-start.9
  245.1 3.3 %collective-permute-done.9 = f32[20,128]{1,0:T(8,128)S(1)} collective-permute-done((f32[20,128]{1,0:T(8,128)S(1)}, f32[20,128]{1,0:T(8,128)S(1)}, u32[]{:S(2)}, u32[]{:S(2)}) %collective-permute-start.9) | collective-permute-done | bytes 10272 | tf_op jit(solution)/shard_map/ppermute | solution.py:93
  248.4 1.2 collective-permute-done.10
  249.5 0.6 copy.50
  250.1 2.1 reshape.200
  252.3 3.6 %copy.33 = bf16[2,256,2,4,128]{1,4,3,2,0:T(8,128)(2,1)} copy(bf16[2,256,2,4,128]{4,2,1,3,0:T(2,128)(2,1)} %bitcast.97) | data formatting | bytes 2097152 | tf_op jit(solution)/shard_map/transpose | solution.py:164
  255.9 2.3 copy.34
  258.2 1.0 slice_bitcast_fusion.3
  259.1 7.7 %all-to-all-done.4 = bf16[16,64,640]{2,1,0:T(8,128)(2,1)S(1)} async-done(((bf16[16,64,640]{2,1,0:T(8,128)(2,1)}), bf16[16,64,640]{2,1,0:T(8,128)(2,1)S(1)}, u32[]{:S(2)}, u32[]{:S(2)}) %all-to-all-start.4) | async-done | bytes 1310752 | tf_op jit(solution)/shard_map/all_to_all | solution.py:149
  267.0 0.4 maximum_bitcast_fusion
  267.4 2.0 copy.32
  269.4 2.4 reshape.198
  (40 shorter events, 0.7 us)
Async XLA Ops:
  2.1 21.1 %all-to-all-start.1 = ((f32[16,8,128]{2,1,0:T(8,128)}), f32[16,8,128]{2,1,0:T(8,128)S(1)}, u32[]{:S(2)}, u32[]{:S(2)}) async-start(f32[16,8,128]{2,1,0:T(8,128)} %reshape.190), calls=%async_computation.1 | async-start | bytes 131072 | tf_op jit(solution)/shard_map/all_to_all | solution.py:131
  18.1 1.5 copy-start.2
  23.2 10.1 %copy-start.5 = (bf16[1,2,256,1024]{3,2,1,0:T(8,128)(2,1)S(1)}, bf16[1,2,256,1024]{3,2,1,0:T(8,128)(2,1)}, u32[]{:S(2)}) copy-start(bf16[1,2,256,1024]{3,2,1,0:T(8,128)(2,1)} %param.7) | copy-start | bytes 3145732
  23.2 41.1 %all-to-all-start.2 = ((bf16[16,64,640]{2,1,0:T(8,128)(2,1)}), bf16[16,64,640]{2,1,0:T(8,128)(2,1)S(1)}, u32[]{:S(2)}, u32[]{:S(2)}) async-start(bf16[16,64,640]{2,1,0:T(8,128)(2,1)} %bitcast.17), calls=%async_computation.2 | async-start | bytes 2621440 | tf_op jit(solution)/shard_map/all_to_all | solution.py:135
  64.2 69.4 %all-to-all-start = ((bf16[16,64,640]{2,1,0:T(8,128)(2,1)}), bf16[16,64,640]{2,1,0:T(8,128)(2,1)S(1)}, u32[]{:S(2)}, u32[]{:S(2)}) async-start(bf16[16,64,640]{2,1,0:T(8,128)(2,1)} %bitcast.94), calls=%async_computation | async-start | bytes 2621440 | tf_op jit(solution)/shard_map/all_to_all | solution.py:136
  68.8 17.2 %copy-start.6 = (s32[2,256]{1,0:T(2,128)S(1)}, s32[2,256]{1,0:T(2,128)}, u32[]{:S(2)}) copy-start(s32[2,256]{1,0:T(2,128)} %param.8) | copy-start | bytes 6148
  73.2 15.0 %collective-permute-start.1 = (bf16[2,256,256]{2,1,0:T(8,128)(2,1)}, bf16[2,256,256]{2,1,0:T(8,128)(2,1)S(1)}, u32[]{:S(2)}, u32[]{:S(2)}) collective-permute-start(bf16[2,256,256]{2,1,0:T(8,128)(2,1)} %get-tuple-element.26), channel_id=1, source_target_pairs={{0,128},{1,129},{2,130},{3,131},{4,132},{5,133},{6,134},{7,135},{8... | collective-permute-start | bytes 786440 | tf_op jit(solution)/shard_map/ppermute | solution.py:93
  78.6 25.3 %collective-permute-start.2 = (bf16[2,256,256]{2,1,0:T(8,128)(2,1)}, bf16[2,256,256]{2,1,0:T(8,128)(2,1)S(1)}, u32[]{:S(2)}, u32[]{:S(2)}) collective-permute-start(bf16[2,256,256]{2,1,0:T(8,128)(2,1)} %get-tuple-element.27), channel_id=1, source_target_pairs={{0,192},{1,193},{2,194},{3,195},{4,196},{5,197},{6,198},{7,199},{8... | collective-permute-start | bytes 786440 | tf_op jit(solution)/shard_map/ppermute | solution.py:93
  84.1 24.5 %collective-permute-start = (bf16[2,256,256]{2,1,0:T(8,128)(2,1)}, bf16[2,256,256]{2,1,0:T(8,128)(2,1)S(1)}, u32[]{:S(2)}, u32[]{:S(2)}) collective-permute-start(bf16[2,256,256]{2,1,0:T(8,128)(2,1)} %get-tuple-element.28), channel_id=1, source_target_pairs={{0,64},{1,65},{2,66},{3,67},{4,68},{5,69},{6,70},{7,71},{8,72},{9,... | collective-permute-start | bytes 786440 | tf_op jit(solution)/shard_map/ppermute | solution.py:93
  109.5 0.7 copy-start.4
  111.0 9.7 %collective-permute-start.5 = (bf16[256,256]{1,0:T(8,128)(2,1)}, bf16[256,256]{1,0:T(8,128)(2,1)}, u32[]{:S(2)}, u32[]{:S(2)}) collective-permute-start(bf16[256,256]{1,0:T(8,128)(2,1)} %get-tuple-element.32), channel_id=1, source_target_pairs={{0,48},{64,112},{128,176},{192,240},{1,49},{65,113},{129,177},{193... | collective-permute-start | bytes 393224 | tf_op jit(solution)/shard_map/ppermute | solution.py:93
  112.9 7.7 %collective-permute-start.4 = (bf16[256,256]{1,0:T(8,128)(2,1)}, bf16[256,256]{1,0:T(8,128)(2,1)}, u32[]{:S(2)}, u32[]{:S(2)}) collective-permute-start(bf16[256,256]{1,0:T(8,128)(2,1)} %get-tuple-element.32), channel_id=1, source_target_pairs={{0,32},{64,96},{128,160},{192,224},{1,33},{65,97},{129,161},{193,2... | collective-permute-start | bytes 393224 | tf_op jit(solution)/shard_map/ppermute | solution.py:93
  114.8 5.8 %collective-permute-start.3 = (bf16[256,256]{1,0:T(8,128)(2,1)}, bf16[256,256]{1,0:T(8,128)(2,1)}, u32[]{:S(2)}, u32[]{:S(2)}) collective-permute-start(bf16[256,256]{1,0:T(8,128)(2,1)} %get-tuple-element.31), channel_id=1, source_target_pairs={{0,16},{64,80},{128,144},{192,208},{1,17},{65,81},{129,145},{193,2... | collective-permute-start | bytes 393224 | tf_op jit(solution)/shard_map/ppermute | solution.py:93
  132.9 0.7 copy-start
  133.6 1.0 copy-start.1
  142.0 10.9 %collective-permute-start.6 = (f32[128,256]{1,0:T(8,128)S(1)}, f32[128,256]{1,0:T(8,128)S(1)}, u32[]{:S(2)}, u32[]{:S(2)}) collective-permute-start(f32[128,256]{1,0:T(8,128)S(1)} %dynamic-slice_bitcast_fusion), channel_id=1, source_target_pairs={{0,16},{16,0},{32,48},{48,32},{64,80},{80,64},{96,112},{112,96},{1... | collective-permute-start | bytes 393224 | tf_op jit(solution)/shard_map/ppermute | solution.py:93
  145.2 17.7 %all-to-all-start.6 = ((f32[16,8,128]{2,1,0:T(8,128)}), f32[16,8,128]{2,1,0:T(8,128)S(1)}, u32[]{:S(2)}, u32[]{:S(2)}) async-start(f32[16,8,128]{2,1,0:T(8,128)} %bitcast.48), calls=%async_computation.6 | async-start | bytes 131072 | tf_op jit(solution)/shard_map/all_to_all | solution.py:154
  229.3 37.5 %all-to-all-start.4 = ((bf16[16,64,640]{2,1,0:T(8,128)(2,1)}), bf16[16,64,640]{2,1,0:T(8,128)(2,1)S(1)}, u32[]{:S(2)}, u32[]{:S(2)}) async-start(bf16[16,64,640]{2,1,0:T(8,128)(2,1)} %get-tuple-element.12), calls=%async_computation.4 | async-start | bytes 2621440 | tf_op jit(solution)/shard_map/all_to_all | solution.py:149
  233.9 5.5 %collective-permute-start.7 = (f32[20,128]{1,0:T(8,128)S(1)}, f32[20,128]{1,0:T(8,128)S(1)}, u32[]{:S(2)}, u32[]{:S(2)}) collective-permute-start(f32[20,128]{1,0:T(8,128)S(1)} %reshape.204), channel_id=1, source_target_pairs={{0,8},{1,9},{2,10},{3,11},{4,12},{5,13},{6,14},{7,15},{8,0},{9,1},... | collective-permute-start | bytes 30728 | tf_op jit(solution)/shard_map/ppermute | solution.py:93
  239.4 5.2 %collective-permute-start.8 = (f32[20,128]{1,0:T(8,128)S(1)}, f32[20,128]{1,0:T(8,128)S(1)}, u32[]{:S(2)}, u32[]{:S(2)}) collective-permute-start(f32[20,128]{1,0:T(8,128)S(1)} %add.108), channel_id=1, source_target_pairs={{0,4},{1,5},{2,6},{3,7},{4,0},{5,1},{6,2},{7,3},{8,12},{9,13},{10,... | collective-permute-start | bytes 30728 | tf_op jit(solution)/shard_map/ppermute | solution.py:93
  244.7 3.7 %collective-permute-start.9 = (f32[20,128]{1,0:T(8,128)S(1)}, f32[20,128]{1,0:T(8,128)S(1)}, u32[]{:S(2)}, u32[]{:S(2)}) collective-permute-start(f32[20,128]{1,0:T(8,128)S(1)} %add.109), channel_id=1, source_target_pairs={{0,2},{1,3},{2,0},{3,1},{4,6},{5,7},{6,4},{7,5},{8,10},{9,11},{10,... | collective-permute-start | bytes 30728 | tf_op jit(solution)/shard_map/ppermute | solution.py:93
  248.4 1.2 collective-permute-start.10
  259.1 7.9 %copy-start.3 = (bf16[2,1,4,64,640]{4,3,2,0,1:T(8,128)(2,1)S(1)}, bf16[2,1,4,64,640]{4,3,2,0,1:T(8,128)(2,1)}, u32[]{:S(2)}) copy-start(bf16[2,1,4,64,640]{4,3,2,0,1:T(8,128)(2,1)} %get-tuple-element.23) | copy-start | bytes 1966084

commit v2 on v1

v2 whole, which is shorter than its diff:
```python
import jax
import jax.numpy as jnp
from jax import lax
from jax.experimental import pallas as pl
from jax.experimental.pallas import tpu as pltpu
from jax.sharding import PartitionSpec as P

HEADS = 20
KV_HEADS = 4
HEAD = 128
GROUP = HEADS // KV_HEADS
WIDE = GROUP * HEAD
STACK = GROUP * 64
TAIL = 16
KEY_WIDTH = KV_HEADS * HEAD
SECTIONS = 16
RING = 8
MICROS = 2
LENGTH = 256
BLOCK = 64
LOG2E = 1.4426950408889634
SCALE = HEAD ** -0.5
MASKED = -1e30
RING_ORDER = (4, 3, 5, 2, 6, 1, 7)

VMEM = pl.BlockSpec(memory_space=pltpu.VMEM)
SMEM = pl.BlockSpec(memory_space=pltpu.SMEM)
IN_HBM = pl.BlockSpec(memory_space=pltpu.HBM)


def moved(array, pairs):
    return lax.ppermute(array, "section", pairs)


def turned(array, by):
    return moved(array, [(i, i // RING * RING + (i + by) % RING) for i in range(SECTIONS)])


def swapped(array, bit, axis="section"):
    return lax.ppermute(array, axis, [(i, i ^ bit) for i in range(16)])


def exchange(array):
    return lax.all_to_all(array, "section", 0, 0, tiled=True)


def after(array, *others):
    return lax.optimization_barrier((array, *others))[0]


def run_copies(stages):
    for first, _ in stages:
        first.start()
    for first, later in stages:
        first.wait()
        for copy in later:
            copy.start()
    for _, later in stages:
        for copy in later:
            copy.wait()


def moving_call(kernel, out_shape, scratch, in_specs, aliases=None):
    outs = out_shape if isinstance(out_shape, list) else [out_shape]
    size = sum(2 * out.size * out.dtype.itemsize for out in outs)
    out_specs = [IN_HBM] + [VMEM] * (len(outs) - 1)
    return pl.pallas_call(
        kernel,
        out_shape=out_shape,
        in_specs=in_specs,
        out_specs=out_specs if isinstance(out_shape, list) else IN_HBM,
        input_output_aliases=aliases or {},
        scratch_shapes=scratch,
        compiler_params=pltpu.CompilerParams(vmem_limit_bytes=12 * 1024 * 1024),
        cost_estimate=pl.CostEstimate(flops=0, bytes_accessed=size, transcendentals=0),
    )


def home_places(late):
    for owner in range(SECTIONS):
        micro, head, half = owner // RING, owner % RING // 2, owner % 2
        block = 3 - half if late else half
        yield owner, (micro, pl.ds(block * BLOCK, BLOCK), pl.ds(head * WIDE, WIDE))


def cache_units(cache):
    def kernel(cache_ref, out_ref, held, in_sems, out_sems):
        copies = []
        for unit in range(2 * KV_HEADS):
            micro, head = unit // KV_HEADS, unit % KV_HEADS
            for part in range(2):
                column = part * KEY_WIDTH + head * HEAD
                slot = held.at[unit, part]
                copies.append((
                    pltpu.make_async_copy(
                        cache_ref.at[micro, :, pl.ds(column, HEAD)], slot, in_sems.at[unit, part]
                    ),
                    [pltpu.make_async_copy(
                        slot, out_ref.at[unit, :, pl.ds(part * HEAD, HEAD)],
                        out_sems.at[2 * unit + part],
                    )],
                ))
        run_copies(copies)

    units = 2 * KV_HEADS
    out = jax.ShapeDtypeStruct((units, LENGTH, 2 * HEAD), cache.dtype)
    scratch = [
        pltpu.VMEM((units, 2, LENGTH, HEAD), cache.dtype),
        pltpu.SemaphoreType.DMA((units, 2)),
        pltpu.SemaphoreType.DMA((2 * units,)),
    ]
    return moving_call(kernel, out, scratch, [IN_HBM])(cache)


def cache_whole(me, near, far):
    def kernel(me_ref, near_ref, far_ref, whole_ref, held, in_sems, out_sems):
        here = me_ref[0]
        copies = []
        for side, source in enumerate((near_ref, far_ref)):
            for j in range(RING):
                owner = lax.rem(here + RING - j, RING)
                micro = lax.rem(here // RING + side, 2)
                head, half = owner // 2, lax.rem(owner, 2)
                start = pl.multiple_of(half * (LENGTH // 2), LENGTH // 2)
                later = []
                for part in range(2):
                    column = pl.multiple_of(head * HEAD + part * KEY_WIDTH, HEAD)
                    later.append(
                        pltpu.make_async_copy(
                            held.at[side, j, :, pl.ds(part * HEAD, HEAD)],
                            whole_ref.at[micro, pl.ds(start, LENGTH // 2), pl.ds(column, HEAD)],
                            out_sems.at[(side * RING + j) * 2 + part],
                        )
                    )
                first = pltpu.make_async_copy(source.at[j], held.at[side, j], in_sems.at[side, j])
                copies.append((first, later))
        run_copies(copies)

    out = jax.ShapeDtypeStruct((MICROS, LENGTH, 2 * KEY_WIDTH), near.dtype)
    scratch = [
        pltpu.VMEM((2,) + near.shape, near.dtype),
        pltpu.SemaphoreType.DMA((2, RING)),
        pltpu.SemaphoreType.DMA((4 * RING,)),
    ]
    return moving_call(kernel, out, scratch, [SMEM, IN_HBM, IN_HBM])(me.reshape(1), near, far)


def stack_heads(rows):
    return jnp.concatenate([rows[:, h * HEAD : (h + 1) * HEAD] for h in range(GROUP)], axis=0)


def unstack_heads(rows):
    return jnp.concatenate([rows[h * BLOCK : (h + 1) * BLOCK] for h in range(GROUP)], axis=1)


def three_parts(rows):
    parts = []
    for i in range(GROUP):
        left = rows[i : i + 1]
        for _ in range(3):
            part = left.astype(jnp.bfloat16).astype(jnp.float32)
            parts.append(part)
            left = left - part
    parts.append(jnp.zeros_like(parts[0]))
    return jnp.concatenate(parts, axis=0).astype(jnp.bfloat16)


def from_parts(parts):
    parts = parts.astype(jnp.float32)
    return jnp.concatenate(
        [
            parts[3 * i : 3 * i + 1] + parts[3 * i + 1 : 3 * i + 2] + parts[3 * i + 2 : 3 * i + 3]
            for i in range(GROUP)
        ],
        axis=0,
    )


def pack(whole, late, gains=None):
    tall = STACK if gains is None else STACK + TAIL

    def kernel(*refs):
        whole_ref, (out_ref, held, stacked, in_sems, out_sems) = refs[-6], refs[-5:]
        arriving = [
            pltpu.make_async_copy(whole_ref.at[place], held.at[owner], in_sems.at[owner])
            for owner, place in home_places(late)
        ]
        for copy in arriving:
            copy.start()
        leaving = []
        for owner in range(SECTIONS):
            if gains is not None:
                first = owner % RING // 2 * GROUP
                stacked[owner, STACK:] = three_parts(refs[0][first : first + GROUP])
            arriving[owner].wait()
            for h in range(GROUP):
                stacked[owner, h * BLOCK : (h + 1) * BLOCK] = held[owner, :, h * HEAD : (h + 1) * HEAD]
            copy = pltpu.make_async_copy(stacked.at[owner], out_ref.at[owner], out_sems.at[owner])
            copy.start()
            leaving.append(copy)
        for copy in leaving:
            copy.wait()

    out = jax.ShapeDtypeStruct((SECTIONS, tall, HEAD), whole.dtype)
    scratch = [
        pltpu.VMEM((SECTIONS, BLOCK, WIDE), whole.dtype),
        pltpu.VMEM(out.shape, whole.dtype),
        pltpu.SemaphoreType.DMA((SECTIONS,)),
        pltpu.SemaphoreType.DMA((SECTIONS,)),
    ]
    if gains is None:
        return moving_call(kernel, out, scratch, [IN_HBM])(whole)
    return moving_call(kernel, out, scratch, [VMEM, IN_HBM])(gains, whole)


def unpack(came, late, whole=None):
    tall = came.shape[1]

    def kernel(came_ref, *rest):
        if whole is None:
            out_ref, (held, spread, in_sems, out_sems) = rest[0], rest[1:]
        else:
            _, out_ref, gain_ref, held, spread, in_sems, out_sems = rest
        arriving = [
            pltpu.make_async_copy(came_ref.at[owner], held.at[owner], in_sems.at[owner])
            for owner in range(SECTIONS)
        ]
        for copy in arriving:
            copy.start()
        leaving = []
        for owner, place in home_places(late):
            arriving[owner].wait()
            for h in range(GROUP):
                spread[owner, :, h * HEAD : (h + 1) * HEAD] = held[owner, h * BLOCK : (h + 1) * BLOCK]
            copy = pltpu.make_async_copy(spread.at[owner], out_ref.at[place], out_sems.at[owner])
            copy.start()
            leaving.append(copy)
        if whole is not None:
            for head in range(KV_HEADS):
                total = jnp.zeros((GROUP, HEAD), jnp.float32)
                for owner in (2 * head, 2 * head + 1, RING + 2 * head, RING + 2 * head + 1):
                    total += from_parts(held[owner, STACK:])
                gain_ref[head * GROUP : (head + 1) * GROUP] = total
        for copy in leaving:
            copy.wait()

    out = jax.ShapeDtypeStruct((MICROS, LENGTH, HEADS * HEAD), came.dtype)
    scratch = [
        pltpu.VMEM(came.shape, came.dtype),
        pltpu.VMEM((SECTIONS, BLOCK, WIDE), came.dtype),
        pltpu.SemaphoreType.DMA((SECTIONS,)),
        pltpu.SemaphoreType.DMA((SECTIONS,)),
    ]
    if whole is None:
        return moving_call(kernel, out, scratch, [IN_HBM])(came)
    outs = [out, jax.ShapeDtypeStruct((HEADS, HEAD), jnp.float32)]
    return moving_call(kernel, outs, scratch, [IN_HBM, IN_HBM], {1: 0})(came, whole)


def with_gains(grads, gain_part):
    def kernel(gain_ref, _, out_ref, tails, sems):
        copies = []
        for s in range(SECTIONS):
            tails[s] = three_parts(gain_ref[s])
            copy = pltpu.make_async_copy(tails.at[s], out_ref.at[s, pl.ds(STACK, TAIL)], sems.at[s])
            copy.start()
            copies.append(copy)
        for copy in copies:
            copy.wait()

    out = jax.ShapeDtypeStruct(grads.shape, grads.dtype)
    scratch = [
        pltpu.VMEM((SECTIONS, TAIL, HEAD), grads.dtype),
        pltpu.SemaphoreType.DMA((SECTIONS,)),
    ]
    return moving_call(kernel, out, scratch, [VMEM, IN_HBM], {1: 0})(gain_part, grads)


def per_row(gains):
    return jnp.concatenate(
        [jnp.broadcast_to(gains[h : h + 1], (BLOCK, HEAD)) for h in range(GROUP)], axis=0
    )


def per_head(rows):
    sums = [
        jnp.sum(rows[h * BLOCK : (h + 1) * BLOCK], axis=0, keepdims=True) for h in range(GROUP)
    ]
    return jnp.concatenate(sums + [jnp.zeros((8 - GROUP, HEAD), jnp.float32)], axis=0)


def run_layers(saved_ref, gain_of, kv_ref, bias_ref, top_ref, grads_ref, cache_ref, add_gain):
    seen = bias_ref.shape[0]
    contract_last = (((1,), (1,)), ((), ()))
    contract_first = (((0,), (0,)), ((), ()))

    def layer(step, incoming):
        s = SECTIONS - 1 - step
        keys, values = kv_ref[:seen, :HEAD], kv_ref[:seen, HEAD:]
        gain = per_row(gain_of(s))
        saved = saved_ref[s, :STACK].astype(jnp.float32)
        queries = (saved * gain).astype(jnp.bfloat16)
        scores = lax.dot_general(keys, queries, contract_last, preferred_element_type=jnp.float32)
        scores = scores * (SCALE * LOG2E) + bias_ref[...]
        exp_terms = jnp.exp2(scores - jnp.max(scores, axis=0, keepdims=True))
        probs = exp_terms * (1.0 / jnp.sum(exp_terms, axis=0, keepdims=True))
        dprob = lax.dot_general(values, incoming, contract_last, preferred_element_type=jnp.float32)
        delta = jnp.sum(probs * dprob, axis=0, keepdims=True)
        dscore = (probs * (dprob - delta)).astype(jnp.bfloat16)
        dquery = SCALE * lax.dot_general(
            dscore, keys, contract_first, preferred_element_type=jnp.float32
        )
        cache_ref[:seen, :HEAD] += SCALE * jnp.dot(dscore, queries, preferred_element_type=jnp.float32)
        cache_ref[:seen, HEAD:] += jnp.dot(
            probs.astype(jnp.bfloat16), incoming, preferred_element_type=jnp.float32
        )
        add_gain(s, per_head(dquery * saved))
        grads = (incoming.astype(jnp.float32) + gain * dquery).astype(jnp.bfloat16)
        grads_ref[s, :STACK] = grads
        return grads

    top = jnp.concatenate([top_ref[:, h * HEAD : (h + 1) * HEAD] for h in range(GROUP)], axis=0)
    lax.fori_loop(0, SECTIONS, layer, top, unroll=2)


def late_kernel(saved_ref, kv_ref, bias_ref, top_ref, grads_ref, cache_ref, gain_ref, part_ref):
    for s in range(SECTIONS):
        gain_ref[s, :GROUP] = from_parts(saved_ref[s, STACK:])
    cache_ref[...] = jnp.zeros_like(cache_ref)

    def add_gain(s, part):
        part_ref[s] = part

    run_layers(
        saved_ref, lambda s: gain_ref[s], kv_ref, bias_ref, top_ref, grads_ref, cache_ref, add_gain
    )


def early_kernel(saved_ref, kv_ref, bias_ref, top_ref, cache_before, gain_ref, part_before,
                 grads_ref, cache_ref, part_ref):
    cache_ref[...] = cache_before[...]

    def add_gain(s, part):
        part_ref[s] = part_before[s] + part

    run_layers(
        saved_ref, lambda s: gain_ref[s], kv_ref, bias_ref, top_ref, grads_ref, cache_ref, add_gain
    )


def chain(kernel, saved, kv_unit, bias, top, grads_tall, *before):
    seen, columns = bias.shape
    shapes = [
        ((SECTIONS, grads_tall, HEAD), jnp.bfloat16),
        ((LENGTH, 2 * HEAD), jnp.float32),
        ((SECTIONS, 8, HEAD), jnp.float32),
    ]
    if not before:
        shapes.append(shapes[-1])
    return pl.pallas_call(
        kernel,
        out_shape=[jax.ShapeDtypeStruct(*shape) for shape in shapes],
        in_specs=[VMEM] * (4 + len(before)),
        out_specs=[VMEM] * len(shapes),
        compiler_params=pltpu.CompilerParams(vmem_limit_bytes=24 * 1024 * 1024),
        cost_estimate=pl.CostEstimate(
            flops=SECTIONS * 10 * columns * seen * HEAD,
            bytes_accessed=6 * 1024 * 1024,
            transcendentals=SECTIONS * columns * seen,
        ),
    )(saved, kv_unit, bias, top, *before)


def bias_of(segments, block, keys_seen):
    rows = lax.dynamic_slice(segments, (block * BLOCK,), (BLOCK,))
    key_pos = jnp.arange(keys_seen)
    query_pos = block * BLOCK + jnp.arange(BLOCK)
    allowed = (key_pos[:, None] <= query_pos[None, :]) & (
        segments[:keys_seen, None] == rows[None, :]
    )
    bias = jnp.where(allowed, 0.0, MASKED).astype(jnp.float32)
    return jnp.tile(bias, (1, GROUP))


def on_device(saved_inputs, query_gains, cache_slots, segment_ids, output_grad):
    me = lax.axis_index("section")
    micro, head, half = me // RING, me % RING // 2, me % 2

    units = cache_units(cache_slots[0])
    across = moved(units[KV_HEADS:], [(0, RING)])
    late_packed = pack(saved_inputs[0], True, query_gains.reshape(HEADS, HEAD))
    late_saved = exchange(after(late_packed, across))
    four = jnp.where(me < RING, units[:KV_HEADS], across)
    came = [moved(four[k], [(0, 2 * k), (RING, RING + 2 * k)]) for k in (2, 1, 3)]
    at_even = jnp.where(me % RING == 0, four[0], came[0] + came[1] + came[2])
    at_odd = moved(at_even, [(i, i + 1) for i in range(0, SECTIONS, 2)])
    kv_unit = jnp.where(half == 0, at_even, at_odd)
    early_packed = after(pack(saved_inputs[0], False), late_saved, at_odd)
    early_saved = exchange(early_packed)

    segments = lax.dynamic_index_in_dim(segment_ids, micro, 0, keepdims=False)
    late_block, early_block = 3 - half, half

    def top_of(block):
        start = (micro, block * BLOCK, head * WIDE)
        return lax.dynamic_slice(output_grad, start, (1, BLOCK, WIDE))[0]

    late_grads, cache_part, gains, gain_part = chain(
        late_kernel, late_saved, kv_unit, bias_of(segments, late_block, LENGTH),
        top_of(late_block), STACK,
    )
    late_home = exchange(late_grads)
    early_grads, cache_part, gain_part = chain(
        early_kernel, early_saved, kv_unit, bias_of(segments, early_block, LENGTH // 2),
        top_of(early_block), STACK + TAIL, cache_part, gains, gain_part,
    )
    halves = cache_part.reshape(2, LENGTH // 2, 2 * HEAD)
    theirs = swapped(lax.dynamic_index_in_dim(halves, 1 - half, 0, keepdims=False), 1)
    for bit in (1, 2, 4, 8):
        gain_part = gain_part + swapped(gain_part, bit, "dp")
    early_grads = with_gains(early_grads, gain_part)

    mine = lax.dynamic_index_in_dim(halves, half, 0, keepdims=False) + theirs
    mine = after(mine.astype(jnp.bfloat16), early_grads)
    ring = {0: mine}
    for r in RING_ORDER:
        ring[r] = turned(mine, r)
    early_home = exchange(after(early_grads, late_home, *(ring[r] for r in RING_ORDER)))
    whole = unpack(late_home, True)
    near = jnp.stack([ring[r] for r in range(RING)])
    cache_grad = cache_whole(me, near, swapped(near, RING))
    layer_out, gain_sum = unpack(early_home, False, whole)
    return (layer_out[None], cache_grad, gain_sum.reshape(1, HEADS * HEAD))


def solution(mesh):
    return jax.shard_map(
        on_device,
        mesh=mesh,
        in_specs=(
            P("section", "dp", None, None),
            P("section", None),
            P("section", "dp", None, None),
            P("dp", None),
            P("dp", None, None),
        ),
        out_specs=(P("section", "dp", None, None), P("dp", None, None), P("section", None)),
        check_vma=False,
    )
```

time: 273 us -> 206 us (0.75)
  blocking collectives: 66.3 us -> 0 us
  local copies, waits for them, and re-layouts: 35.8 us -> 12.3 us
  Pallas kernels: 18.5 us -> 35.3 us
  starting transfers between devices: 59.2 us -> 68.3 us
  other arithmetic: 7.58 us -> 2.31 us
    all_to_all x2 -> x0, blocking collectives: 66.3 us -> none  [the longest x1 36.8 us: on_device(): early_home = exchange(early_grads)]
    ppermute x11 -> x18, waiting for transfers between devices: 33.4 us -> 62.4 us  [the longest x12 32.2 us: moved(): return lax.ppermute(array, 'section', pairs)]
    all_to_all x5 -> x4, waiting for transfers between devices: 50 us -> 23.4 us  [exchange(): return lax.all_to_all(array, 'section', 0, 0, tiled=True)]
    ppermute x11 -> x18, starting transfers between devices: 23.9 us -> 42.6 us  [the longest x12 33.5 us: moved(): return lax.ppermute(array, 'section', pairs)]
    pallas_call x2 -> x9, Pallas kernels: 18.5 us -> 35.3 us  [the longest x2 19.8 us: chain(): pl.pallas_call(kernel, out_shape=[jax.ShapeDtypeStruct(*shape) for shape...]
    reshape x9 -> x0, local copies, waits for them, and re-layouts: 11.6 us -> none  [the longest x2 4.98 us: on_device(): saved_inputs.reshape(MICROS, 4, BLOCK, KV_HEADS, WIDE)]
    all_to_all x5 -> x4, starting transfers between devices: 35.3 us -> 25.7 us  [exchange(): return lax.all_to_all(array, 'section', 0, 0, tiled=True)]
    transpose x2 -> x0, local copies, waits for them, and re-layouts: 5.68 us -> none  [the longest x1 3.65 us: on_device(): whole.reshape(MICROS, KV_HEADS, LENGTH, 2, HEAD).transpose(0, 2, 3, 1, 4)]
  transfers between devices with their start and end apart: 16 -> 22, of which waited for: 12 -> 13; matrix products, arithmetic and copies ran while one was open for 12% -> 3% of each run, Pallas kernels for 4% -> 15%
where the time goes in v2:
time: 206 us; the launch traced here: 205 us
  waiting for transfers between devices  85.8 us (42%)
  starting transfers between devices  68.3 us (33%)
  Pallas kernels  35.3 us (17%)
  local copies, waits for them, and re-layouts  12.3 us (6%)
  other arithmetic  2.31 us (1%)
    ppermute x12, starting transfers between devices, moved(): return lax.ppermute(array, 'section', pairs)  33.5 us
    ppermute x12, waiting for transfers between devices, moved(): return lax.ppermute(array, 'section', pairs)  32.2 us
    ppermute x6, waiting for transfers between devices, swapped(): return lax.ppermute(array, axis, [(i, i ^ bit) for i in range(16)])  30.1 us
    all_to_all x4, starting transfers between devices, exchange(): return lax.all_to_all(array, 'section', 0, 0, tiled=True)  25.7 us
    all_to_all x4, waiting for transfers between devices, exchange(): return lax.all_to_all(array, 'section', 0, 0, tiled=True)  23.4 us
    pallas_call x2, Pallas kernels, chain(): pl.pallas_call(kernel, out_shape=[jax.ShapeDtypeStruct(*shape) for shape...  19.8 us
    ppermute x6, starting transfers between devices, swapped(): return lax.ppermute(array, axis, [(i, i ^ bit) for i in range(16)])  9.1 us
    unnamed x30, local copies, waits for them, and re-layouts  7.78 us
  transfers between devices with their start and end apart: 22, of which 13 were waited for; matrix products, arithmetic and copies ran while one was open for 3% of the time, Pallas kernels for 15%

profile of v2, /device:TPU:8, one launch (start us, length us, event | category | flops | bytes accessed | tf_op | source)
XLA Modules:
  0.0 205.2 jit_solution(13062369818441306628)
XLA Ops:
  0.6 1.2 copy-done.5
  1.9 0.8 shard_map.78
  2.7 0.0 copy-start.3
  2.7 1.0 copy-done.3
  3.6 0.8 slice.29
  4.5 4.9 %collective-permute-start = (bf16[4,256,256]{2,1,0:T(8,128)(2,1)}, bf16[4,256,256]{2,1,0:T(8,128)(2,1)S(1)}, u32[]{:S(2)}, u32[]{:S(2)}) collective-permute-start(bf16[4,256,256]{2,1,0:T(8,128)(2,1)} %slice.29), channel_id=1, source_target_pairs={{0,128},{1,129},{2,130},{3,131},{4,132},{5,133},{6,134},{7,135},{8... | collective-permute-start | bytes 1572872 | tf_op jit(solution)/shard_map/ppermute | solution.py:32
  9.5 2.7 %shard_map.77 = bf16[16,336,128]{2,1,0:T(8,128)(2,1)S(1)} custom-call(f32[20,128]{1,0:T(8,128)S(1)} %bitcast.61, bf16[2,256,2560]{2,1,0:T(8,128)(2,1)S(1)} %bitcast.56), custom_call_target="tpu_custom_call" | custom-call | bytes 2752512 | tf_op jit(solution)/shard_map/pallas_call | solution.py:213
  12.2 0.0 copy-start.1
  12.2 1.1 copy-done.1
  13.3 7.6 %collective-permute-done = bf16[4,256,256]{2,1,0:T(8,128)(2,1)S(1)} collective-permute-done((bf16[4,256,256]{2,1,0:T(8,128)(2,1)}, bf16[4,256,256]{2,1,0:T(8,128)(2,1)S(1)}, u32[]{:S(2)}, u32[]{:S(2)}) %collective-permute-start) | collective-permute-done | bytes 524320 | tf_op jit(solution)/shard_map/ppermute | solution.py:32
  20.9 0.8 copy-done.8
  21.7 5.3 %all-to-all-start = ((bf16[16,336,128]{2,1,0:T(8,128)(2,1)}), bf16[16,336,128]{2,1,0:T(8,128)(2,1)}, u32[]{:S(2)}, u32[]{:S(2)}) async-start(bf16[16,336,128]{2,1,0:T(8,128)(2,1)} %copy-done.1), calls=%async_computation | async-start | bytes 2752512 | tf_op jit(solution)/shard_map/all_to_all | solution.py:44
  27.0 1.1 slice_select_fusion
  28.1 0.7 slice_bitcast_fusion.1
  28.8 5.9 %collective-permute-start.3 = (bf16[256,256]{1,0:T(8,128)(2,1)}, bf16[256,256]{1,0:T(8,128)(2,1)S(1)}, u32[]{:S(2)}, u32[]{:S(2)}) collective-permute-start(bf16[256,256]{1,0:T(8,128)(2,1)} %get-tuple-element.32), channel_id=1, source_target_pairs={{0,96},{128,224},{1,97},{129,225},{2,98},{130,226},{3,99},{131,227... | collective-permute-start | bytes 393224 | tf_op jit(solution)/shard_map/ppermute | solution.py:32
  34.7 2.5 %collective-permute-start.1 = (bf16[256,256]{1,0:T(8,128)(2,1)}, bf16[256,256]{1,0:T(8,128)(2,1)S(1)}, u32[]{:S(2)}, u32[]{:S(2)}) collective-permute-start(bf16[256,256]{1,0:T(8,128)(2,1)} %get-tuple-element.33), channel_id=1, source_target_pairs={{0,64},{128,192},{1,65},{129,193},{2,66},{130,194},{3,67},{131,195... | collective-permute-start | bytes 393224 | tf_op jit(solution)/shard_map/ppermute | solution.py:32
  37.2 2.0 collective-permute-start.2
  39.1 19.4 %collective-permute-done.3 = bf16[256,256]{1,0:T(8,128)(2,1)S(1)} collective-permute-done((bf16[256,256]{1,0:T(8,128)(2,1)}, bf16[256,256]{1,0:T(8,128)(2,1)S(1)}, u32[]{:S(2)}, u32[]{:S(2)}) %collective-permute-start.3) | collective-permute-done | bytes 131104 | tf_op jit(solution)/shard_map/ppermute | solution.py:32
  58.5 1.5 collective-permute-done.1
  60.0 1.3 collective-permute-done.2
  61.3 0.9 fusion
  62.2 1.3 collective-permute-start.4
  63.5 2.4 %shard_map.76 = bf16[16,320,128]{2,1,0:T(8,128)(2,1)S(1)} custom-call(bf16[2,256,2560]{2,1,0:T(8,128)(2,1)S(1)} %bitcast.57), custom_call_target="tpu_custom_call" | custom-call | bytes 2621440 | tf_op jit(solution)/shard_map/pallas_call | solution.py:212
  66.0 1.1 copy-done.2
  67.1 9.1 %all-to-all-start.1 = ((bf16[16,320,128]{2,1,0:T(8,128)(2,1)}), bf16[16,320,128]{2,1,0:T(8,128)(2,1)S(1)}, u32[]{:S(2)}, u32[]{:S(2)}) async-start(bf16[16,320,128]{2,1,0:T(8,128)(2,1)} %copy-done.2), calls=%async_computation.1 | async-start | bytes 2621440 | tf_op jit(solution)/shard_map/all_to_all | solution.py:44
  76.3 0.1 dynamic-slice_bitcast_fusion.3
  76.3 0.1 fusion.3
  76.5 0.2 copy.10.bias_ref
  76.6 1.0 dynamic-slice_bitcast_fusion.1
  77.6 11.3 %shard_map.79 = (bf16[16,320,128]{2,1,0:T(8,128)(2,1)S(1)}, f32[256,256]{1,0:T(8,128)S(1)}, f32[16,8,128]{2,1,0:T(8,128)S(1)}, f32[16,8,128]{2,1,0:T(8,128)S(1)}) custom-call(bf16[16,336,128]{2,1,0:T(8,128)(2,1)} %all-to-all-done.saved_ref, bf16[256,256]{1,0:T(8,128)(2,1)S(1)} %broadcast_select_fusion.kv_ref, f32[256,320]{1,0:T(8,128)S(1)} %copy.10.bias_ref, ...), custom_call_target="tpu_custom_call" | custom-call | flops 1677721600 | bytes 6291456 | tf_op jit(solution)/shard_map/pallas_call | solution.py:360
  88.9 1.0 copy-done.4
  90.0 16.4 %all-to-all-done.1.saved_ref = bf16[16,320,128]{2,1,0:T(8,128)(2,1)S(1)} async-done(((bf16[16,320,128]{2,1,0:T(8,128)(2,1)}), bf16[16,320,128]{2,1,0:T(8,128)(2,1)S(1)}, u32[]{:S(2)}, u32[]{:S(2)}) %all-to-all-start.1) | async-done | bytes 1310752 | tf_op jit(solution)/shard_map/all_to_all | solution.py:44
  106.4 4.6 %all-to-all-start.2 = ((bf16[16,320,128]{2,1,0:T(8,128)(2,1)}), bf16[16,320,128]{2,1,0:T(8,128)(2,1)S(1)}, u32[]{:S(2)}, u32[]{:S(2)}) async-start(bf16[16,320,128]{2,1,0:T(8,128)(2,1)} %copy-done.4), calls=%async_computation.2 | async-start | bytes 2621440 | tf_op jit(solution)/shard_map/all_to_all | solution.py:44
  111.0 0.1 fusion.5
  111.1 0.7 tile.8
  111.8 1.0 copy.11.bias_ref
  112.8 0.9 copy-done.7
  113.8 8.5 %shard_map.80 = (bf16[16,336,128]{2,1,0:T(8,128)(2,1)}, f32[256,256]{1,0:T(8,128)S(1)}, f32[16,8,128]{2,1,0:T(8,128)S(1)}) custom-call(bf16[16,320,128]{2,1,0:T(8,128)(2,1)S(1)} %all-to-all-done.1.saved_ref, bf16[256,256]{1,0:T(8,128)(2,1)S(1)} %broadcast_select_fusion.kv_ref, f32[128,320]{1,0:T(8,128)S(1)} %copy.11.bias_ref, ...), custom_call_target="tpu_custom_call" | custom-call | flops 838860800 | bytes 6291456 | tf_op jit(solution)/shard_map/pallas_call | solution.py:360
  122.3 1.3 collective-permute-done.5
  123.5 0.5 collective-permute-start.6
  124.1 2.0 collective-permute-start.9
  126.1 1.8 collective-permute-done.6
  127.9 2.4 %collective-permute-start.7 = (f32[16,8,128]{2,1,0:T(8,128)S(1)}, f32[16,8,128]{2,1,0:T(8,128)S(1)}, u32[]{:S(2)}, u32[]{:S(2)}) collective-permute-start(f32[16,8,128]{2,1,0:T(8,128)S(1)} %add.92), channel_id=1, source_target_pairs={{0,4},{1,5},{2,6},{3,7},{4,0},{5,1},{6,2},{7,3},{8,12},{9,13},{10,... | collective-permute-start | bytes 196616 | tf_op jit(solution)/shard_map/ppermute | solution.py:40
  130.3 3.5 %collective-permute-done.7 = f32[16,8,128]{2,1,0:T(8,128)S(1)} collective-permute-done((f32[16,8,128]{2,1,0:T(8,128)S(1)}, f32[16,8,128]{2,1,0:T(8,128)S(1)}, u32[]{:S(2)}, u32[]{:S(2)}) %collective-permute-start.7) | collective-permute-done | bytes 65568 | tf_op jit(solution)/shard_map/ppermute | solution.py:40
  133.8 0.7 collective-permute-start.8
  134.4 7.1 %collective-permute-done.9 = f32[128,256]{1,0:T(8,128)S(1)} collective-permute-done((f32[128,256]{1,0:T(8,128)S(1)}, f32[128,256]{1,0:T(8,128)S(1)}, u32[]{:S(2)}, u32[]{:S(2)}) %collective-permute-start.9) | collective-permute-done | bytes 131104 | tf_op jit(solution)/shard_map/ppermute | solution.py:40
  141.6 0.8 shard_map.81
  142.4 4.6 %collective-permute-start.10 = (bf16[128,256]{1,0:T(8,128)(2,1)S(1)}, bf16[128,256]{1,0:T(8,128)(2,1)S(1)}, u32[]{:S(2)}, u32[]{:S(2)}) collective-permute-start(bf16[128,256]{1,0:T(8,128)(2,1)S(1)} %fusion.1), channel_id=1, source_target_pairs={{0,64},{16,80},{32,96},{48,112},{64,0},{80,16},{96,32},{112,48},{1... | collective-permute-start | bytes 196616 | tf_op jit(solution)/shard_map/ppermute | solution.py:32
  146.9 1.5 collective-permute-start.11
  148.4 3.6 %collective-permute-start.12 = (bf16[128,256]{1,0:T(8,128)(2,1)S(1)}, bf16[128,256]{1,0:T(8,128)(2,1)S(1)}, u32[]{:S(2)}, u32[]{:S(2)}) collective-permute-start(bf16[128,256]{1,0:T(8,128)(2,1)S(1)} %fusion.1), channel_id=1, source_target_pairs={{0,80},{16,96},{32,112},{48,0},{64,16},{80,32},{96,48},{112,64},{1... | collective-permute-start | bytes 196616 | tf_op jit(solution)/shard_map/ppermute | solution.py:32
  152.0 0.3 collective-permute-start.13
  152.3 3.8 %collective-permute-start.14 = (bf16[128,256]{1,0:T(8,128)(2,1)S(1)}, bf16[128,256]{1,0:T(8,128)(2,1)S(1)}, u32[]{:S(2)}, u32[]{:S(2)}) collective-permute-start(bf16[128,256]{1,0:T(8,128)(2,1)S(1)} %fusion.1), channel_id=1, source_target_pairs={{0,96},{16,112},{32,0},{48,16},{64,32},{80,48},{96,64},{112,80},{1... | collective-permute-start | bytes 196616 | tf_op jit(solution)/shard_map/ppermute | solution.py:32
  156.1 1.5 collective-permute-start.15
  157.6 1.8 collective-permute-start.16
  159.4 2.2 %collective-permute-done.15 = bf16[128,256]{1,0:T(8,128)(2,1)S(1)} collective-permute-done((bf16[128,256]{1,0:T(8,128)(2,1)S(1)}, bf16[128,256]{1,0:T(8,128)(2,1)S(1)}, u32[]{:S(2)}, u32[]{:S(2)}) %collective-permute-start.15) | collective-permute-done | bytes 65568 | tf_op jit(solution)/shard_map/ppermute | solution.py:32
  161.6 0.3 collective-permute-done.16
  161.8 6.8 %all-to-all-start.3 = ((bf16[16,336,128]{2,1,0:T(8,128)(2,1)}), bf16[16,336,128]{2,1,0:T(8,128)(2,1)S(1)}, u32[]{:S(2)}, u32[]{:S(2)}) async-start(bf16[16,336,128]{2,1,0:T(8,128)(2,1)} %shard_map.81), calls=%async_computation.3 | async-start | bytes 2752512 | tf_op jit(solution)/shard_map/all_to_all | solution.py:44
  168.7 3.5 %collective-permute-start.17 = (bf16[8,128,256]{2,1,0:T(8,128)(2,1)S(1)}, bf16[8,128,256]{2,1,0:T(8,128)(2,1)S(1)}, u32[]{:S(2)}, u32[]{:S(2)}) collective-permute-start(bf16[8,128,256]{2,1,0:T(8,128)(2,1)S(1)} %bitcast_dynamic-update-slice_fusion.near_ref), channel_id=1, source_target_pairs={{0,128},{16,144},{32,160},{48,176},{64,192},{80,208},{96,224},{112... | collective-permute-start | bytes 1572872 | tf_op jit(solution)/shard_map/ppermute | solution.py:40
  172.3 3.0 %shard_map.82.rest_0_ = bf16[2,256,2560]{2,1,0:T(8,128)(2,1)} custom-call(bf16[16,320,128]{2,1,0:T(8,128)(2,1)S(1)} %all-to-all-done.2.came_ref), custom_call_target="tpu_custom_call" | custom-call | bytes 5242880 | tf_op jit(solution)/shard_map/pallas_call | solution.py:255
  175.3 16.5 %collective-permute-done.17.far_ref = bf16[8,128,256]{2,1,0:T(8,128)(2,1)S(1)} collective-permute-done((bf16[8,128,256]{2,1,0:T(8,128)(2,1)S(1)}, bf16[8,128,256]{2,1,0:T(8,128)(2,1)S(1)}, u32[]{:S(2)}, u32[]{:S(2)}) %collective-permute-start.17) | collective-permute-done | bytes 524320 | tf_op jit(solution)/shard_map/ppermute | solution.py:40
  191.8 2.7 %shard_map.84 = bf16[2,256,1024]{2,1,0:T(8,128)(2,1)} custom-call(s32[1]{0:T(128)} %bitcast.18.me_ref, bf16[8,128,256]{2,1,0:T(8,128)(2,1)S(1)} %bitcast_dynamic-update-slice_fusion.near_ref, bf16[8,128,256]{2,1,0:T(8,128)(2,1)S(1)} %collective-permute-done.17.far_ref), custom_call_target="tpu_custom_call" | custom-call | bytes 2097152 | tf_op jit(solution)/shard_map/pallas_call | solution.py:145
  194.5 7.0 %all-to-all-done.3.came_ref = bf16[16,336,128]{2,1,0:T(8,128)(2,1)S(1)} async-done(((bf16[16,336,128]{2,1,0:T(8,128)(2,1)}), bf16[16,336,128]{2,1,0:T(8,128)(2,1)S(1)}, u32[]{:S(2)}, u32[]{:S(2)}) %all-to-all-start.3) | async-done | bytes 1376288 | tf_op jit(solution)/shard_map/all_to_all | solution.py:44
  201.5 3.1 %shard_map.83 = (bf16[2,256,2560]{2,1,0:T(8,128)(2,1)}, f32[20,128]{1,0:T(8,128)S(1)}) custom-call(bf16[16,336,128]{2,1,0:T(8,128)(2,1)S(1)} %all-to-all-done.3.came_ref, bf16[2,256,2560]{2,1,0:T(8,128)(2,1)} %shard_map.82.rest_0_), custom_call_target="tpu_custom_call", output_to_operand_aliasing={{0}: (1, {})} | custom-call | bytes 5263360 | tf_op jit(solution)/shard_map/pallas_call | solution.py:257
  204.6 0.6 copy.14
  (44 shorter events, 0.3 us)
Async XLA Ops:
  0.6 1.2 copy-start.5
  1.9 7.6 %copy-start.9 = (f32[1,2560]{1,0:T(1,128)S(1)}, f32[1,2560]{1,0:T(1,128)}, u32[]{:S(2)}) copy-start(f32[1,2560]{1,0:T(1,128)} %param.6) | copy-start | bytes 30724
  1.9 7.6 %copy-start = (bf16[1,2,256,2560]{3,2,1,0:T(8,128)(2,1)S(1)}, bf16[1,2,256,2560]{3,2,1,0:T(8,128)(2,1)}, u32[]{:S(2)}) copy-start(bf16[1,2,256,2560]{3,2,1,0:T(8,128)(2,1)} %param.5) | copy-start | bytes 7864324
  2.7 1.0 copy-start.3
  4.5 16.4 %collective-permute-start = (bf16[4,256,256]{2,1,0:T(8,128)(2,1)}, bf16[4,256,256]{2,1,0:T(8,128)(2,1)S(1)}, u32[]{:S(2)}, u32[]{:S(2)}) collective-permute-start(bf16[4,256,256]{2,1,0:T(8,128)(2,1)} %slice.29), channel_id=1, source_target_pairs={{0,128},{1,129},{2,130},{3,131},{4,132},{5,133},{6,134},{7,135},{8... | collective-permute-start | bytes 1572872 | tf_op jit(solution)/shard_map/ppermute | solution.py:32
  12.2 1.1 copy-start.1
  20.9 0.8 copy-start.8
  21.7 45.4 %all-to-all-start = ((bf16[16,336,128]{2,1,0:T(8,128)(2,1)}), bf16[16,336,128]{2,1,0:T(8,128)(2,1)}, u32[]{:S(2)}, u32[]{:S(2)}) async-start(bf16[16,336,128]{2,1,0:T(8,128)(2,1)} %copy-done.1), calls=%async_computation | async-start | bytes 2752512 | tf_op jit(solution)/shard_map/all_to_all | solution.py:44
  28.8 29.7 %collective-permute-start.3 = (bf16[256,256]{1,0:T(8,128)(2,1)}, bf16[256,256]{1,0:T(8,128)(2,1)S(1)}, u32[]{:S(2)}, u32[]{:S(2)}) collective-permute-start(bf16[256,256]{1,0:T(8,128)(2,1)} %get-tuple-element.32), channel_id=1, source_target_pairs={{0,96},{128,224},{1,97},{129,225},{2,98},{130,226},{3,99},{131,227... | collective-permute-start | bytes 393224 | tf_op jit(solution)/shard_map/ppermute | solution.py:32
  34.7 25.3 %collective-permute-start.1 = (bf16[256,256]{1,0:T(8,128)(2,1)}, bf16[256,256]{1,0:T(8,128)(2,1)S(1)}, u32[]{:S(2)}, u32[]{:S(2)}) collective-permute-start(bf16[256,256]{1,0:T(8,128)(2,1)} %get-tuple-element.33), channel_id=1, source_target_pairs={{0,64},{128,192},{1,65},{129,193},{2,66},{130,194},{3,67},{131,195... | collective-permute-start | bytes 393224 | tf_op jit(solution)/shard_map/ppermute | solution.py:32
  37.2 24.1 %collective-permute-start.2 = (bf16[256,256]{1,0:T(8,128)(2,1)S(1)}, bf16[256,256]{1,0:T(8,128)(2,1)}, u32[]{:S(2)}, u32[]{:S(2)}) collective-permute-start(bf16[256,256]{1,0:T(8,128)(2,1)S(1)} %get-tuple-element.31), channel_id=1, source_target_pairs={{0,32},{128,160},{1,33},{129,161},{2,34},{130,162},{3,35},{131,163... | collective-permute-start | bytes 393224 | tf_op jit(solution)/shard_map/ppermute | solution.py:32
  62.2 4.8 %collective-permute-start.4 = (bf16[256,256]{1,0:T(8,128)(2,1)S(1)}, bf16[256,256]{1,0:T(8,128)(2,1)S(1)}, u32[]{:S(2)}, u32[]{:S(2)}) collective-permute-start(bf16[256,256]{1,0:T(8,128)(2,1)S(1)} %fusion), channel_id=1, source_target_pairs={{0,16},{32,48},{64,80},{96,112},{128,144},{160,176},{192,208},{224... | collective-permute-start | bytes 393224 | tf_op jit(solution)/shard_map/ppermute | solution.py:32
  66.0 1.1 copy-start.2
  67.1 9.2 %copy-start.10 = (s32[2,256]{1,0:T(2,128)S(1)}, s32[2,256]{1,0:T(2,128)}, u32[]{:S(2)}) copy-start(s32[2,256]{1,0:T(2,128)} %param.8) | copy-start | bytes 6148
  67.1 39.3 %all-to-all-start.1 = ((bf16[16,320,128]{2,1,0:T(8,128)(2,1)}), bf16[16,320,128]{2,1,0:T(8,128)(2,1)S(1)}, u32[]{:S(2)}, u32[]{:S(2)}) async-start(bf16[16,320,128]{2,1,0:T(8,128)(2,1)} %copy-done.2), calls=%async_computation.1 | async-start | bytes 2621440 | tf_op jit(solution)/shard_map/all_to_all | solution.py:44
  88.9 1.1 copy-start.4
  90.0 21.8 %copy-start.6 = (f32[256,256]{1,0:T(8,128)}, f32[256,256]{1,0:T(8,128)S(1)}, u32[]{:S(2)}) copy-start(f32[256,256]{1,0:T(8,128)S(1)} %get-tuple-element.18.cache_before) | copy-start | bytes 786436
  106.4 53.0 %all-to-all-start.2 = ((bf16[16,320,128]{2,1,0:T(8,128)(2,1)}), bf16[16,320,128]{2,1,0:T(8,128)(2,1)S(1)}, u32[]{:S(2)}, u32[]{:S(2)}) async-start(bf16[16,320,128]{2,1,0:T(8,128)(2,1)} %copy-done.4), calls=%async_computation.2 | async-start | bytes 2621440 | tf_op jit(solution)/shard_map/all_to_all | solution.py:44
  112.8 1.0 copy-start.7
  122.3 1.3 collective-permute-start.5
  123.5 4.4 %collective-permute-start.6 = (f32[16,8,128]{2,1,0:T(8,128)S(1)}, f32[16,8,128]{2,1,0:T(8,128)S(1)}, u32[]{:S(2)}, u32[]{:S(2)}) collective-permute-start(f32[16,8,128]{2,1,0:T(8,128)S(1)} %add.91), channel_id=1, source_target_pairs={{0,2},{1,3},{2,0},{3,1},{4,6},{5,7},{6,4},{7,5},{8,10},{9,11},{10,... | collective-permute-start | bytes 196616 | tf_op jit(solution)/shard_map/ppermute | solution.py:40
  124.1 17.4 %collective-permute-start.9 = (f32[128,256]{1,0:T(8,128)S(1)}, f32[128,256]{1,0:T(8,128)S(1)}, u32[]{:S(2)}, u32[]{:S(2)}) collective-permute-start(f32[128,256]{1,0:T(8,128)S(1)} %dynamic-slice_bitcast_fusion), channel_id=1, source_target_pairs={{0,16},{16,0},{32,48},{48,32},{64,80},{80,64},{96,112},{112,96},{1... | collective-permute-start | bytes 393224 | tf_op jit(solution)/shard_map/ppermute | solution.py:40
  127.9 5.9 %collective-permute-start.7 = (f32[16,8,128]{2,1,0:T(8,128)S(1)}, f32[16,8,128]{2,1,0:T(8,128)S(1)}, u32[]{:S(2)}, u32[]{:S(2)}) collective-permute-start(f32[16,8,128]{2,1,0:T(8,128)S(1)} %add.92), channel_id=1, source_target_pairs={{0,4},{1,5},{2,6},{3,7},{4,0},{5,1},{6,2},{7,3},{8,12},{9,13},{10,... | collective-permute-start | bytes 196616 | tf_op jit(solution)/shard_map/ppermute | solution.py:40
  133.8 7.8 %collective-permute-start.8 = (f32[16,8,128]{2,1,0:T(8,128)S(1)}, f32[16,8,128]{2,1,0:T(8,128)S(1)}, u32[]{:S(2)}, u32[]{:S(2)}) collective-permute-start(f32[16,8,128]{2,1,0:T(8,128)S(1)} %add.93), channel_id=1, source_target_pairs={{0,8},{1,9},{2,10},{3,11},{4,12},{5,13},{6,14},{7,15},{8,0},{9,1},... | collective-permute-start | bytes 196616 | tf_op jit(solution)/shard_map/ppermute | solution.py:40
  142.4 13.7 %collective-permute-start.10 = (bf16[128,256]{1,0:T(8,128)(2,1)S(1)}, bf16[128,256]{1,0:T(8,128)(2,1)S(1)}, u32[]{:S(2)}, u32[]{:S(2)}) collective-permute-start(bf16[128,256]{1,0:T(8,128)(2,1)S(1)} %fusion.1), channel_id=1, source_target_pairs={{0,64},{16,80},{32,96},{48,112},{64,0},{80,16},{96,32},{112,48},{1... | collective-permute-start | bytes 196616 | tf_op jit(solution)/shard_map/ppermute | solution.py:32
  146.9 10.6 %collective-permute-start.11 = (bf16[128,256]{1,0:T(8,128)(2,1)S(1)}, bf16[128,256]{1,0:T(8,128)(2,1)S(1)}, u32[]{:S(2)}, u32[]{:S(2)}) collective-permute-start(bf16[128,256]{1,0:T(8,128)(2,1)S(1)} %fusion.1), channel_id=1, source_target_pairs={{0,48},{16,64},{32,80},{48,96},{64,112},{80,0},{96,16},{112,32},{1... | collective-permute-start | bytes 196616 | tf_op jit(solution)/shard_map/ppermute | solution.py:32
  148.4 11.0 %collective-permute-start.12 = (bf16[128,256]{1,0:T(8,128)(2,1)S(1)}, bf16[128,256]{1,0:T(8,128)(2,1)S(1)}, u32[]{:S(2)}, u32[]{:S(2)}) collective-permute-start(bf16[128,256]{1,0:T(8,128)(2,1)S(1)} %fusion.1), channel_id=1, source_target_pairs={{0,80},{16,96},{32,112},{48,0},{64,16},{80,32},{96,48},{112,64},{1... | collective-permute-start | bytes 196616 | tf_op jit(solution)/shard_map/ppermute | solution.py:32
  152.0 7.4 %collective-permute-start.13 = (bf16[128,256]{1,0:T(8,128)(2,1)S(1)}, bf16[128,256]{1,0:T(8,128)(2,1)S(1)}, u32[]{:S(2)}, u32[]{:S(2)}) collective-permute-start(bf16[128,256]{1,0:T(8,128)(2,1)S(1)} %fusion.1), channel_id=1, source_target_pairs={{0,32},{16,48},{32,64},{48,80},{64,96},{80,112},{96,0},{112,16},{1... | collective-permute-start | bytes 196616 | tf_op jit(solution)/shard_map/ppermute | solution.py:32
  152.3 7.1 %collective-permute-start.14 = (bf16[128,256]{1,0:T(8,128)(2,1)S(1)}, bf16[128,256]{1,0:T(8,128)(2,1)S(1)}, u32[]{:S(2)}, u32[]{:S(2)}) collective-permute-start(bf16[128,256]{1,0:T(8,128)(2,1)S(1)} %fusion.1), channel_id=1, source_target_pairs={{0,96},{16,112},{32,0},{48,16},{64,32},{80,48},{96,64},{112,80},{1... | collective-permute-start | bytes 196616 | tf_op jit(solution)/shard_map/ppermute | solution.py:32
  156.1 5.5 %collective-permute-start.15 = (bf16[128,256]{1,0:T(8,128)(2,1)S(1)}, bf16[128,256]{1,0:T(8,128)(2,1)S(1)}, u32[]{:S(2)}, u32[]{:S(2)}) collective-permute-start(bf16[128,256]{1,0:T(8,128)(2,1)S(1)} %fusion.1), channel_id=1, source_target_pairs={{0,16},{16,32},{32,48},{48,64},{64,80},{80,96},{96,112},{112,0},{1... | collective-permute-start | bytes 196616 | tf_op jit(solution)/shard_map/ppermute | solution.py:32
  157.6 4.3 %collective-permute-start.16 = (bf16[128,256]{1,0:T(8,128)(2,1)S(1)}, bf16[128,256]{1,0:T(8,128)(2,1)S(1)}, u32[]{:S(2)}, u32[]{:S(2)}) collective-permute-start(bf16[128,256]{1,0:T(8,128)(2,1)S(1)} %fusion.1), channel_id=1, source_target_pairs={{0,112},{16,0},{32,16},{48,32},{64,48},{80,64},{96,80},{112,96},{1... | collective-permute-start | bytes 196616 | tf_op jit(solution)/shard_map/ppermute | solution.py:32
  161.8 39.7 %all-to-all-start.3 = ((bf16[16,336,128]{2,1,0:T(8,128)(2,1)}), bf16[16,336,128]{2,1,0:T(8,128)(2,1)S(1)}, u32[]{:S(2)}, u32[]{:S(2)}) async-start(bf16[16,336,128]{2,1,0:T(8,128)(2,1)} %shard_map.81), calls=%async_computation.3 | async-start | bytes 2752512 | tf_op jit(solution)/shard_map/all_to_all | solution.py:44
  168.7 23.0 %collective-permute-start.17 = (bf16[8,128,256]{2,1,0:T(8,128)(2,1)S(1)}, bf16[8,128,256]{2,1,0:T(8,128)(2,1)S(1)}, u32[]{:S(2)}, u32[]{:S(2)}) collective-permute-start(bf16[8,128,256]{2,1,0:T(8,128)(2,1)S(1)} %bitcast_dynamic-update-slice_fusion.near_ref), channel_id=1, source_target_pairs={{0,128},{16,144},{32,160},{48,176},{64,192},{80,208},{96,224},{112... | collective-permute-start | bytes 1572872 | tf_op jit(solution)/shard_map/ppermute | solution.py:40

commit v3 on v2

--- a/solution.py
+++ b/solution.py
@@ -22,6 +22,10 @@
 SCALE = HEAD ** -0.5
 MASKED = -1e30
 RING_ORDER = (4, 3, 5, 2, 6, 1, 7)
+UNITS_FLOPS = 40_000_000_000
+ALL_ROOM = 56 * 1024 * 1024
+SOME_ROOM = 12 * 1024 * 1024
+GATHERED = ((0, 4), (1, 5), (7, 3), (2,), (6,))
 
 VMEM = pl.BlockSpec(memory_space=pltpu.VMEM)
 SMEM = pl.BlockSpec(memory_space=pltpu.SMEM)
@@ -60,7 +64,7 @@
             copy.wait()
 
 
-def moving_call(kernel, out_shape, scratch, in_specs, aliases=None):
+def moving_call(kernel, out_shape, scratch, in_specs, aliases=None, room=SOME_ROOM):
     outs = out_shape if isinstance(out_shape, list) else [out_shape]
     size = sum(2 * out.size * out.dtype.itemsize for out in outs)
     out_specs = [IN_HBM] + [VMEM] * (len(outs) - 1)
@@ -71,7 +75,7 @@
         out_specs=out_specs if isinstance(out_shape, list) else IN_HBM,
         input_output_aliases=aliases or {},
         scratch_shapes=scratch,
-        compiler_params=pltpu.CompilerParams(vmem_limit_bytes=12 * 1024 * 1024),
+        compiler_params=pltpu.CompilerParams(vmem_limit_bytes=room),
         cost_estimate=pl.CostEstimate(flops=0, bytes_accessed=size, transcendentals=0),
     )
 
@@ -83,74 +87,84 @@
         yield owner, (micro, pl.ds(block * BLOCK, BLOCK), pl.ds(head * WIDE, WIDE))
 
 
-def cache_units(cache):
-    def kernel(cache_ref, out_ref, held, in_sems, out_sems):
-        copies = []
-        for unit in range(2 * KV_HEADS):
-            micro, head = unit // KV_HEADS, unit % KV_HEADS
-            for part in range(2):
-                column = part * KEY_WIDTH + head * HEAD
-                slot = held.at[unit, part]
-                copies.append((
-                    pltpu.make_async_copy(
-                        cache_ref.at[micro, :, pl.ds(column, HEAD)], slot, in_sems.at[unit, part]
-                    ),
-                    [pltpu.make_async_copy(
-                        slot, out_ref.at[unit, :, pl.ds(part * HEAD, HEAD)],
-                        out_sems.at[2 * unit + part],
-                    )],
-                ))
-        run_copies(copies)
-
-    units = 2 * KV_HEADS
-    out = jax.ShapeDtypeStruct((units, LENGTH, 2 * HEAD), cache.dtype)
-    scratch = [
-        pltpu.VMEM((units, 2, LENGTH, HEAD), cache.dtype),
-        pltpu.SemaphoreType.DMA((units, 2)),
-        pltpu.SemaphoreType.DMA((2 * units,)),
-    ]
-    return moving_call(kernel, out, scratch, [IN_HBM])(cache)
-
-
-def cache_whole(me, near, far):
-    def kernel(me_ref, near_ref, far_ref, whole_ref, held, in_sems, out_sems):
+def own_units(me, raw, across):
+    def kernel(me_ref, raw_ref, across_ref, *rest):
+        out_refs, (held, in_sems, out_sems) = rest[:KV_HEADS], rest[KV_HEADS:]
+
+        def take(source):
+            copies = []
+            for head in range(KV_HEADS):
+                for part in range(2):
+                    column = part * KEY_WIDTH + head * HEAD
+                    slot = held.at[head, part]
+                    copies.append((
+                        pltpu.make_async_copy(
+                            source.at[:, pl.ds(column, HEAD)], slot, in_sems.at[head, part]
+                        ),
+                        [pltpu.make_async_copy(
+                            slot, out_refs[head].at[:, pl.ds(part * HEAD, HEAD)],
+                            out_sems.at[head, part],
+                        )],
+                    ))
+            run_copies(copies)
+
+        pl.when(me_ref[0] < RING)(lambda: take(raw_ref.at[0]))
+        pl.when(me_ref[0] >= RING)(lambda: take(across_ref))
+
+    return pl.pallas_call(
+        kernel,
+        out_shape=[jax.ShapeDtypeStruct((LENGTH, 2 * HEAD), raw.dtype)] * KV_HEADS,
+        in_specs=[SMEM, IN_HBM, IN_HBM],
+        out_specs=[IN_HBM] * KV_HEADS,
+        scratch_shapes=[
+            pltpu.VMEM((KV_HEADS, 2, LENGTH, HEAD), raw.dtype),
+            pltpu.SemaphoreType.DMA((KV_HEADS, 2)),
+            pltpu.SemaphoreType.DMA((KV_HEADS, 2)),
+        ],
+        compiler_params=pltpu.CompilerParams(vmem_limit_bytes=SOME_ROOM),
+        cost_estimate=pl.CostEstimate(
+            flops=UNITS_FLOPS, bytes_accessed=1024 * 1024, transcendentals=0
+        ),
+    )(me.reshape(1), raw, across)
+
+
+def cache_whole(me, *pieces):
+    def kernel(me_ref, *refs):
+        sources, (whole_ref, held, in_sems, out_sems) = refs[: len(GATHERED)], refs[len(GATHERED) :]
         here = me_ref[0]
         copies = []
-        for side, source in enumerate((near_ref, far_ref)):
-            for j in range(RING):
-                owner = lax.rem(here + RING - j, RING)
-                micro = lax.rem(here // RING + side, 2)
-                head, half = owner // 2, lax.rem(owner, 2)
-                start = pl.multiple_of(half * (LENGTH // 2), LENGTH // 2)
-                later = []
-                for part in range(2):
-                    column = pl.multiple_of(head * HEAD + part * KEY_WIDTH, HEAD)
-                    later.append(
-                        pltpu.make_async_copy(
-                            held.at[side, j, :, pl.ds(part * HEAD, HEAD)],
-                            whole_ref.at[micro, pl.ds(start, LENGTH // 2), pl.ds(column, HEAD)],
-                            out_sems.at[(side * RING + j) * 2 + part],
+        n = 0
+        for source, places in zip(sources, GATHERED):
+            later = []
+            first_slot = n
+            for i, back in enumerate(places):
+                for side in range(2):
+                    owner = lax.rem(here + RING - back, RING)
+                    micro = lax.rem(here // RING + side, 2)
+                    head, half = owner // 2, lax.rem(owner, 2)
+                    start = pl.multiple_of(half * (LENGTH // 2), LENGTH // 2)
+                    for part in range(2):
+                        column = pl.multiple_of(head * HEAD + part * KEY_WIDTH, HEAD)
+                        later.append(
+                            pltpu.make_async_copy(
+                                held.at[n, :, pl.ds(part * HEAD, HEAD)],
+                                whole_ref.at[micro, pl.ds(start, LENGTH // 2), pl.ds(column, HEAD)],
+                                out_sems.at[n, part],
+                            )
                         )
-                    )
-                first = pltpu.make_async_copy(source.at[j], held.at[side, j], in_sems.at[side, j])
-                copies.append((first, later))
+                    n += 1
+            slots = held.at[pl.ds(first_slot, n - first_slot)]
+            copies.append((pltpu.make_async_copy(source, slots, in_sems.at[first_slot]), later))
         run_copies(copies)
 
-    out = jax.ShapeDtypeStruct((MICROS, LENGTH, 2 * KEY_WIDTH), near.dtype)
+    out = jax.ShapeDtypeStruct((MICROS, LENGTH, 2 * KEY_WIDTH), pieces[0].dtype)
     scratch = [
-        pltpu.VMEM((2,) + near.shape, near.dtype),
-        pltpu.SemaphoreType.DMA((2, RING)),
-        pltpu.SemaphoreType.DMA((4 * RING,)),
-    ]
-    return moving_call(kernel, out, scratch, [SMEM, IN_HBM, IN_HBM])(me.reshape(1), near, far)
-
-
-def stack_heads(rows):
-    return jnp.concatenate([rows[:, h * HEAD : (h + 1) * HEAD] for h in range(GROUP)], axis=0)
-
-
-def unstack_heads(rows):
-    return jnp.concatenate([rows[h * BLOCK : (h + 1) * BLOCK] for h in range(GROUP)], axis=1)
+        pltpu.VMEM((SECTIONS, LENGTH // 2, 2 * HEAD), out.dtype),
+        pltpu.SemaphoreType.DMA((SECTIONS,)),
+        pltpu.SemaphoreType.DMA((SECTIONS, 2)),
+    ]
+    in_specs = [SMEM] + [IN_HBM] * len(pieces)
+    return moving_call(kernel, out, scratch, in_specs)(me.reshape(1), *pieces)
 
 
 def three_parts(rows):
@@ -190,8 +204,9 @@
         leaving = []
         for owner in range(SECTIONS):
             if gains is not None:
-                first = owner % RING // 2 * GROUP
-                stacked[owner, STACK:] = three_parts(refs[0][first : first + GROUP])
+                first = owner % RING // 2 * WIDE
+                heads = [refs[0][:, first + h * HEAD : first + (h + 1) * HEAD] for h in range(GROUP)]
+                stacked[owner, STACK:] = three_parts(jnp.concatenate(heads, axis=0))
             arriving[owner].wait()
             for h in range(GROUP):
                 stacked[owner, h * BLOCK : (h + 1) * BLOCK] = held[owner, :, h * HEAD : (h + 1) * HEAD]
@@ -209,8 +224,8 @@
         pltpu.SemaphoreType.DMA((SECTIONS,)),
     ]
     if gains is None:
-        return moving_call(kernel, out, scratch, [IN_HBM])(whole)
-    return moving_call(kernel, out, scratch, [VMEM, IN_HBM])(gains, whole)
+        return moving_call(kernel, out, scratch, [IN_HBM], room=ALL_ROOM)(whole)
+    return moving_call(kernel, out, scratch, [VMEM, IN_HBM], room=ALL_ROOM)(gains, whole)
 
 
 def unpack(came, late, whole=None):
@@ -240,7 +255,9 @@
                 total = jnp.zeros((GROUP, HEAD), jnp.float32)
                 for owner in (2 * head, 2 * head + 1, RING + 2 * head, RING + 2 * head + 1):
                     total += from_parts(held[owner, STACK:])
-                gain_ref[head * GROUP : (head + 1) * GROUP] = total
+                for h in range(GROUP):
+                    first = head * WIDE + h * HEAD
+                    gain_ref[:, first : first + HEAD] = total[h : h + 1]
         for copy in leaving:
             copy.wait()
 
@@ -253,7 +270,7 @@
     ]
     if whole is None:
         return moving_call(kernel, out, scratch, [IN_HBM])(came)
-    outs = [out, jax.ShapeDtypeStruct((HEADS, HEAD), jnp.float32)]
+    outs = [out, jax.ShapeDtypeStruct((1, HEADS * HEAD), jnp.float32)]
     return moving_call(kernel, outs, scratch, [IN_HBM, IN_HBM], {1: 0})(came, whole)
 
 
@@ -362,7 +379,7 @@
         out_shape=[jax.ShapeDtypeStruct(*shape) for shape in shapes],
         in_specs=[VMEM] * (4 + len(before)),
         out_specs=[VMEM] * len(shapes),
-        compiler_params=pltpu.CompilerParams(vmem_limit_bytes=24 * 1024 * 1024),
+        compiler_params=pltpu.CompilerParams(vmem_limit_bytes=ALL_ROOM if not before else 24 * 1024 * 1024),
         cost_estimate=pl.CostEstimate(
             flops=SECTIONS * 10 * columns * seen * HEAD,
             bytes_accessed=6 * 1024 * 1024,
@@ -386,17 +403,17 @@
     me = lax.axis_index("section")
     micro, head, half = me // RING, me % RING // 2, me % 2
 
-    units = cache_units(cache_slots[0])
-    across = moved(units[KV_HEADS:], [(0, RING)])
-    late_packed = pack(saved_inputs[0], True, query_gains.reshape(HEADS, HEAD))
-    late_saved = exchange(after(late_packed, across))
-    four = jnp.where(me < RING, units[:KV_HEADS], across)
+    raw = cache_slots[0]
+    across = moved(raw[1], [(0, RING)])
+    late_saved = exchange(pack(saved_inputs[0], True, query_gains))
+    early_packed = pack(saved_inputs[0], False)
+    four = own_units(me, raw, across)
     came = [moved(four[k], [(0, 2 * k), (RING, RING + 2 * k)]) for k in (2, 1, 3)]
     at_even = jnp.where(me % RING == 0, four[0], came[0] + came[1] + came[2])
+    at_even = after(at_even, early_packed)
     at_odd = moved(at_even, [(i, i + 1) for i in range(0, SECTIONS, 2)])
     kv_unit = jnp.where(half == 0, at_even, at_odd)
-    early_packed = after(pack(saved_inputs[0], False), late_saved, at_odd)
-    early_saved = exchange(early_packed)
+    early_saved = exchange(after(early_packed, late_saved, at_odd))
 
     segments = lax.dynamic_index_in_dim(segment_ids, micro, 0, keepdims=False)
     late_block, early_block = 3 - half, half
@@ -420,17 +437,18 @@
         gain_part = gain_part + swapped(gain_part, bit, "dp")
     early_grads = with_gains(early_grads, gain_part)
 
+    early_home = exchange(after(early_grads, late_home, theirs))
     mine = lax.dynamic_index_in_dim(halves, half, 0, keepdims=False) + theirs
     mine = after(mine.astype(jnp.bfloat16), early_grads)
-    ring = {0: mine}
-    for r in RING_ORDER:
-        ring[r] = turned(mine, r)
-    early_home = exchange(after(early_grads, late_home, *(ring[r] for r in RING_ORDER)))
+    came = [swapped(mine, bit) for bit in (4, 12, 8)]
     whole = unpack(late_home, True)
-    near = jnp.stack([ring[r] for r in range(RING)])
-    cache_grad = cache_whole(me, near, swapped(near, RING))
+    here = jnp.stack([mine, came[2]])
+    both = jnp.stack([mine, came[2], came[0], came[1]])
+    both, here = lax.optimization_barrier((both, here, whole, early_home))[:2]
+    pieces = [both, turned(both, 1), turned(both, -1), turned(here, 2), turned(here, -2)]
+    cache_grad = cache_whole(me, *pieces)
     layer_out, gain_sum = unpack(early_home, False, whole)
-    return (layer_out[None], cache_grad, gain_sum.reshape(1, HEADS * HEAD))
+    return (layer_out[None], cache_grad, gain_sum)
 
 
 def solution(mesh):

time: 206 us -> 197 us (0.956)
  local copies, waits for them, and re-layouts: 12.3 us -> 4.81 us
  starting transfers between devices: 68.3 us -> 62.5 us
  waiting for transfers between devices: 85.8 us -> 91 us
    ppermute x12 -> x9, starting transfers between devices: 33.5 us -> 21.4 us  [moved(): return lax.ppermute(array, 'section', pairs)]
    ppermute x6 -> x8, waiting for transfers between devices: 30.1 us -> 38.9 us  [swapped(): return lax.ppermute(array, axis, [(i, i ^ bit) for i in range(16)])]
    unnamed x30 -> x14, local copies, waits for them, and re-layouts: 7.78 us -> 0.97 us
    ppermute x6 -> x8, starting transfers between devices: 9.1 us -> 14.7 us  [swapped(): return lax.ppermute(array, axis, [(i, i ^ bit) for i in range(16)])]
    ppermute x12 -> x9, waiting for transfers between devices: 32.2 us -> 28.7 us  [moved(): return lax.ppermute(array, 'section', pairs)]
  transfers between devices with their start and end apart: 22 -> 21, of which waited for: 13 -> 15; matrix products, arithmetic and copies ran while one was open for 3% -> 2% of each run, Pallas kernels for 15% -> 18%
where the time goes in v3:
time: 197 us; the launch traced here: 196 us
  waiting for transfers between devices  91 us (46%)
  starting transfers between devices  62.5 us (32%)
  Pallas kernels  36.1 us (18%)
  local copies, waits for them, and re-layouts  4.81 us (2%)
    ppermute x8, waiting for transfers between devices, swapped(): return lax.ppermute(array, axis, [(i, i ^ bit) for i in range(16)])  38.9 us
    ppermute x9, waiting for transfers between devices, moved(): return lax.ppermute(array, 'section', pairs)  28.7 us
    all_to_all x4, starting transfers between devices, exchange(): return lax.all_to_all(array, 'section', 0, 0, tiled=True)  26.4 us
    all_to_all x4, waiting for transfers between devices, exchange(): return lax.all_to_all(array, 'section', 0, 0, tiled=True)  23.4 us
    ppermute x9, starting transfers between devices, moved(): return lax.ppermute(array, 'section', pairs)  21.4 us
    pallas_call x2, Pallas kernels, chain(): pl.pallas_call(kernel, out_shape=[jax.ShapeDtypeStruct(*shape) for shape...  21 us
    ppermute x8, starting transfers between devices, swapped(): return lax.ppermute(array, axis, [(i, i ^ bit) for i in range(16)])  14.7 us
  transfers between devices with their start and end apart: 21, of which 15 were waited for; matrix products, arithmetic and copies ran while one was open for 2% of the time, Pallas kernels for 18%

profile of v3, /device:TPU:8, one launch (start us, length us, event | category | flops | bytes accessed | tf_op | source)
XLA Modules:
  0.0 196.4 jit_solution(18203196251206426539)
XLA Ops:
  0.6 1.1 slice_bitcast_fusion
  1.7 5.0 %collective-permute-start = (bf16[256,1024]{1,0:T(8,128)(2,1)S(1)}, bf16[256,1024]{1,0:T(8,128)(2,1)S(1)}, u32[]{:S(2)}, u32[]{:S(2)}) collective-permute-start(bf16[256,1024]{1,0:T(8,128)(2,1)S(1)} %slice_bitcast_fusion), channel_id=1, source_target_pairs={{0,128},{1,129},{2,130},{3,131},{4,132},{5,133},{6,134},{7,135},{8... | collective-permute-start | bytes 1572872 | tf_op jit(solution)/shard_map/ppermute | solution.py:36
  6.7 3.1 %shard_map.77 = bf16[16,336,128]{2,1,0:T(8,128)(2,1)} custom-call(f32[1,2560]{1,0:T(1,128)} %refs_0_.1, bf16[2,256,2560]{2,1,0:T(8,128)(2,1)} %bitcast.33), custom_call_target="tpu_custom_call" | custom-call | bytes 2752512 | tf_op jit(solution)/shard_map/pallas_call | solution.py:228
  9.8 0.0 copy-start
  9.8 6.9 %all-to-all-start = ((bf16[16,336,128]{2,1,0:T(8,128)(2,1)}), bf16[16,336,128]{2,1,0:T(8,128)(2,1)S(1)}, u32[]{:S(2)}, u32[]{:S(2)}) async-start(bf16[16,336,128]{2,1,0:T(8,128)(2,1)} %shard_map.77), calls=%async_computation | async-start | bytes 2752512 | tf_op jit(solution)/shard_map/all_to_all | solution.py:48
  16.7 2.1 %collective-permute-done.across_ref = bf16[256,1024]{1,0:T(8,128)(2,1)S(1)} collective-permute-done((bf16[256,1024]{1,0:T(8,128)(2,1)S(1)}, bf16[256,1024]{1,0:T(8,128)(2,1)S(1)}, u32[]{:S(2)}, u32[]{:S(2)}) %collective-permute-start) | collective-permute-done | bytes 524320 | tf_op jit(solution)/shard_map/ppermute | solution.py:36
  18.8 0.4 shard_map.78
  19.2 3.9 %collective-permute-start.3 = (bf16[256,256]{1,0:T(8,128)(2,1)S(1)}, bf16[256,256]{1,0:T(8,128)(2,1)S(1)}, u32[]{:S(2)}, u32[]{:S(2)}) collective-permute-start(bf16[256,256]{1,0:T(8,128)(2,1)S(1)} %get-tuple-element.25), channel_id=1, source_target_pairs={{0,96},{128,224},{1,97},{129,225},{2,98},{130,226},{3,99},{131,227... | collective-permute-start | bytes 393224 | tf_op jit(solution)/shard_map/ppermute | solution.py:36
  23.1 2.5 %collective-permute-start.1 = (bf16[256,256]{1,0:T(8,128)(2,1)S(1)}, bf16[256,256]{1,0:T(8,128)(2,1)S(1)}, u32[]{:S(2)}, u32[]{:S(2)}) collective-permute-start(bf16[256,256]{1,0:T(8,128)(2,1)S(1)} %get-tuple-element.23), channel_id=1, source_target_pairs={{0,64},{128,192},{1,65},{129,193},{2,66},{130,194},{3,67},{131,195... | collective-permute-start | bytes 393224 | tf_op jit(solution)/shard_map/ppermute | solution.py:36
  25.6 1.3 collective-permute-start.2
  26.9 2.4 %shard_map.76 = bf16[16,320,128]{2,1,0:T(8,128)(2,1)} custom-call(bf16[2,256,2560]{2,1,0:T(8,128)(2,1)} %bitcast.34), custom_call_target="tpu_custom_call" | custom-call | bytes 2621440 | tf_op jit(solution)/shard_map/pallas_call | solution.py:227
  29.2 19.8 %collective-permute-done.3 = bf16[256,256]{1,0:T(8,128)(2,1)S(1)} collective-permute-done((bf16[256,256]{1,0:T(8,128)(2,1)S(1)}, bf16[256,256]{1,0:T(8,128)(2,1)S(1)}, u32[]{:S(2)}, u32[]{:S(2)}) %collective-permute-start.3) | collective-permute-done | bytes 131104 | tf_op jit(solution)/shard_map/ppermute | solution.py:36
  49.1 1.2 collective-permute-done.1
  50.3 1.7 collective-permute-done.2
  52.0 0.0 copy-start.6
  52.0 1.3 collective-permute-start.4
  53.3 2.5 %collective-permute-done.4 = bf16[256,256]{1,0:T(8,128)(2,1)S(1)} collective-permute-done((bf16[256,256]{1,0:T(8,128)(2,1)S(1)}, bf16[256,256]{1,0:T(8,128)(2,1)S(1)}, u32[]{:S(2)}, u32[]{:S(2)}) %collective-permute-start.4) | collective-permute-done | bytes 131104 | tf_op jit(solution)/shard_map/ppermute | solution.py:36
  55.8 0.0 all-to-all-done.saved_ref
  55.8 10.0 %all-to-all-start.1 = ((bf16[16,320,128]{2,1,0:T(8,128)(2,1)}), bf16[16,320,128]{2,1,0:T(8,128)(2,1)S(1)}, u32[]{:S(2)}, u32[]{:S(2)}) async-start(bf16[16,320,128]{2,1,0:T(8,128)(2,1)} %shard_map.76), calls=%async_computation.1 | async-start | bytes 2621440 | tf_op jit(solution)/shard_map/all_to_all | solution.py:48
  65.9 0.0 copy-done.6
  65.9 0.1 dynamic-slice_bitcast_fusion.3
  66.0 0.1 fusion.2
  66.1 0.0 copy-done.5
  66.2 0.9 copy.10.bias_ref
  67.1 1.6 dynamic-slice_bitcast_fusion.1
  68.6 0.7 broadcast_select_fusion.kv_ref
  69.3 12.6 %shard_map.79 = (bf16[16,320,128]{2,1,0:T(8,128)(2,1)}, f32[256,256]{1,0:T(8,128)}, f32[16,8,128]{2,1,0:T(8,128)}, f32[16,8,128]{2,1,0:T(8,128)}) custom-call(bf16[16,336,128]{2,1,0:T(8,128)(2,1)} %copy-done.5, bf16[256,256]{1,0:T(8,128)(2,1)} %broadcast_select_fusion.kv_ref, f32[256,320]{1,0:T(8,128)} %copy.10.bias_ref, ...), custom_call_target="tpu_custom_call" | custom-call | flops 1677721600 | bytes 6291456 | tf_op jit(solution)/shard_map/pallas_call | solution.py:377
  81.8 15.8 %all-to-all-done.1.saved_ref = bf16[16,320,128]{2,1,0:T(8,128)(2,1)S(1)} async-done(((bf16[16,320,128]{2,1,0:T(8,128)(2,1)}), bf16[16,320,128]{2,1,0:T(8,128)(2,1)S(1)}, u32[]{:S(2)}, u32[]{:S(2)}) %all-to-all-start.1) | async-done | bytes 1310752 | tf_op jit(solution)/shard_map/all_to_all | solution.py:48
  97.6 3.9 %all-to-all-start.2 = ((bf16[16,320,128]{2,1,0:T(8,128)(2,1)}), bf16[16,320,128]{2,1,0:T(8,128)(2,1)S(1)}, u32[]{:S(2)}, u32[]{:S(2)}) async-start(bf16[16,320,128]{2,1,0:T(8,128)(2,1)} %get-tuple-element.33), calls=%async_computation.2 | async-start | bytes 2621440 | tf_op jit(solution)/shard_map/all_to_all | solution.py:48
  101.5 0.1 fusion.4
  101.6 0.1 copy.11.bias_ref
  101.8 0.9 copy-done.2
  102.8 8.5 %shard_map.80 = (bf16[16,336,128]{2,1,0:T(8,128)(2,1)}, f32[256,256]{1,0:T(8,128)S(1)}, f32[16,8,128]{2,1,0:T(8,128)S(1)}) custom-call(bf16[16,320,128]{2,1,0:T(8,128)(2,1)S(1)} %all-to-all-done.1.saved_ref, bf16[256,256]{1,0:T(8,128)(2,1)S(1)} %copy-done.1, f32[128,320]{1,0:T(8,128)S(1)} %copy.11.bias_ref, bf16[64,640]{1,0:T(8,128)(2,1)S(1)} %get-tuple-element.42.top_ref, ...), custom_call_target="tpu_custom_call" | custom-call | flops 838860800 | bytes 6291456 | tf_op jit(solution)/shard_map/pallas_call | solution.py:377
  111.2 0.0 collective-permute-start.5
  111.2 1.3 collective-permute-done.5
  112.5 0.5 collective-permute-start.6
  113.0 3.8 %collective-permute-done.6 = f32[16,8,128]{2,1,0:T(8,128)S(1)} collective-permute-done((f32[16,8,128]{2,1,0:T(8,128)S(1)}, f32[16,8,128]{2,1,0:T(8,128)S(1)}, u32[]{:S(2)}, u32[]{:S(2)}) %collective-permute-start.6) | collective-permute-done | bytes 65568 | tf_op jit(solution)/shard_map/ppermute | solution.py:44
  116.9 2.4 %collective-permute-start.7 = (f32[16,8,128]{2,1,0:T(8,128)S(1)}, f32[16,8,128]{2,1,0:T(8,128)S(1)}, u32[]{:S(2)}, u32[]{:S(2)}) collective-permute-start(f32[16,8,128]{2,1,0:T(8,128)S(1)} %add.92), channel_id=1, source_target_pairs={{0,4},{1,5},{2,6},{3,7},{4,0},{5,1},{6,2},{7,3},{8,12},{9,13},{10,... | collective-permute-start | bytes 196616 | tf_op jit(solution)/shard_map/ppermute | solution.py:44
  119.3 2.0 %collective-permute-start.9 = (f32[128,256]{1,0:T(8,128)S(1)}, f32[128,256]{1,0:T(8,128)S(1)}, u32[]{:S(2)}, u32[]{:S(2)}) collective-permute-start(f32[128,256]{1,0:T(8,128)S(1)} %dynamic-slice_bitcast_fusion), channel_id=1, source_target_pairs={{0,16},{16,0},{32,48},{48,32},{64,80},{80,64},{96,112},{112,96},{1... | collective-permute-start | bytes 393224 | tf_op jit(solution)/shard_map/ppermute | solution.py:44
  121.3 1.5 collective-permute-done.7
  122.7 0.7 collective-permute-start.8
  123.4 4.0 %collective-permute-done.8 = f32[16,8,128]{2,1,0:T(8,128)S(1)} collective-permute-done((f32[16,8,128]{2,1,0:T(8,128)S(1)}, f32[16,8,128]{2,1,0:T(8,128)S(1)}, u32[]{:S(2)}, u32[]{:S(2)}) %collective-permute-start.8) | collective-permute-done | bytes 65568 | tf_op jit(solution)/shard_map/ppermute | solution.py:44
  127.4 0.8 shard_map.81
  128.3 7.6 %all-to-all-done.2.came_ref = bf16[16,320,128]{2,1,0:T(8,128)(2,1)S(1)} async-done(((bf16[16,320,128]{2,1,0:T(8,128)(2,1)}), bf16[16,320,128]{2,1,0:T(8,128)(2,1)S(1)}, u32[]{:S(2)}, u32[]{:S(2)}) %all-to-all-start.2) | async-done | bytes 1310752 | tf_op jit(solution)/shard_map/all_to_all | solution.py:48
  135.9 0.0 collective-permute-done.9
  135.9 5.6 %all-to-all-start.3 = ((bf16[16,336,128]{2,1,0:T(8,128)(2,1)}), bf16[16,336,128]{2,1,0:T(8,128)(2,1)S(1)}, u32[]{:S(2)}, u32[]{:S(2)}) async-start(bf16[16,336,128]{2,1,0:T(8,128)(2,1)} %shard_map.81), calls=%async_computation.3 | async-start | bytes 2752512 | tf_op jit(solution)/shard_map/all_to_all | solution.py:48
  141.5 3.5 %collective-permute-start.10 = (bf16[128,256]{1,0:T(8,128)(2,1)S(1)}, bf16[128,256]{1,0:T(8,128)(2,1)S(1)}, u32[]{:S(2)}, u32[]{:S(2)}) collective-permute-start(bf16[128,256]{1,0:T(8,128)(2,1)S(1)} %fusion), channel_id=1, source_target_pairs={{0,128},{16,144},{32,160},{48,176},{64,192},{80,208},{96,224},{112... | collective-permute-start | bytes 196616 | tf_op jit(solution)/shard_map/ppermute | solution.py:44
  145.0 3.0 %shard_map.82.rest_0_ = bf16[2,256,2560]{2,1,0:T(8,128)(2,1)} custom-call(bf16[16,320,128]{2,1,0:T(8,128)(2,1)S(1)} %all-to-all-done.2.came_ref), custom_call_target="tpu_custom_call" | custom-call | bytes 5242880 | tf_op jit(solution)/shard_map/pallas_call | solution.py:272
  148.0 5.5 %collective-permute-start.12 = (bf16[128,256]{1,0:T(8,128)(2,1)S(1)}, bf16[128,256]{1,0:T(8,128)(2,1)S(1)}, u32[]{:S(2)}, u32[]{:S(2)}) collective-permute-start(bf16[128,256]{1,0:T(8,128)(2,1)S(1)} %fusion), channel_id=1, source_target_pairs={{0,192},{16,208},{32,224},{48,240},{64,128},{80,144},{96,160},{112... | collective-permute-start | bytes 196616 | tf_op jit(solution)/shard_map/ppermute | solution.py:44
  153.5 0.1 collective-permute-start.11
  153.6 0.0 collective-permute-done.10
  153.6 28.1 %collective-permute-done.12 = bf16[128,256]{1,0:T(8,128)(2,1)S(1)} collective-permute-done((bf16[128,256]{1,0:T(8,128)(2,1)S(1)}, bf16[128,256]{1,0:T(8,128)(2,1)S(1)}, u32[]{:S(2)}, u32[]{:S(2)}) %collective-permute-start.12) | collective-permute-done | bytes 65568 | tf_op jit(solution)/shard_map/ppermute | solution.py:44
  181.8 0.2 collective-permute-done.11
  182.0 0.0 all-to-all-done.3.came_ref
  182.0 1.8 collective-permute-start.13
  183.8 1.6 collective-permute-start.14
  185.3 0.0 collective-permute-start.15
  185.3 4.1 %collective-permute-start.16 = (bf16[2,128,256]{2,1,0:T(8,128)(2,1)S(1)}, bf16[2,128,256]{2,1,0:T(8,128)(2,1)S(1)}, u32[]{:S(2)}, u32[]{:S(2)}) collective-permute-start(bf16[2,128,256]{2,1,0:T(8,128)(2,1)S(1)} %pad_maximum_fusion.1), channel_id=1, source_target_pairs={{0,96},{16,112},{32,0},{48,16},{64,32},{80,48},{96,64},{112,80},{1... | collective-permute-start | bytes 393224 | tf_op jit(solution)/shard_map/ppermute | solution.py:36
  189.5 3.7 %shard_map.83 = (bf16[2,256,2560]{2,1,0:T(8,128)(2,1)}, f32[1,2560]{1,0:T(1,128)}) custom-call(bf16[16,336,128]{2,1,0:T(8,128)(2,1)S(1)} %all-to-all-done.3.came_ref, bf16[2,256,2560]{2,1,0:T(8,128)(2,1)} %shard_map.82.rest_0_), custom_call_target="tpu_custom_call", output_to_operand_aliasing={{0}: (1, {})} | custom-call | bytes 5263360 | tf_op jit(solution)/shard_map/pallas_call | solution.py:274
  193.2 0.3 collective-permute-done.15.refs_3_
  193.4 1.2 collective-permute-done.16.refs_4_
  194.6 0.0 collective-permute-done.13.refs_1_
  194.6 0.0 collective-permute-done.14.refs_2_
  194.6 1.8 shard_map.84
  (24 shorter events, 0.2 us)
Async XLA Ops:
  1.7 17.0 %collective-permute-start = (bf16[256,1024]{1,0:T(8,128)(2,1)S(1)}, bf16[256,1024]{1,0:T(8,128)(2,1)S(1)}, u32[]{:S(2)}, u32[]{:S(2)}) collective-permute-start(bf16[256,1024]{1,0:T(8,128)(2,1)S(1)} %slice_bitcast_fusion), channel_id=1, source_target_pairs={{0,128},{1,129},{2,130},{3,131},{4,132},{5,133},{6,134},{7,135},{8... | collective-permute-start | bytes 1572872 | tf_op jit(solution)/shard_map/ppermute | solution.py:36
  9.8 9.0 %copy-start = (bf16[1,2,256,1024]{3,2,1,0:T(8,128)(2,1)S(1)}, bf16[1,2,256,1024]{3,2,1,0:T(8,128)(2,1)}, u32[]{:S(2)}) copy-start(bf16[1,2,256,1024]{3,2,1,0:T(8,128)(2,1)} %param.7) | copy-start | bytes 3145732
  9.8 46.0 %all-to-all-start = ((bf16[16,336,128]{2,1,0:T(8,128)(2,1)}), bf16[16,336,128]{2,1,0:T(8,128)(2,1)S(1)}, u32[]{:S(2)}, u32[]{:S(2)}) async-start(bf16[16,336,128]{2,1,0:T(8,128)(2,1)} %shard_map.77), calls=%async_computation | async-start | bytes 2752512 | tf_op jit(solution)/shard_map/all_to_all | solution.py:48
  19.2 29.9 %collective-permute-start.3 = (bf16[256,256]{1,0:T(8,128)(2,1)S(1)}, bf16[256,256]{1,0:T(8,128)(2,1)S(1)}, u32[]{:S(2)}, u32[]{:S(2)}) collective-permute-start(bf16[256,256]{1,0:T(8,128)(2,1)S(1)} %get-tuple-element.25), channel_id=1, source_target_pairs={{0,96},{128,224},{1,97},{129,225},{2,98},{130,226},{3,99},{131,227... | collective-permute-start | bytes 393224 | tf_op jit(solution)/shard_map/ppermute | solution.py:36
  23.1 27.2 %collective-permute-start.1 = (bf16[256,256]{1,0:T(8,128)(2,1)S(1)}, bf16[256,256]{1,0:T(8,128)(2,1)S(1)}, u32[]{:S(2)}, u32[]{:S(2)}) collective-permute-start(bf16[256,256]{1,0:T(8,128)(2,1)S(1)} %get-tuple-element.23), channel_id=1, source_target_pairs={{0,64},{128,192},{1,65},{129,193},{2,66},{130,194},{3,67},{131,195... | collective-permute-start | bytes 393224 | tf_op jit(solution)/shard_map/ppermute | solution.py:36
  25.6 26.4 %collective-permute-start.2 = (bf16[256,256]{1,0:T(8,128)(2,1)S(1)}, bf16[256,256]{1,0:T(8,128)(2,1)S(1)}, u32[]{:S(2)}, u32[]{:S(2)}) collective-permute-start(bf16[256,256]{1,0:T(8,128)(2,1)S(1)} %get-tuple-element.24), channel_id=1, source_target_pairs={{0,32},{128,160},{1,33},{129,161},{2,34},{130,162},{3,35},{131,163... | collective-permute-start | bytes 393224 | tf_op jit(solution)/shard_map/ppermute | solution.py:36
  52.0 14.0 %copy-start.6 = (s32[2,256]{1,0:T(2,128)S(1)}, s32[2,256]{1,0:T(2,128)}, u32[]{:S(2)}) copy-start(s32[2,256]{1,0:T(2,128)} %param.8) | copy-start | bytes 6148
  52.0 3.8 %collective-permute-start.4 = (bf16[256,256]{1,0:T(8,128)(2,1)S(1)}, bf16[256,256]{1,0:T(8,128)(2,1)S(1)}, u32[]{:S(2)}, u32[]{:S(2)}) collective-permute-start(bf16[256,256]{1,0:T(8,128)(2,1)S(1)} %add_select_fusion), channel_id=1, source_target_pairs={{0,16},{32,48},{64,80},{96,112},{128,144},{160,176},{192,208},{224... | collective-permute-start | bytes 393224 | tf_op jit(solution)/shard_map/ppermute | solution.py:36
  55.8 10.3 %copy-start.5 = (bf16[16,336,128]{2,1,0:T(8,128)(2,1)}, bf16[16,336,128]{2,1,0:T(8,128)(2,1)S(1)}, u32[]{:S(2)}) copy-start(bf16[16,336,128]{2,1,0:T(8,128)(2,1)S(1)} %all-to-all-done.saved_ref) | copy-start | bytes 4128772
  55.8 41.8 %all-to-all-start.1 = ((bf16[16,320,128]{2,1,0:T(8,128)(2,1)}), bf16[16,320,128]{2,1,0:T(8,128)(2,1)S(1)}, u32[]{:S(2)}, u32[]{:S(2)}) async-start(bf16[16,320,128]{2,1,0:T(8,128)(2,1)} %shard_map.76), calls=%async_computation.1 | async-start | bytes 2621440 | tf_op jit(solution)/shard_map/all_to_all | solution.py:48
  97.6 4.2 %copy-start.1 = (bf16[256,256]{1,0:T(8,128)(2,1)S(1)}, bf16[256,256]{1,0:T(8,128)(2,1)}, u32[]{:S(2)}) copy-start(bf16[256,256]{1,0:T(8,128)(2,1)} %broadcast_select_fusion.kv_ref) | copy-start | bytes 393220
  97.6 4.2 %copy-start.3 = (f32[16,8,128]{2,1,0:T(8,128)S(1)}, f32[16,8,128]{2,1,0:T(8,128)}, u32[]{:S(2)}) copy-start(f32[16,8,128]{2,1,0:T(8,128)} %get-tuple-element.29.gain_ref) | copy-start | bytes 196612
  97.6 4.2 %copy-start.4 = (f32[16,8,128]{2,1,0:T(8,128)S(1)}, f32[16,8,128]{2,1,0:T(8,128)}, u32[]{:S(2)}) copy-start(f32[16,8,128]{2,1,0:T(8,128)} %get-tuple-element.30.part_before) | copy-start | bytes 196612
  97.6 38.3 %all-to-all-start.2 = ((bf16[16,320,128]{2,1,0:T(8,128)(2,1)}), bf16[16,320,128]{2,1,0:T(8,128)(2,1)S(1)}, u32[]{:S(2)}, u32[]{:S(2)}) async-start(bf16[16,320,128]{2,1,0:T(8,128)(2,1)} %get-tuple-element.33), calls=%async_computation.2 | async-start | bytes 2621440 | tf_op jit(solution)/shard_map/all_to_all | solution.py:48
  101.8 1.0 copy-start.2
  111.2 1.3 collective-permute-start.5
  112.5 4.4 %collective-permute-start.6 = (f32[16,8,128]{2,1,0:T(8,128)S(1)}, f32[16,8,128]{2,1,0:T(8,128)S(1)}, u32[]{:S(2)}, u32[]{:S(2)}) collective-permute-start(f32[16,8,128]{2,1,0:T(8,128)S(1)} %add.91), channel_id=1, source_target_pairs={{0,2},{1,3},{2,0},{3,1},{4,6},{5,7},{6,4},{7,5},{8,10},{9,11},{10,... | collective-permute-start | bytes 196616 | tf_op jit(solution)/shard_map/ppermute | solution.py:44
  116.9 5.9 %collective-permute-start.7 = (f32[16,8,128]{2,1,0:T(8,128)S(1)}, f32[16,8,128]{2,1,0:T(8,128)S(1)}, u32[]{:S(2)}, u32[]{:S(2)}) collective-permute-start(f32[16,8,128]{2,1,0:T(8,128)S(1)} %add.92), channel_id=1, source_target_pairs={{0,4},{1,5},{2,6},{3,7},{4,0},{5,1},{6,2},{7,3},{8,12},{9,13},{10,... | collective-permute-start | bytes 196616 | tf_op jit(solution)/shard_map/ppermute | solution.py:44
  119.3 16.6 %collective-permute-start.9 = (f32[128,256]{1,0:T(8,128)S(1)}, f32[128,256]{1,0:T(8,128)S(1)}, u32[]{:S(2)}, u32[]{:S(2)}) collective-permute-start(f32[128,256]{1,0:T(8,128)S(1)} %dynamic-slice_bitcast_fusion), channel_id=1, source_target_pairs={{0,16},{16,0},{32,48},{48,32},{64,80},{80,64},{96,112},{112,96},{1... | collective-permute-start | bytes 393224 | tf_op jit(solution)/shard_map/ppermute | solution.py:44
  122.7 4.7 %collective-permute-start.8 = (f32[16,8,128]{2,1,0:T(8,128)S(1)}, f32[16,8,128]{2,1,0:T(8,128)S(1)}, u32[]{:S(2)}, u32[]{:S(2)}) collective-permute-start(f32[16,8,128]{2,1,0:T(8,128)S(1)} %add.93), channel_id=1, source_target_pairs={{0,8},{1,9},{2,10},{3,11},{4,12},{5,13},{6,14},{7,15},{8,0},{9,1},... | collective-permute-start | bytes 196616 | tf_op jit(solution)/shard_map/ppermute | solution.py:44
  135.9 46.1 %all-to-all-start.3 = ((bf16[16,336,128]{2,1,0:T(8,128)(2,1)}), bf16[16,336,128]{2,1,0:T(8,128)(2,1)S(1)}, u32[]{:S(2)}, u32[]{:S(2)}) async-start(bf16[16,336,128]{2,1,0:T(8,128)(2,1)} %shard_map.81), calls=%async_computation.3 | async-start | bytes 2752512 | tf_op jit(solution)/shard_map/all_to_all | solution.py:48
  141.5 12.1 %collective-permute-start.10 = (bf16[128,256]{1,0:T(8,128)(2,1)S(1)}, bf16[128,256]{1,0:T(8,128)(2,1)S(1)}, u32[]{:S(2)}, u32[]{:S(2)}) collective-permute-start(bf16[128,256]{1,0:T(8,128)(2,1)S(1)} %fusion), channel_id=1, source_target_pairs={{0,128},{16,144},{32,160},{48,176},{64,192},{80,208},{96,224},{112... | collective-permute-start | bytes 196616 | tf_op jit(solution)/shard_map/ppermute | solution.py:44
  148.0 33.7 %collective-permute-start.12 = (bf16[128,256]{1,0:T(8,128)(2,1)S(1)}, bf16[128,256]{1,0:T(8,128)(2,1)S(1)}, u32[]{:S(2)}, u32[]{:S(2)}) collective-permute-start(bf16[128,256]{1,0:T(8,128)(2,1)S(1)} %fusion), channel_id=1, source_target_pairs={{0,192},{16,208},{32,224},{48,240},{64,128},{80,144},{96,160},{112... | collective-permute-start | bytes 196616 | tf_op jit(solution)/shard_map/ppermute | solution.py:44
  153.5 28.5 %collective-permute-start.11 = (bf16[128,256]{1,0:T(8,128)(2,1)S(1)}, bf16[128,256]{1,0:T(8,128)(2,1)S(1)}, u32[]{:S(2)}, u32[]{:S(2)}) collective-permute-start(bf16[128,256]{1,0:T(8,128)(2,1)S(1)} %fusion), channel_id=1, source_target_pairs={{0,64},{16,80},{32,96},{48,112},{64,0},{80,16},{96,32},{112,48},{1... | collective-permute-start | bytes 196616 | tf_op jit(solution)/shard_map/ppermute | solution.py:44
  182.0 12.6 %collective-permute-start.13 = (bf16[4,128,256]{2,1,0:T(8,128)(2,1)S(1)}, bf16[4,128,256]{2,1,0:T(8,128)(2,1)S(1)}, u32[]{:S(2)}, u32[]{:S(2)}) collective-permute-start(bf16[4,128,256]{2,1,0:T(8,128)(2,1)S(1)} %pad_maximum_fusion.refs_0_), channel_id=1, source_target_pairs={{0,16},{16,32},{32,48},{48,64},{64,80},{80,96},{96,112},{112,0},{1... | collective-permute-start | bytes 786440 | tf_op jit(solution)/shard_map/ppermute | solution.py:36
  183.8 10.9 %collective-permute-start.14 = (bf16[4,128,256]{2,1,0:T(8,128)(2,1)S(1)}, bf16[4,128,256]{2,1,0:T(8,128)(2,1)S(1)}, u32[]{:S(2)}, u32[]{:S(2)}) collective-permute-start(bf16[4,128,256]{2,1,0:T(8,128)(2,1)S(1)} %pad_maximum_fusion.refs_0_), channel_id=1, source_target_pairs={{0,112},{16,0},{32,16},{48,32},{64,48},{80,64},{96,80},{112,96},{1... | collective-permute-start | bytes 786440 | tf_op jit(solution)/shard_map/ppermute | solution.py:36
  185.3 8.1 %collective-permute-start.15 = (bf16[2,128,256]{2,1,0:T(8,128)(2,1)S(1)}, bf16[2,128,256]{2,1,0:T(8,128)(2,1)S(1)}, u32[]{:S(2)}, u32[]{:S(2)}) collective-permute-start(bf16[2,128,256]{2,1,0:T(8,128)(2,1)S(1)} %pad_maximum_fusion.1), channel_id=1, source_target_pairs={{0,32},{16,48},{32,64},{48,80},{64,96},{80,112},{96,0},{112,16},{1... | collective-permute-start | bytes 393224 | tf_op jit(solution)/shard_map/ppermute | solution.py:36
  185.3 9.3 %collective-permute-start.16 = (bf16[2,128,256]{2,1,0:T(8,128)(2,1)S(1)}, bf16[2,128,256]{2,1,0:T(8,128)(2,1)S(1)}, u32[]{:S(2)}, u32[]{:S(2)}) collective-permute-start(bf16[2,128,256]{2,1,0:T(8,128)(2,1)S(1)} %pad_maximum_fusion.1), channel_id=1, source_target_pairs={{0,96},{16,112},{32,0},{48,16},{64,32},{80,48},{96,64},{112,80},{1... | collective-permute-start | bytes 393224 | tf_op jit(solution)/shard_map/ppermute | solution.py:36

commit v4 on v3

--- a/solution.py
+++ b/solution.py
@@ -126,6 +126,22 @@
             flops=UNITS_FLOPS, bytes_accessed=1024 * 1024, transcendentals=0
         ),
     )(me.reshape(1), raw, across)
+
+
+def pick(me, at_even, at_odd):
+    def kernel(me_ref, even_ref, odd_ref, out_ref):
+        out_ref[...] = jnp.where(lax.rem(me_ref[0], 2) == 0, even_ref[...], odd_ref[...])
+
+    return pl.pallas_call(
+        kernel,
+        out_shape=jax.ShapeDtypeStruct(at_even.shape, at_even.dtype),
+        in_specs=[SMEM, VMEM, VMEM],
+        out_specs=VMEM,
+        compiler_params=pltpu.CompilerParams(vmem_limit_bytes=SOME_ROOM),
+        cost_estimate=pl.CostEstimate(
+            flops=UNITS_FLOPS, bytes_accessed=1024 * 1024, transcendentals=0
+        ),
+    )(me.reshape(1), at_even, at_odd)
 
 
 def cache_whole(me, *pieces):
@@ -379,7 +395,7 @@
         out_shape=[jax.ShapeDtypeStruct(*shape) for shape in shapes],
         in_specs=[VMEM] * (4 + len(before)),
         out_specs=[VMEM] * len(shapes),
-        compiler_params=pltpu.CompilerParams(vmem_limit_bytes=ALL_ROOM if not before else 24 * 1024 * 1024),
+        compiler_params=pltpu.CompilerParams(vmem_limit_bytes=24 * 1024 * 1024),
         cost_estimate=pl.CostEstimate(
             flops=SECTIONS * 10 * columns * seen * HEAD,
             bytes_accessed=6 * 1024 * 1024,
@@ -389,47 +405,50 @@
 
 
 def bias_of(segments, block, keys_seen):
-    rows = lax.dynamic_slice(segments, (block * BLOCK,), (BLOCK,))
+    rows = jnp.tile(lax.dynamic_slice(segments, (block * BLOCK,), (BLOCK,)), GROUP)
+    query_pos = block * BLOCK + jnp.tile(jnp.arange(BLOCK), GROUP)
     key_pos = jnp.arange(keys_seen)
-    query_pos = block * BLOCK + jnp.arange(BLOCK)
     allowed = (key_pos[:, None] <= query_pos[None, :]) & (
         segments[:keys_seen, None] == rows[None, :]
     )
-    bias = jnp.where(allowed, 0.0, MASKED).astype(jnp.float32)
-    return jnp.tile(bias, (1, GROUP))
+    return jnp.where(allowed, 0.0, MASKED).astype(jnp.float32)
 
 
 def on_device(saved_inputs, query_gains, cache_slots, segment_ids, output_grad):
     me = lax.axis_index("section")
     micro, head, half = me // RING, me % RING // 2, me % 2
 
+    segments = lax.dynamic_index_in_dim(segment_ids, micro, 0, keepdims=False)
+    late_block, early_block = 3 - half, half
+
+    def top_of(block):
+        start = (micro, block * BLOCK, head * WIDE)
+        return lax.dynamic_slice(output_grad, start, (1, BLOCK, WIDE))[0]
+
+    late_bias = bias_of(segments, late_block, LENGTH)
+    early_bias = bias_of(segments, early_block, LENGTH // 2)
+    late_top, early_top = top_of(late_block), top_of(early_block)
+
     raw = cache_slots[0]
     across = moved(raw[1], [(0, RING)])
     late_saved = exchange(pack(saved_inputs[0], True, query_gains))
-    early_packed = pack(saved_inputs[0], False)
-    four = own_units(me, raw, across)
+    ready = after(saved_inputs[0], late_bias, early_bias, late_top, early_top)
+    early_packed = pack(ready, False)
+    four = own_units(me, raw, after(across, early_packed))
     came = [moved(four[k], [(0, 2 * k), (RING, RING + 2 * k)]) for k in (2, 1, 3)]
     at_even = jnp.where(me % RING == 0, four[0], came[0] + came[1] + came[2])
     at_even = after(at_even, early_packed)
     at_odd = moved(at_even, [(i, i + 1) for i in range(0, SECTIONS, 2)])
-    kv_unit = jnp.where(half == 0, at_even, at_odd)
-    early_saved = exchange(after(early_packed, late_saved, at_odd))
-
-    segments = lax.dynamic_index_in_dim(segment_ids, micro, 0, keepdims=False)
-    late_block, early_block = 3 - half, half
-
-    def top_of(block):
-        start = (micro, block * BLOCK, head * WIDE)
-        return lax.dynamic_slice(output_grad, start, (1, BLOCK, WIDE))[0]
+    kv_unit = pick(me, at_even, at_odd)
+    early_saved = exchange(after(early_packed, late_saved, at_even))
 
     late_grads, cache_part, gains, gain_part = chain(
-        late_kernel, late_saved, kv_unit, bias_of(segments, late_block, LENGTH),
-        top_of(late_block), STACK,
+        late_kernel, late_saved, kv_unit, late_bias, late_top, STACK,
     )
     late_home = exchange(late_grads)
     early_grads, cache_part, gain_part = chain(
-        early_kernel, early_saved, kv_unit, bias_of(segments, early_block, LENGTH // 2),
-        top_of(early_block), STACK + TAIL, cache_part, gains, gain_part,
+        early_kernel, early_saved, kv_unit, early_bias, early_top, STACK + TAIL,
+        cache_part, gains, gain_part,
     )
     halves = cache_part.reshape(2, LENGTH // 2, 2 * HEAD)
     theirs = swapped(lax.dynamic_index_in_dim(halves, 1 - half, 0, keepdims=False), 1)

time: 197 us -> 195 us (0.990)
  waiting for transfers between devices: 91 us -> 86.1 us
  starting transfers between devices: 62.5 us -> 64.5 us
    ppermute x9, waiting for transfers between devices: 28.7 us -> 21.2 us  [moved(): return lax.ppermute(array, 'section', pairs)]
    all_to_all x4, starting transfers between devices: 26.4 us -> 30.4 us  [exchange(): return lax.all_to_all(array, 'section', 0, 0, tiled=True)]
    all_to_all x4, waiting for transfers between devices: 23.4 us -> 26 us  [exchange(): return lax.all_to_all(array, 'section', 0, 0, tiled=True)]
    unnamed x14 -> x18, local copies, waits for them, and re-layouts: 0.97 us -> 2.94 us
  transfers between devices with their start and end apart: 21 -> 21, of which waited for: 15 -> 14; matrix products, arithmetic and copies ran while one was open for 2% -> 2% of each run, Pallas kernels for 18% -> 16%
where the time goes in v4:
time: 195 us; the launch traced here: 194 us
  waiting for transfers between devices  86.1 us (44%)
  starting transfers between devices  64.5 us (33%)
  Pallas kernels  36.1 us (19%)
  local copies, waits for them, and re-layouts  5.77 us (3%)
    ppermute x8, waiting for transfers between devices, swapped(): return lax.ppermute(array, axis, [(i, i ^ bit) for i in range(16)])  38.9 us
    all_to_all x4, starting transfers between devices, exchange(): return lax.all_to_all(array, 'section', 0, 0, tiled=True)  30.4 us
    all_to_all x4, waiting for transfers between devices, exchange(): return lax.all_to_all(array, 'section', 0, 0, tiled=True)  26 us
    ppermute x9, waiting for transfers between devices, moved(): return lax.ppermute(array, 'section', pairs)  21.2 us
    ppermute x9, starting transfers between devices, moved(): return lax.ppermute(array, 'section', pairs)  19.4 us
    pallas_call x2, Pallas kernels, chain(): pl.pallas_call(kernel, out_shape=[jax.ShapeDtypeStruct(*shape) for shape...  19.4 us
    ppermute x8, starting transfers between devices, swapped(): return lax.ppermute(array, axis, [(i, i ^ bit) for i in range(16)])  14.7 us
  transfers between devices with their start and end apart: 21, of which 14 were waited for; matrix products, arithmetic and copies ran while one was open for 2% of the time, Pallas kernels for 16%

profile of v4, /device:TPU:8, one launch (start us, length us, event | category | flops | bytes accessed | tf_op | source)
XLA Modules:
  0.0 193.8 jit_solution(14032411377775675022)
XLA Ops:
  0.6 3.1 %shard_map.77 = bf16[16,336,128]{2,1,0:T(8,128)(2,1)} custom-call(f32[1,2560]{1,0:T(1,128)} %refs_0_.1, bf16[2,256,2560]{2,1,0:T(8,128)(2,1)} %bitcast.31), custom_call_target="tpu_custom_call" | custom-call | bytes 2752512 | tf_op jit(solution)/shard_map/pallas_call | solution.py:244
  3.7 0.0 copy-start
  3.7 0.0 copy-start.8
  3.7 11.2 %all-to-all-start = ((bf16[16,336,128]{2,1,0:T(8,128)(2,1)}), bf16[16,336,128]{2,1,0:T(8,128)(2,1)S(1)}, u32[]{:S(2)}, u32[]{:S(2)}) async-start(bf16[16,336,128]{2,1,0:T(8,128)(2,1)} %shard_map.77), calls=%async_computation | async-start | bytes 2752512 | tf_op jit(solution)/shard_map/all_to_all | solution.py:48
  14.9 0.8 slice_bitcast_fusion
  15.8 6.1 %collective-permute-start = (bf16[256,1024]{1,0:T(8,128)(2,1)}, bf16[256,1024]{1,0:T(8,128)(2,1)}, u32[]{:S(2)}, u32[]{:S(2)}) collective-permute-start(bf16[256,1024]{1,0:T(8,128)(2,1)} %slice_bitcast_fusion), channel_id=1, source_target_pairs={{0,128},{1,129},{2,130},{3,131},{4,132},{5,133},{6,134},{7,135},{8... | collective-permute-start | bytes 1572872 | tf_op jit(solution)/shard_map/ppermute | solution.py:36
  21.9 0.1 dynamic-slice_bitcast_fusion.3
  22.0 0.1 eq.43
  22.1 0.1 add.88
  22.2 0.1 eq.48
  22.2 0.1 add.93
  22.3 1.6 dynamic-slice_bitcast_fusion.1
  23.9 0.1 fusion.3.bias_ref
  24.0 0.1 fusion.1.bias_ref
  24.1 2.4 %shard_map.76 = bf16[16,320,128]{2,1,0:T(8,128)(2,1)} custom-call(bf16[2,256,2560]{2,1,0:T(8,128)(2,1)} %bitcast.32), custom_call_target="tpu_custom_call" | custom-call | bytes 2621440 | tf_op jit(solution)/shard_map/pallas_call | solution.py:243
  26.5 15.0 %collective-permute-done.across_ref = bf16[256,1024]{1,0:T(8,128)(2,1)} collective-permute-done((bf16[256,1024]{1,0:T(8,128)(2,1)}, bf16[256,1024]{1,0:T(8,128)(2,1)}, u32[]{:S(2)}, u32[]{:S(2)}) %collective-permute-start) | collective-permute-done | bytes 524320 | tf_op jit(solution)/shard_map/ppermute | solution.py:36
  41.5 1.0 shard_map.78
  42.5 1.3 collective-permute-start.3
  43.8 1.3 collective-permute-start.1
  45.1 1.3 collective-permute-start.2
  46.4 0.9 collective-permute-done.3
  47.4 2.0 %collective-permute-done.1 = bf16[256,256]{1,0:T(8,128)(2,1)S(1)} collective-permute-done((bf16[256,256]{1,0:T(8,128)(2,1)S(1)}, bf16[256,256]{1,0:T(8,128)(2,1)S(1)}, u32[]{:S(2)}, u32[]{:S(2)}) %collective-permute-start.1) | collective-permute-done | bytes 131104 | tf_op jit(solution)/shard_map/ppermute | solution.py:36
  49.4 1.8 collective-permute-done.2
  51.2 2.0 %collective-permute-start.4 = (bf16[256,256]{1,0:T(8,128)(2,1)S(1)}, bf16[256,256]{1,0:T(8,128)(2,1)}, u32[]{:S(2)}, u32[]{:S(2)}) collective-permute-start(bf16[256,256]{1,0:T(8,128)(2,1)S(1)} %add_select_fusion.even_ref), channel_id=1, source_target_pairs={{0,16},{32,48},{64,80},{96,112},{128,144},{160,176},{192,208},{224... | collective-permute-start | bytes 393224 | tf_op jit(solution)/shard_map/ppermute | solution.py:36
  53.1 0.0 all-to-all-done.saved_ref
  53.1 9.7 %all-to-all-start.1 = ((bf16[16,320,128]{2,1,0:T(8,128)(2,1)}), bf16[16,320,128]{2,1,0:T(8,128)(2,1)S(1)}, u32[]{:S(2)}, u32[]{:S(2)}) async-start(bf16[16,320,128]{2,1,0:T(8,128)(2,1)} %shard_map.76), calls=%async_computation.1 | async-start | bytes 2621440 | tf_op jit(solution)/shard_map/all_to_all | solution.py:48
  62.9 0.0 collective-permute-done.4.odd_ref
  62.9 1.0 shard_map.79.kv_ref
  63.9 10.9 %shard_map.80 = (bf16[16,320,128]{2,1,0:T(8,128)(2,1)}, f32[256,256]{1,0:T(8,128)S(1)}, f32[16,8,128]{2,1,0:T(8,128)S(1)}, f32[16,8,128]{2,1,0:T(8,128)S(1)}) custom-call(bf16[16,336,128]{2,1,0:T(8,128)(2,1)S(1)} %all-to-all-done.saved_ref, bf16[256,256]{1,0:T(8,128)(2,1)S(1)} %shard_map.79.kv_ref, f32[256,320]{1,0:T(8,128)S(1)} %fusion.1.bias_ref, ...), custom_call_target="tpu_custom_call" | custom-call | flops 1677721600 | bytes 6291456 | tf_op jit(solution)/shard_map/pallas_call | solution.py:393
  74.8 0.7 copy-done.2
  75.5 0.7 copy-done.4
  76.1 0.6 copy-done.6
  76.7 18.2 %all-to-all-done.1.saved_ref = bf16[16,320,128]{2,1,0:T(8,128)(2,1)S(1)} async-done(((bf16[16,320,128]{2,1,0:T(8,128)(2,1)}), bf16[16,320,128]{2,1,0:T(8,128)(2,1)S(1)}, u32[]{:S(2)}, u32[]{:S(2)}) %all-to-all-start.1) | async-done | bytes 1310752 | tf_op jit(solution)/shard_map/all_to_all | solution.py:48
  94.9 3.9 %all-to-all-start.2 = ((bf16[16,320,128]{2,1,0:T(8,128)(2,1)}), bf16[16,320,128]{2,1,0:T(8,128)(2,1)S(1)}, u32[]{:S(2)}, u32[]{:S(2)}) async-start(bf16[16,320,128]{2,1,0:T(8,128)(2,1)} %get-tuple-element.37), calls=%async_computation.2 | async-start | bytes 2621440 | tf_op jit(solution)/shard_map/all_to_all | solution.py:48
  98.8 0.0 copy-start.3
  98.8 0.9 copy-done.3
  99.8 8.5 %shard_map.81 = (bf16[16,336,128]{2,1,0:T(8,128)(2,1)}, f32[256,256]{1,0:T(8,128)S(1)}, f32[16,8,128]{2,1,0:T(8,128)S(1)}) custom-call(bf16[16,320,128]{2,1,0:T(8,128)(2,1)S(1)} %all-to-all-done.1.saved_ref, bf16[256,256]{1,0:T(8,128)(2,1)S(1)} %copy-done.5, f32[128,320]{1,0:T(8,128)S(1)} %fusion.3.bias_ref, bf16[64,640]{1,0:T(8,128)(2,1)S(1)} %get-tuple-element.45.top_ref, ...), custom_call_target="tpu_custom_call" | custom-call | flops 838860800 | bytes 6291456 | tf_op jit(solution)/shard_map/pallas_call | solution.py:393
  108.2 1.3 collective-permute-done.5
  109.5 0.5 collective-permute-start.6
  110.1 3.8 %collective-permute-done.6 = f32[16,8,128]{2,1,0:T(8,128)S(1)} collective-permute-done((f32[16,8,128]{2,1,0:T(8,128)S(1)}, f32[16,8,128]{2,1,0:T(8,128)S(1)}, u32[]{:S(2)}, u32[]{:S(2)}) %collective-permute-start.6) | collective-permute-done | bytes 65568 | tf_op jit(solution)/shard_map/ppermute | solution.py:44
  113.9 2.4 %collective-permute-start.7 = (f32[16,8,128]{2,1,0:T(8,128)S(1)}, f32[16,8,128]{2,1,0:T(8,128)S(1)}, u32[]{:S(2)}, u32[]{:S(2)}) collective-permute-start(f32[16,8,128]{2,1,0:T(8,128)S(1)} %add.100), channel_id=1, source_target_pairs={{0,4},{1,5},{2,6},{3,7},{4,0},{5,1},{6,2},{7,3},{8,12},{9,13},{10,... | collective-permute-start | bytes 196616 | tf_op jit(solution)/shard_map/ppermute | solution.py:44
  116.3 2.0 %collective-permute-start.9 = (f32[128,256]{1,0:T(8,128)S(1)}, f32[128,256]{1,0:T(8,128)S(1)}, u32[]{:S(2)}, u32[]{:S(2)}) collective-permute-start(f32[128,256]{1,0:T(8,128)S(1)} %dynamic-slice_bitcast_fusion), channel_id=1, source_target_pairs={{0,16},{16,0},{32,48},{48,32},{64,80},{80,64},{96,112},{112,96},{1... | collective-permute-start | bytes 393224 | tf_op jit(solution)/shard_map/ppermute | solution.py:44
  118.3 1.5 collective-permute-done.7
  119.8 0.7 collective-permute-start.8
  120.4 4.1 %collective-permute-done.8 = f32[16,8,128]{2,1,0:T(8,128)S(1)} collective-permute-done((f32[16,8,128]{2,1,0:T(8,128)S(1)}, f32[16,8,128]{2,1,0:T(8,128)S(1)}, u32[]{:S(2)}, u32[]{:S(2)}) %collective-permute-start.8) | collective-permute-done | bytes 65568 | tf_op jit(solution)/shard_map/ppermute | solution.py:44
  124.5 0.8 shard_map.82
  125.3 7.9 %all-to-all-done.2.came_ref = bf16[16,320,128]{2,1,0:T(8,128)(2,1)S(1)} async-done(((bf16[16,320,128]{2,1,0:T(8,128)(2,1)}), bf16[16,320,128]{2,1,0:T(8,128)(2,1)S(1)}, u32[]{:S(2)}, u32[]{:S(2)}) %all-to-all-start.2) | async-done | bytes 1310752 | tf_op jit(solution)/shard_map/all_to_all | solution.py:48
  133.2 0.0 collective-permute-done.9
  133.2 5.6 %all-to-all-start.3 = ((bf16[16,336,128]{2,1,0:T(8,128)(2,1)}), bf16[16,336,128]{2,1,0:T(8,128)(2,1)S(1)}, u32[]{:S(2)}, u32[]{:S(2)}) async-start(bf16[16,336,128]{2,1,0:T(8,128)(2,1)} %shard_map.82), calls=%async_computation.3 | async-start | bytes 2752512 | tf_op jit(solution)/shard_map/all_to_all | solution.py:48
  138.9 3.5 %collective-permute-start.10 = (bf16[128,256]{1,0:T(8,128)(2,1)S(1)}, bf16[128,256]{1,0:T(8,128)(2,1)S(1)}, u32[]{:S(2)}, u32[]{:S(2)}) collective-permute-start(bf16[128,256]{1,0:T(8,128)(2,1)S(1)} %fusion.4), channel_id=1, source_target_pairs={{0,128},{16,144},{32,160},{48,176},{64,192},{80,208},{96,224},{112... | collective-permute-start | bytes 196616 | tf_op jit(solution)/shard_map/ppermute | solution.py:44
  142.4 3.0 %shard_map.83.rest_0_ = bf16[2,256,2560]{2,1,0:T(8,128)(2,1)} custom-call(bf16[16,320,128]{2,1,0:T(8,128)(2,1)S(1)} %all-to-all-done.2.came_ref), custom_call_target="tpu_custom_call" | custom-call | bytes 5242880 | tf_op jit(solution)/shard_map/pallas_call | solution.py:288
  145.4 5.5 %collective-permute-start.12 = (bf16[128,256]{1,0:T(8,128)(2,1)S(1)}, bf16[128,256]{1,0:T(8,128)(2,1)S(1)}, u32[]{:S(2)}, u32[]{:S(2)}) collective-permute-start(bf16[128,256]{1,0:T(8,128)(2,1)S(1)} %fusion.4), channel_id=1, source_target_pairs={{0,192},{16,208},{32,224},{48,240},{64,128},{80,144},{96,160},{112... | collective-permute-start | bytes 196616 | tf_op jit(solution)/shard_map/ppermute | solution.py:44
  150.9 0.1 collective-permute-start.11
  151.0 28.1 %collective-permute-done.12 = bf16[128,256]{1,0:T(8,128)(2,1)S(1)} collective-permute-done((bf16[128,256]{1,0:T(8,128)(2,1)S(1)}, bf16[128,256]{1,0:T(8,128)(2,1)S(1)}, u32[]{:S(2)}, u32[]{:S(2)}) %collective-permute-start.12) | collective-permute-done | bytes 65568 | tf_op jit(solution)/shard_map/ppermute | solution.py:44
  179.1 0.2 collective-permute-done.11
  179.4 0.0 all-to-all-done.3.came_ref
  179.4 1.8 collective-permute-start.13
  181.1 1.6 collective-permute-start.14
  182.7 4.1 %collective-permute-start.16 = (bf16[2,128,256]{2,1,0:T(8,128)(2,1)S(1)}, bf16[2,128,256]{2,1,0:T(8,128)(2,1)S(1)}, u32[]{:S(2)}, u32[]{:S(2)}) collective-permute-start(bf16[2,128,256]{2,1,0:T(8,128)(2,1)S(1)} %pad_maximum_fusion.1), channel_id=1, source_target_pairs={{0,96},{16,112},{32,0},{48,16},{64,32},{80,48},{96,64},{112,80},{1... | collective-permute-start | bytes 393224 | tf_op jit(solution)/shard_map/ppermute | solution.py:36
  186.8 3.7 %shard_map.84 = (bf16[2,256,2560]{2,1,0:T(8,128)(2,1)}, f32[1,2560]{1,0:T(1,128)}) custom-call(bf16[16,336,128]{2,1,0:T(8,128)(2,1)S(1)} %all-to-all-done.3.came_ref, bf16[2,256,2560]{2,1,0:T(8,128)(2,1)} %shard_map.83.rest_0_), custom_call_target="tpu_custom_call", output_to_operand_aliasing={{0}: (1, {})} | custom-call | bytes 5263360 | tf_op jit(solution)/shard_map/pallas_call | solution.py:290
  190.5 0.3 collective-permute-done.15.refs_3_
  190.8 1.2 collective-permute-done.16.refs_4_
  192.0 0.0 collective-permute-done.14.refs_2_
  192.0 1.8 shard_map.85
  (30 shorter events, 0.2 us)
Async XLA Ops:
  3.7 11.2 %copy-start = (bf16[1,2,256,1024]{3,2,1,0:T(8,128)(2,1)S(1)}, bf16[1,2,256,1024]{3,2,1,0:T(8,128)(2,1)}, u32[]{:S(2)}) copy-start(bf16[1,2,256,1024]{3,2,1,0:T(8,128)(2,1)} %param.7) | copy-start | bytes 3145732
  3.7 18.2 %copy-start.8 = (s32[2,256]{1,0:T(2,128)S(1)}, s32[2,256]{1,0:T(2,128)}, u32[]{:S(2)}) copy-start(s32[2,256]{1,0:T(2,128)} %param.8) | copy-start | bytes 6148
  3.7 49.4 %all-to-all-start = ((bf16[16,336,128]{2,1,0:T(8,128)(2,1)}), bf16[16,336,128]{2,1,0:T(8,128)(2,1)S(1)}, u32[]{:S(2)}, u32[]{:S(2)}) async-start(bf16[16,336,128]{2,1,0:T(8,128)(2,1)} %shard_map.77), calls=%async_computation | async-start | bytes 2752512 | tf_op jit(solution)/shard_map/all_to_all | solution.py:48
  15.8 25.7 %collective-permute-start = (bf16[256,1024]{1,0:T(8,128)(2,1)}, bf16[256,1024]{1,0:T(8,128)(2,1)}, u32[]{:S(2)}, u32[]{:S(2)}) collective-permute-start(bf16[256,1024]{1,0:T(8,128)(2,1)} %slice_bitcast_fusion), channel_id=1, source_target_pairs={{0,128},{1,129},{2,130},{3,131},{4,132},{5,133},{6,134},{7,135},{8... | collective-permute-start | bytes 1572872 | tf_op jit(solution)/shard_map/ppermute | solution.py:36
  42.5 4.9 %collective-permute-start.3 = (bf16[256,256]{1,0:T(8,128)(2,1)}, bf16[256,256]{1,0:T(8,128)(2,1)S(1)}, u32[]{:S(2)}, u32[]{:S(2)}) collective-permute-start(bf16[256,256]{1,0:T(8,128)(2,1)} %get-tuple-element.29), channel_id=1, source_target_pairs={{0,96},{128,224},{1,97},{129,225},{2,98},{130,226},{3,99},{131,227... | collective-permute-start | bytes 393224 | tf_op jit(solution)/shard_map/ppermute | solution.py:36
  43.8 5.5 %collective-permute-start.1 = (bf16[256,256]{1,0:T(8,128)(2,1)S(1)}, bf16[256,256]{1,0:T(8,128)(2,1)S(1)}, u32[]{:S(2)}, u32[]{:S(2)}) collective-permute-start(bf16[256,256]{1,0:T(8,128)(2,1)S(1)} %get-tuple-element.27), channel_id=1, source_target_pairs={{0,64},{128,192},{1,65},{129,193},{2,66},{130,194},{3,67},{131,195... | collective-permute-start | bytes 393224 | tf_op jit(solution)/shard_map/ppermute | solution.py:36
  45.1 6.0 %collective-permute-start.2 = (bf16[256,256]{1,0:T(8,128)(2,1)S(1)}, bf16[256,256]{1,0:T(8,128)(2,1)S(1)}, u32[]{:S(2)}, u32[]{:S(2)}) collective-permute-start(bf16[256,256]{1,0:T(8,128)(2,1)S(1)} %get-tuple-element.28), channel_id=1, source_target_pairs={{0,32},{128,160},{1,33},{129,161},{2,34},{130,162},{3,35},{131,163... | collective-permute-start | bytes 393224 | tf_op jit(solution)/shard_map/ppermute | solution.py:36
  51.2 11.7 %collective-permute-start.4 = (bf16[256,256]{1,0:T(8,128)(2,1)S(1)}, bf16[256,256]{1,0:T(8,128)(2,1)}, u32[]{:S(2)}, u32[]{:S(2)}) collective-permute-start(bf16[256,256]{1,0:T(8,128)(2,1)S(1)} %add_select_fusion.even_ref), channel_id=1, source_target_pairs={{0,16},{32,48},{64,80},{96,112},{128,144},{160,176},{192,208},{224... | collective-permute-start | bytes 393224 | tf_op jit(solution)/shard_map/ppermute | solution.py:36
  53.1 41.8 %all-to-all-start.1 = ((bf16[16,320,128]{2,1,0:T(8,128)(2,1)}), bf16[16,320,128]{2,1,0:T(8,128)(2,1)S(1)}, u32[]{:S(2)}, u32[]{:S(2)}) async-start(bf16[16,320,128]{2,1,0:T(8,128)(2,1)} %shard_map.76), calls=%async_computation.1 | async-start | bytes 2621440 | tf_op jit(solution)/shard_map/all_to_all | solution.py:48
  62.9 1.0 copy-start.1
  74.8 0.7 copy-start.2
  75.5 0.7 copy-start.4
  76.1 0.6 copy-start.6
  94.9 3.9 %copy-start.5 = (bf16[256,256]{1,0:T(8,128)(2,1)S(1)}, bf16[256,256]{1,0:T(8,128)(2,1)}, u32[]{:S(2)}) copy-start(bf16[256,256]{1,0:T(8,128)(2,1)} %copy-done.4) | copy-start | bytes 393220
  94.9 3.9 %copy-start.7 = (f32[16,8,128]{2,1,0:T(8,128)S(1)}, f32[16,8,128]{2,1,0:T(8,128)}, u32[]{:S(2)}) copy-start(f32[16,8,128]{2,1,0:T(8,128)} %copy-done.6) | copy-start | bytes 196612
  94.9 38.3 %all-to-all-start.2 = ((bf16[16,320,128]{2,1,0:T(8,128)(2,1)}), bf16[16,320,128]{2,1,0:T(8,128)(2,1)S(1)}, u32[]{:S(2)}, u32[]{:S(2)}) async-start(bf16[16,320,128]{2,1,0:T(8,128)(2,1)} %get-tuple-element.37), calls=%async_computation.2 | async-start | bytes 2621440 | tf_op jit(solution)/shard_map/all_to_all | solution.py:48
  98.8 1.0 copy-start.3
  108.2 1.3 collective-permute-start.5
  109.5 4.4 %collective-permute-start.6 = (f32[16,8,128]{2,1,0:T(8,128)S(1)}, f32[16,8,128]{2,1,0:T(8,128)S(1)}, u32[]{:S(2)}, u32[]{:S(2)}) collective-permute-start(f32[16,8,128]{2,1,0:T(8,128)S(1)} %add.99), channel_id=1, source_target_pairs={{0,2},{1,3},{2,0},{3,1},{4,6},{5,7},{6,4},{7,5},{8,10},{9,11},{10,... | collective-permute-start | bytes 196616 | tf_op jit(solution)/shard_map/ppermute | solution.py:44
  113.9 5.9 %collective-permute-start.7 = (f32[16,8,128]{2,1,0:T(8,128)S(1)}, f32[16,8,128]{2,1,0:T(8,128)S(1)}, u32[]{:S(2)}, u32[]{:S(2)}) collective-permute-start(f32[16,8,128]{2,1,0:T(8,128)S(1)} %add.100), channel_id=1, source_target_pairs={{0,4},{1,5},{2,6},{3,7},{4,0},{5,1},{6,2},{7,3},{8,12},{9,13},{10,... | collective-permute-start | bytes 196616 | tf_op jit(solution)/shard_map/ppermute | solution.py:44
  116.3 16.9 %collective-permute-start.9 = (f32[128,256]{1,0:T(8,128)S(1)}, f32[128,256]{1,0:T(8,128)S(1)}, u32[]{:S(2)}, u32[]{:S(2)}) collective-permute-start(f32[128,256]{1,0:T(8,128)S(1)} %dynamic-slice_bitcast_fusion), channel_id=1, source_target_pairs={{0,16},{16,0},{32,48},{48,32},{64,80},{80,64},{96,112},{112,96},{1... | collective-permute-start | bytes 393224 | tf_op jit(solution)/shard_map/ppermute | solution.py:44
  119.8 4.8 %collective-permute-start.8 = (f32[16,8,128]{2,1,0:T(8,128)S(1)}, f32[16,8,128]{2,1,0:T(8,128)S(1)}, u32[]{:S(2)}, u32[]{:S(2)}) collective-permute-start(f32[16,8,128]{2,1,0:T(8,128)S(1)} %add.101), channel_id=1, source_target_pairs={{0,8},{1,9},{2,10},{3,11},{4,12},{5,13},{6,14},{7,15},{8,0},{9,1},... | collective-permute-start | bytes 196616 | tf_op jit(solution)/shard_map/ppermute | solution.py:44
  133.2 46.1 %all-to-all-start.3 = ((bf16[16,336,128]{2,1,0:T(8,128)(2,1)}), bf16[16,336,128]{2,1,0:T(8,128)(2,1)S(1)}, u32[]{:S(2)}, u32[]{:S(2)}) async-start(bf16[16,336,128]{2,1,0:T(8,128)(2,1)} %shard_map.82), calls=%async_computation.3 | async-start | bytes 2752512 | tf_op jit(solution)/shard_map/all_to_all | solution.py:48
  138.9 12.1 %collective-permute-start.10 = (bf16[128,256]{1,0:T(8,128)(2,1)S(1)}, bf16[128,256]{1,0:T(8,128)(2,1)S(1)}, u32[]{:S(2)}, u32[]{:S(2)}) collective-permute-start(bf16[128,256]{1,0:T(8,128)(2,1)S(1)} %fusion.4), channel_id=1, source_target_pairs={{0,128},{16,144},{32,160},{48,176},{64,192},{80,208},{96,224},{112... | collective-permute-start | bytes 196616 | tf_op jit(solution)/shard_map/ppermute | solution.py:44
  145.4 33.7 %collective-permute-start.12 = (bf16[128,256]{1,0:T(8,128)(2,1)S(1)}, bf16[128,256]{1,0:T(8,128)(2,1)S(1)}, u32[]{:S(2)}, u32[]{:S(2)}) collective-permute-start(bf16[128,256]{1,0:T(8,128)(2,1)S(1)} %fusion.4), channel_id=1, source_target_pairs={{0,192},{16,208},{32,224},{48,240},{64,128},{80,144},{96,160},{112... | collective-permute-start | bytes 196616 | tf_op jit(solution)/shard_map/ppermute | solution.py:44
  150.9 28.5 %collective-permute-start.11 = (bf16[128,256]{1,0:T(8,128)(2,1)S(1)}, bf16[128,256]{1,0:T(8,128)(2,1)S(1)}, u32[]{:S(2)}, u32[]{:S(2)}) collective-permute-start(bf16[128,256]{1,0:T(8,128)(2,1)S(1)} %fusion.4), channel_id=1, source_target_pairs={{0,64},{16,80},{32,96},{48,112},{64,0},{80,16},{96,32},{112,48},{1... | collective-permute-start | bytes 196616 | tf_op jit(solution)/shard_map/ppermute | solution.py:44
  179.4 12.6 %collective-permute-start.13 = (bf16[4,128,256]{2,1,0:T(8,128)(2,1)S(1)}, bf16[4,128,256]{2,1,0:T(8,128)(2,1)S(1)}, u32[]{:S(2)}, u32[]{:S(2)}) collective-permute-start(bf16[4,128,256]{2,1,0:T(8,128)(2,1)S(1)} %pad_maximum_fusion.refs_0_), channel_id=1, source_target_pairs={{0,16},{16,32},{32,48},{48,64},{64,80},{80,96},{96,112},{112,0},{1... | collective-permute-start | bytes 786440 | tf_op jit(solution)/shard_map/ppermute | solution.py:36
  181.1 10.9 %collective-permute-start.14 = (bf16[4,128,256]{2,1,0:T(8,128)(2,1)S(1)}, bf16[4,128,256]{2,1,0:T(8,128)(2,1)S(1)}, u32[]{:S(2)}, u32[]{:S(2)}) collective-permute-start(bf16[4,128,256]{2,1,0:T(8,128)(2,1)S(1)} %pad_maximum_fusion.refs_0_), channel_id=1, source_target_pairs={{0,112},{16,0},{32,16},{48,32},{64,48},{80,64},{96,80},{112,96},{1... | collective-permute-start | bytes 786440 | tf_op jit(solution)/shard_map/ppermute | solution.py:36
  182.7 8.1 %collective-permute-start.15 = (bf16[2,128,256]{2,1,0:T(8,128)(2,1)S(1)}, bf16[2,128,256]{2,1,0:T(8,128)(2,1)S(1)}, u32[]{:S(2)}, u32[]{:S(2)}) collective-permute-start(bf16[2,128,256]{2,1,0:T(8,128)(2,1)S(1)} %pad_maximum_fusion.1), channel_id=1, source_target_pairs={{0,32},{16,48},{32,64},{48,80},{64,96},{80,112},{96,0},{112,16},{1... | collective-permute-start | bytes 393224 | tf_op jit(solution)/shard_map/ppermute | solution.py:36
  182.7 9.3 %collective-permute-start.16 = (bf16[2,128,256]{2,1,0:T(8,128)(2,1)S(1)}, bf16[2,128,256]{2,1,0:T(8,128)(2,1)S(1)}, u32[]{:S(2)}, u32[]{:S(2)}) collective-permute-start(bf16[2,128,256]{2,1,0:T(8,128)(2,1)S(1)} %pad_maximum_fusion.1), channel_id=1, source_target_pairs={{0,96},{16,112},{32,0},{48,16},{64,32},{80,48},{96,64},{112,80},{1... | collective-permute-start | bytes 393224 | tf_op jit(solution)/shard_map/ppermute | solution.py:36

commit v5 on v4

--- a/solution.py
+++ b/solution.py
@@ -128,31 +128,30 @@
     )(me.reshape(1), raw, across)
 
 
-def pick(me, at_even, at_odd):
-    def kernel(me_ref, even_ref, odd_ref, out_ref):
-        out_ref[...] = jnp.where(lax.rem(me_ref[0], 2) == 0, even_ref[...], odd_ref[...])
+def pick(me, at_first, at_second):
+    def kernel(me_ref, first_ref, second_ref, out_ref):
+        z = lax.rem(me_ref[0], RING)
+        first = lax.rem(z, 2) == z // 4
+        out_ref[...] = jnp.where(first, first_ref[...], second_ref[...])
 
     return pl.pallas_call(
         kernel,
-        out_shape=jax.ShapeDtypeStruct(at_even.shape, at_even.dtype),
+        out_shape=jax.ShapeDtypeStruct(at_first.shape, at_first.dtype),
         in_specs=[SMEM, VMEM, VMEM],
         out_specs=VMEM,
         compiler_params=pltpu.CompilerParams(vmem_limit_bytes=SOME_ROOM),
         cost_estimate=pl.CostEstimate(
             flops=UNITS_FLOPS, bytes_accessed=1024 * 1024, transcendentals=0
         ),
-    )(me.reshape(1), at_even, at_odd)
+    )(me.reshape(1), at_first, at_second)
 
 
 def cache_whole(me, *pieces):
     def kernel(me_ref, *refs):
-        sources, (whole_ref, held, in_sems, out_sems) = refs[: len(GATHERED)], refs[len(GATHERED) :]
+        sources, (whole_ref, sems) = refs[: len(GATHERED)], refs[len(GATHERED) :]
         here = me_ref[0]
         copies = []
-        n = 0
         for source, places in zip(sources, GATHERED):
-            later = []
-            first_slot = n
             for i, back in enumerate(places):
                 for side in range(2):
                     owner = lax.rem(here + RING - back, RING)
@@ -161,25 +160,21 @@
                     start = pl.multiple_of(half * (LENGTH // 2), LENGTH // 2)
                     for part in range(2):
                         column = pl.multiple_of(head * HEAD + part * KEY_WIDTH, HEAD)
-                        later.append(
+                        copies.append(
                             pltpu.make_async_copy(
-                                held.at[n, :, pl.ds(part * HEAD, HEAD)],
+                                source.at[2 * i + side, :, pl.ds(part * HEAD, HEAD)],
                                 whole_ref.at[micro, pl.ds(start, LENGTH // 2), pl.ds(column, HEAD)],
-                                out_sems.at[n, part],
+                                sems.at[len(copies)],
                             )
                         )
-                    n += 1
-            slots = held.at[pl.ds(first_slot, n - first_slot)]
-            copies.append((pltpu.make_async_copy(source, slots, in_sems.at[first_slot]), later))
-        run_copies(copies)
+        for copy in copies:
+            copy.start()
+        for copy in copies:
+            copy.wait()
 
     out = jax.ShapeDtypeStruct((MICROS, LENGTH, 2 * KEY_WIDTH), pieces[0].dtype)
-    scratch = [
-        pltpu.VMEM((SECTIONS, LENGTH // 2, 2 * HEAD), out.dtype),
-        pltpu.SemaphoreType.DMA((SECTIONS,)),
-        pltpu.SemaphoreType.DMA((SECTIONS, 2)),
-    ]
-    in_specs = [SMEM] + [IN_HBM] * len(pieces)
+    scratch = [pltpu.SemaphoreType.DMA((2 * SECTIONS,))]
+    in_specs = [SMEM] + [VMEM] * len(pieces)
     return moving_call(kernel, out, scratch, in_specs)(me.reshape(1), *pieces)
 
 
@@ -217,12 +212,16 @@
         ]
         for copy in arriving:
             copy.start()
+        if gains is not None:
+            rows = [refs[0][:, i * HEAD : (i + 1) * HEAD] for i in range(HEADS)]
+            parts = [
+                three_parts(jnp.concatenate(rows[k * GROUP : (k + 1) * GROUP], axis=0))
+                for k in range(KV_HEADS)
+            ]
         leaving = []
         for owner in range(SECTIONS):
             if gains is not None:
-                first = owner % RING // 2 * WIDE
-                heads = [refs[0][:, first + h * HEAD : first + (h + 1) * HEAD] for h in range(GROUP)]
-                stacked[owner, STACK:] = three_parts(jnp.concatenate(heads, axis=0))
+                stacked[owner, STACK:] = parts[owner % RING // 2]
             arriving[owner].wait()
             for h in range(GROUP):
                 stacked[owner, h * BLOCK : (h + 1) * BLOCK] = held[owner, :, h * HEAD : (h + 1) * HEAD]
@@ -240,27 +239,28 @@
         pltpu.SemaphoreType.DMA((SECTIONS,)),
     ]
     if gains is None:
-        return moving_call(kernel, out, scratch, [IN_HBM], room=ALL_ROOM)(whole)
+        return moving_call(kernel, out, scratch, [IN_HBM])(whole)
     return moving_call(kernel, out, scratch, [VMEM, IN_HBM], room=ALL_ROOM)(gains, whole)
 
 
 def unpack(came, late, whole=None):
-    tall = came.shape[1]
-
     def kernel(came_ref, *rest):
         if whole is None:
             out_ref, (held, spread, in_sems, out_sems) = rest[0], rest[1:]
         else:
-            _, out_ref, gain_ref, held, spread, in_sems, out_sems = rest
-        arriving = [
-            pltpu.make_async_copy(came_ref.at[owner], held.at[owner], in_sems.at[owner])
-            for owner in range(SECTIONS)
-        ]
-        for copy in arriving:
-            copy.start()
+            _, out_ref, gain_ref, spread, out_sems = rest
+            held = came_ref
+        if whole is None:
+            arriving = [
+                pltpu.make_async_copy(came_ref.at[owner], held.at[owner], in_sems.at[owner])
+                for owner in range(SECTIONS)
+            ]
+            for copy in arriving:
+                copy.start()
         leaving = []
         for owner, place in home_places(late):
-            arriving[owner].wait()
+            if whole is None:
+                arriving[owner].wait()
             for h in range(GROUP):
                 spread[owner, :, h * HEAD : (h + 1) * HEAD] = held[owner, h * BLOCK : (h + 1) * BLOCK]
             copy = pltpu.make_async_copy(spread.at[owner], out_ref.at[place], out_sems.at[owner])
@@ -279,15 +279,14 @@
 
     out = jax.ShapeDtypeStruct((MICROS, LENGTH, HEADS * HEAD), came.dtype)
     scratch = [
-        pltpu.VMEM(came.shape, came.dtype),
         pltpu.VMEM((SECTIONS, BLOCK, WIDE), came.dtype),
-        pltpu.SemaphoreType.DMA((SECTIONS,)),
         pltpu.SemaphoreType.DMA((SECTIONS,)),
     ]
     if whole is None:
-        return moving_call(kernel, out, scratch, [IN_HBM])(came)
+        first = [pltpu.VMEM(came.shape, came.dtype), scratch[0], scratch[1], scratch[1]]
+        return moving_call(kernel, out, first, [IN_HBM])(came)
     outs = [out, jax.ShapeDtypeStruct((1, HEADS * HEAD), jnp.float32)]
-    return moving_call(kernel, outs, scratch, [IN_HBM, IN_HBM], {1: 0})(came, whole)
+    return moving_call(kernel, outs, scratch, [VMEM, IN_HBM], {1: 0})(came, whole)
 
 
 def with_gains(grads, gain_part):
@@ -435,12 +434,13 @@
     ready = after(saved_inputs[0], late_bias, early_bias, late_top, early_top)
     early_packed = pack(ready, False)
     four = own_units(me, raw, after(across, early_packed))
-    came = [moved(four[k], [(0, 2 * k), (RING, RING + 2 * k)]) for k in (2, 1, 3)]
-    at_even = jnp.where(me % RING == 0, four[0], came[0] + came[1] + came[2])
-    at_even = after(at_even, early_packed)
-    at_odd = moved(at_even, [(i, i + 1) for i in range(0, SECTIONS, 2)])
-    kv_unit = pick(me, at_even, at_odd)
-    early_saved = exchange(after(early_packed, late_saved, at_even))
+    came = [moved(four[k], [(0, z), (RING, RING + z)]) for k, z in ((2, 5), (1, 2), (3, 7))]
+    at_first = jnp.where(me % RING == 0, four[0], came[0] + came[1] + came[2])
+    at_first = after(at_first, early_packed)
+    onward = ((0, 1), (2, 3), (5, 4), (7, 6))
+    at_second = moved(at_first, [(x + i, x + j) for x in (0, RING) for i, j in onward])
+    kv_unit = pick(me, at_first, at_second)
+    early_saved = exchange(after(early_packed, late_saved, at_first))
 
     late_grads, cache_part, gains, gain_part = chain(
         late_kernel, late_saved, kv_unit, late_bias, late_top, STACK,

time: 195 us -> 193 us (0.990)
  Pallas kernels: 36.1 us -> 32.6 us
    pallas_call x4, Pallas kernels: 10 us -> 6.37 us  [the longest x1 3 us: unpack(): return moving_call(kernel, out, first, [IN_HBM])(came)]
    unnamed x18 -> x22, local copies, waits for them, and re-layouts: 2.94 us -> 4.34 us
  transfers between devices with their start and end apart: 21 -> 21, of which waited for: 14 -> 13; matrix products, arithmetic and copies ran while one was open for 2% -> 2% of each run, Pallas kernels for 16% -> 15%
where the time goes in v5:
time: 193 us; the launch traced here: 192 us
  waiting for transfers between devices  86.9 us (45%)
  starting transfers between devices  63.8 us (33%)
  Pallas kernels  32.6 us (17%)
  local copies, waits for them, and re-layouts  7.59 us (4%)
    ppermute x8, waiting for transfers between devices, swapped(): return lax.ppermute(array, axis, [(i, i ^ bit) for i in range(16)])  38.6 us
    all_to_all x4, starting transfers between devices, exchange(): return lax.all_to_all(array, 'section', 0, 0, tiled=True)  30.4 us
    all_to_all x4, waiting for transfers between devices, exchange(): return lax.all_to_all(array, 'section', 0, 0, tiled=True)  25.5 us
    ppermute x9, waiting for transfers between devices, moved(): return lax.ppermute(array, 'section', pairs)  22.9 us
    pallas_call x2, Pallas kernels, chain(): pl.pallas_call(kernel, out_shape=[jax.ShapeDtypeStruct(*shape) for shape...  20.7 us
    ppermute x9, starting transfers between devices, moved(): return lax.ppermute(array, 'section', pairs)  18.7 us
    ppermute x8, starting transfers between devices, swapped(): return lax.ppermute(array, axis, [(i, i ^ bit) for i in range(16)])  14.7 us
    unnamed x22, local copies, waits for them, and re-layouts  4.34 us
  transfers between devices with their start and end apart: 21, of which 13 were waited for; matrix products, arithmetic and copies ran while one was open for 2% of the time, Pallas kernels for 15%

profile of v5, /device:TPU:8, one launch (start us, length us, event | category | flops | bytes accessed | tf_op | source)
XLA Modules:
  0.0 192.2 jit_solution(6693418499437010891)
XLA Ops:
  0.6 3.0 %shard_map.77 = bf16[16,336,128]{2,1,0:T(8,128)(2,1)} custom-call(f32[1,2560]{1,0:T(1,128)} %refs_0_.1, bf16[2,256,2560]{2,1,0:T(8,128)(2,1)} %bitcast.28), custom_call_target="tpu_custom_call" | custom-call | bytes 2752512 | tf_op jit(solution)/shard_map/pallas_call | solution.py:243
  3.7 0.0 copy-start.10
  3.7 0.0 copy-start
  3.7 11.3 %all-to-all-start = ((bf16[16,336,128]{2,1,0:T(8,128)(2,1)}), bf16[16,336,128]{2,1,0:T(8,128)(2,1)}, u32[]{:S(2)}, u32[]{:S(2)}) async-start(bf16[16,336,128]{2,1,0:T(8,128)(2,1)} %shard_map.77), calls=%async_computation | async-start | bytes 2752512 | tf_op jit(solution)/shard_map/all_to_all | solution.py:48
  15.0 1.9 slice_bitcast_fusion
  16.9 6.1 %collective-permute-start = (bf16[256,1024]{1,0:T(8,128)(2,1)}, bf16[256,1024]{1,0:T(8,128)(2,1)}, u32[]{:S(2)}, u32[]{:S(2)}) collective-permute-start(bf16[256,1024]{1,0:T(8,128)(2,1)} %slice_bitcast_fusion), channel_id=1, source_target_pairs={{0,128},{1,129},{2,130},{3,131},{4,132},{5,133},{6,134},{7,135},{8... | collective-permute-start | bytes 1572872 | tf_op jit(solution)/shard_map/ppermute | solution.py:36
  23.1 0.1 dynamic-slice_bitcast_fusion.3
  23.1 0.1 eq.43
  23.2 0.1 add.88
  23.3 0.1 eq.48
  23.4 0.1 add.93
  23.5 0.9 dynamic-slice_bitcast_fusion.1
  24.4 0.1 fusion.3.bias_ref
  24.5 0.1 fusion.1.bias_ref
  24.7 0.0 copy-start.1
  24.7 1.6 shard_map.76
  26.2 15.5 %collective-permute-done.across_ref = bf16[256,1024]{1,0:T(8,128)(2,1)} collective-permute-done((bf16[256,1024]{1,0:T(8,128)(2,1)}, bf16[256,1024]{1,0:T(8,128)(2,1)}, u32[]{:S(2)}, u32[]{:S(2)}) %collective-permute-start) | collective-permute-done | bytes 524320 | tf_op jit(solution)/shard_map/ppermute | solution.py:36
  41.7 0.4 shard_map.78
  42.1 1.3 collective-permute-start.3
  43.4 1.3 collective-permute-start.1
  44.7 1.3 collective-permute-start.2
  46.1 2.5 %collective-permute-done.3 = bf16[256,256]{1,0:T(8,128)(2,1)S(1)} collective-permute-done((bf16[256,256]{1,0:T(8,128)(2,1)S(1)}, bf16[256,256]{1,0:T(8,128)(2,1)S(1)}, u32[]{:S(2)}, u32[]{:S(2)}) %collective-permute-start.3) | collective-permute-done | bytes 131104 | tf_op jit(solution)/shard_map/ppermute | solution.py:36
  48.5 1.7 collective-permute-done.1
  50.2 0.0 collective-permute-done.2
  50.2 1.3 collective-permute-start.4
  51.5 9.7 %all-to-all-start.1 = ((bf16[16,320,128]{2,1,0:T(8,128)(2,1)}), bf16[16,320,128]{2,1,0:T(8,128)(2,1)S(1)}, u32[]{:S(2)}, u32[]{:S(2)}) async-start(bf16[16,320,128]{2,1,0:T(8,128)(2,1)} %shard_map.76), calls=%async_computation.1 | async-start | bytes 2621440 | tf_op jit(solution)/shard_map/all_to_all | solution.py:48
  61.2 12.3 %shard_map.80 = (bf16[16,320,128]{2,1,0:T(8,128)(2,1)}, f32[256,256]{1,0:T(8,128)S(1)}, f32[16,8,128]{2,1,0:T(8,128)S(1)}, f32[16,8,128]{2,1,0:T(8,128)S(1)}) custom-call(bf16[16,336,128]{2,1,0:T(8,128)(2,1)} %all-to-all-done.saved_ref, bf16[256,256]{1,0:T(8,128)(2,1)S(1)} %shard_map.79.kv_ref, f32[256,320]{1,0:T(8,128)S(1)} %fusion.1.bias_ref, ...), custom_call_target="tpu_custom_call" | custom-call | flops 1677721600 | bytes 6291456 | tf_op jit(solution)/shard_map/pallas_call | solution.py:392
  73.5 0.7 copy-done.2
  74.2 0.6 copy-done.4
  74.8 0.6 copy-done.6
  75.5 0.6 copy-done.8
  76.1 18.2 %all-to-all-done.1.saved_ref = bf16[16,320,128]{2,1,0:T(8,128)(2,1)S(1)} async-done(((bf16[16,320,128]{2,1,0:T(8,128)(2,1)}), bf16[16,320,128]{2,1,0:T(8,128)(2,1)S(1)}, u32[]{:S(2)}, u32[]{:S(2)}) %all-to-all-start.1) | async-done | bytes 1310752 | tf_op jit(solution)/shard_map/all_to_all | solution.py:48
  94.3 3.9 %all-to-all-start.2 = ((bf16[16,320,128]{2,1,0:T(8,128)(2,1)}), bf16[16,320,128]{2,1,0:T(8,128)(2,1)S(1)}, u32[]{:S(2)}, u32[]{:S(2)}) async-start(bf16[16,320,128]{2,1,0:T(8,128)(2,1)} %get-tuple-element.37), calls=%async_computation.2 | async-start | bytes 2621440 | tf_op jit(solution)/shard_map/all_to_all | solution.py:48
  98.3 0.9 copy-done.5
  99.2 0.8 copy-done.9
  100.0 8.5 %shard_map.81 = (bf16[16,336,128]{2,1,0:T(8,128)(2,1)}, f32[256,256]{1,0:T(8,128)S(1)}, f32[16,8,128]{2,1,0:T(8,128)S(1)}) custom-call(bf16[16,320,128]{2,1,0:T(8,128)(2,1)S(1)} %all-to-all-done.1.saved_ref, bf16[256,256]{1,0:T(8,128)(2,1)S(1)} %copy-done.5, f32[128,320]{1,0:T(8,128)S(1)} %fusion.3.bias_ref, bf16[64,640]{1,0:T(8,128)(2,1)S(1)} %get-tuple-element.45.top_ref, ...), custom_call_target="tpu_custom_call" | custom-call | flops 838860800 | bytes 6291456 | tf_op jit(solution)/shard_map/pallas_call | solution.py:392
  108.5 0.0 collective-permute-start.5
  108.5 1.3 collective-permute-done.5
  109.8 0.5 collective-permute-start.6
  110.3 3.8 %collective-permute-done.6 = f32[16,8,128]{2,1,0:T(8,128)S(1)} collective-permute-done((f32[16,8,128]{2,1,0:T(8,128)S(1)}, f32[16,8,128]{2,1,0:T(8,128)S(1)}, u32[]{:S(2)}, u32[]{:S(2)}) %collective-permute-start.6) | collective-permute-done | bytes 65568 | tf_op jit(solution)/shard_map/ppermute | solution.py:44
  114.1 2.4 %collective-permute-start.7 = (f32[16,8,128]{2,1,0:T(8,128)S(1)}, f32[16,8,128]{2,1,0:T(8,128)S(1)}, u32[]{:S(2)}, u32[]{:S(2)}) collective-permute-start(f32[16,8,128]{2,1,0:T(8,128)S(1)} %add.100), channel_id=1, source_target_pairs={{0,4},{1,5},{2,6},{3,7},{4,0},{5,1},{6,2},{7,3},{8,12},{9,13},{10,... | collective-permute-start | bytes 196616 | tf_op jit(solution)/shard_map/ppermute | solution.py:44
  116.5 2.0 %collective-permute-start.9 = (f32[128,256]{1,0:T(8,128)S(1)}, f32[128,256]{1,0:T(8,128)S(1)}, u32[]{:S(2)}, u32[]{:S(2)}) collective-permute-start(f32[128,256]{1,0:T(8,128)S(1)} %dynamic-slice_bitcast_fusion), channel_id=1, source_target_pairs={{0,16},{16,0},{32,48},{48,32},{64,80},{80,64},{96,112},{112,96},{1... | collective-permute-start | bytes 393224 | tf_op jit(solution)/shard_map/ppermute | solution.py:44
  118.5 1.5 collective-permute-done.7
  120.0 0.7 collective-permute-start.8
  120.7 3.8 %collective-permute-done.8 = f32[16,8,128]{2,1,0:T(8,128)S(1)} collective-permute-done((f32[16,8,128]{2,1,0:T(8,128)S(1)}, f32[16,8,128]{2,1,0:T(8,128)S(1)}, u32[]{:S(2)}, u32[]{:S(2)}) %collective-permute-start.8) | collective-permute-done | bytes 65568 | tf_op jit(solution)/shard_map/ppermute | solution.py:44
  124.5 0.8 shard_map.82
  125.3 7.3 %all-to-all-done.2.came_ref = bf16[16,320,128]{2,1,0:T(8,128)(2,1)S(1)} async-done(((bf16[16,320,128]{2,1,0:T(8,128)(2,1)}), bf16[16,320,128]{2,1,0:T(8,128)(2,1)S(1)}, u32[]{:S(2)}, u32[]{:S(2)}) %all-to-all-start.2) | async-done | bytes 1310752 | tf_op jit(solution)/shard_map/all_to_all | solution.py:48
  132.6 5.4 %all-to-all-start.3 = ((bf16[16,336,128]{2,1,0:T(8,128)(2,1)}), bf16[16,336,128]{2,1,0:T(8,128)(2,1)S(1)}, u32[]{:S(2)}, u32[]{:S(2)}) async-start(bf16[16,336,128]{2,1,0:T(8,128)(2,1)} %shard_map.82), calls=%async_computation.3 | async-start | bytes 2752512 | tf_op jit(solution)/shard_map/all_to_all | solution.py:48
  138.0 3.5 %collective-permute-start.10 = (bf16[128,256]{1,0:T(8,128)(2,1)S(1)}, bf16[128,256]{1,0:T(8,128)(2,1)S(1)}, u32[]{:S(2)}, u32[]{:S(2)}) collective-permute-start(bf16[128,256]{1,0:T(8,128)(2,1)S(1)} %fusion.4), channel_id=1, source_target_pairs={{0,128},{16,144},{32,160},{48,176},{64,192},{80,208},{96,224},{112... | collective-permute-start | bytes 196616 | tf_op jit(solution)/shard_map/ppermute | solution.py:44
  141.5 3.0 %shard_map.83.rest_0_ = bf16[2,256,2560]{2,1,0:T(8,128)(2,1)} custom-call(bf16[16,320,128]{2,1,0:T(8,128)(2,1)S(1)} %all-to-all-done.2.came_ref), custom_call_target="tpu_custom_call" | custom-call | bytes 5242880 | tf_op jit(solution)/shard_map/pallas_call | solution.py:287
  144.5 5.5 %collective-permute-start.12 = (bf16[128,256]{1,0:T(8,128)(2,1)S(1)}, bf16[128,256]{1,0:T(8,128)(2,1)S(1)}, u32[]{:S(2)}, u32[]{:S(2)}) collective-permute-start(bf16[128,256]{1,0:T(8,128)(2,1)S(1)} %fusion.4), channel_id=1, source_target_pairs={{0,192},{16,208},{32,224},{48,240},{64,128},{80,144},{96,160},{112... | collective-permute-start | bytes 196616 | tf_op jit(solution)/shard_map/ppermute | solution.py:44
  150.0 0.1 collective-permute-start.11
  150.1 0.0 collective-permute-done.10
  150.1 28.0 %collective-permute-done.12 = bf16[128,256]{1,0:T(8,128)(2,1)S(1)} collective-permute-done((bf16[128,256]{1,0:T(8,128)(2,1)S(1)}, bf16[128,256]{1,0:T(8,128)(2,1)S(1)}, u32[]{:S(2)}, u32[]{:S(2)}) %collective-permute-start.12) | collective-permute-done | bytes 65568 | tf_op jit(solution)/shard_map/ppermute | solution.py:44
  178.1 0.2 collective-permute-done.11
  178.4 1.9 collective-permute-start.13
  180.3 1.5 collective-permute-start.14
  181.7 0.1 collective-permute-start.15
  181.8 4.0 %collective-permute-start.16 = (bf16[2,128,256]{2,1,0:T(8,128)(2,1)S(1)}, bf16[2,128,256]{2,1,0:T(8,128)(2,1)S(1)}, u32[]{:S(2)}, u32[]{:S(2)}) collective-permute-start(bf16[2,128,256]{2,1,0:T(8,128)(2,1)S(1)} %pad_maximum_fusion.1), channel_id=1, source_target_pairs={{0,96},{16,112},{32,0},{48,16},{64,32},{80,48},{96,64},{112,80},{1... | collective-permute-start | bytes 393224 | tf_op jit(solution)/shard_map/ppermute | solution.py:36
  185.9 1.8 shard_map.84
  187.7 2.1 %collective-permute-done.15.refs_3_ = bf16[2,128,256]{2,1,0:T(8,128)(2,1)S(1)} collective-permute-done((bf16[2,128,256]{2,1,0:T(8,128)(2,1)S(1)}, bf16[2,128,256]{2,1,0:T(8,128)(2,1)S(1)}, u32[]{:S(2)}, u32[]{:S(2)}) %collective-permute-start.15) | collective-permute-done | bytes 131104 | tf_op jit(solution)/shard_map/ppermute | solution.py:36
  189.8 1.2 collective-permute-done.16.refs_4_
  191.0 0.0 collective-permute-done.13.refs_1_
  191.0 1.2 shard_map.85
  (34 shorter events, 0.2 us)
Async XLA Ops:
  3.7 19.4 %copy-start.10 = (s32[2,256]{1,0:T(2,128)S(1)}, s32[2,256]{1,0:T(2,128)}, u32[]{:S(2)}) copy-start(s32[2,256]{1,0:T(2,128)} %param.8) | copy-start | bytes 6148
  3.7 21.0 %copy-start = (bf16[1,2,256,2560]{3,2,1,0:T(8,128)(2,1)S(1)}, bf16[1,2,256,2560]{3,2,1,0:T(8,128)(2,1)}, u32[]{:S(2)}) copy-start(bf16[1,2,256,2560]{3,2,1,0:T(8,128)(2,1)} %param.5) | copy-start | bytes 7864324
  3.7 47.8 %all-to-all-start = ((bf16[16,336,128]{2,1,0:T(8,128)(2,1)}), bf16[16,336,128]{2,1,0:T(8,128)(2,1)}, u32[]{:S(2)}, u32[]{:S(2)}) async-start(bf16[16,336,128]{2,1,0:T(8,128)(2,1)} %shard_map.77), calls=%async_computation | async-start | bytes 2752512 | tf_op jit(solution)/shard_map/all_to_all | solution.py:48
  16.9 24.8 %collective-permute-start = (bf16[256,1024]{1,0:T(8,128)(2,1)}, bf16[256,1024]{1,0:T(8,128)(2,1)}, u32[]{:S(2)}, u32[]{:S(2)}) collective-permute-start(bf16[256,1024]{1,0:T(8,128)(2,1)} %slice_bitcast_fusion), channel_id=1, source_target_pairs={{0,128},{1,129},{2,130},{3,131},{4,132},{5,133},{6,134},{7,135},{8... | collective-permute-start | bytes 1572872 | tf_op jit(solution)/shard_map/ppermute | solution.py:36
  24.7 17.1 %copy-start.1 = (bf16[1,2,256,1024]{3,2,1,0:T(8,128)(2,1)S(1)}, bf16[1,2,256,1024]{3,2,1,0:T(8,128)(2,1)}, u32[]{:S(2)}) copy-start(bf16[1,2,256,1024]{3,2,1,0:T(8,128)(2,1)} %param.7) | copy-start | bytes 3145732
  42.1 6.4 %collective-permute-start.3 = (bf16[256,256]{1,0:T(8,128)(2,1)S(1)}, bf16[256,256]{1,0:T(8,128)(2,1)S(1)}, u32[]{:S(2)}, u32[]{:S(2)}) collective-permute-start(bf16[256,256]{1,0:T(8,128)(2,1)S(1)} %get-tuple-element.29), channel_id=1, source_target_pairs={{0,112},{128,240},{1,113},{129,241},{2,114},{130,242},{3,115},{131... | collective-permute-start | bytes 393224 | tf_op jit(solution)/shard_map/ppermute | solution.py:36
  43.4 6.7 %collective-permute-start.1 = (bf16[256,256]{1,0:T(8,128)(2,1)S(1)}, bf16[256,256]{1,0:T(8,128)(2,1)S(1)}, u32[]{:S(2)}, u32[]{:S(2)}) collective-permute-start(bf16[256,256]{1,0:T(8,128)(2,1)S(1)} %get-tuple-element.27), channel_id=1, source_target_pairs={{0,80},{128,208},{1,81},{129,209},{2,82},{130,210},{3,83},{131,211... | collective-permute-start | bytes 393224 | tf_op jit(solution)/shard_map/ppermute | solution.py:36
  44.7 5.4 %collective-permute-start.2 = (bf16[256,256]{1,0:T(8,128)(2,1)S(1)}, bf16[256,256]{1,0:T(8,128)(2,1)S(1)}, u32[]{:S(2)}, u32[]{:S(2)}) collective-permute-start(bf16[256,256]{1,0:T(8,128)(2,1)S(1)} %get-tuple-element.28), channel_id=1, source_target_pairs={{0,32},{128,160},{1,33},{129,161},{2,34},{130,162},{3,35},{131,163... | collective-permute-start | bytes 393224 | tf_op jit(solution)/shard_map/ppermute | solution.py:36
  50.2 11.0 %collective-permute-start.4 = (bf16[256,256]{1,0:T(8,128)(2,1)S(1)}, bf16[256,256]{1,0:T(8,128)(2,1)S(1)}, u32[]{:S(2)}, u32[]{:S(2)}) collective-permute-start(bf16[256,256]{1,0:T(8,128)(2,1)S(1)} %add_select_fusion.first_ref), channel_id=1, source_target_pairs={{0,16},{32,48},{80,64},{112,96},{128,144},{160,176},{208,192},{240... | collective-permute-start | bytes 393224 | tf_op jit(solution)/shard_map/ppermute | solution.py:36
  51.5 42.8 %all-to-all-start.1 = ((bf16[16,320,128]{2,1,0:T(8,128)(2,1)}), bf16[16,320,128]{2,1,0:T(8,128)(2,1)S(1)}, u32[]{:S(2)}, u32[]{:S(2)}) async-start(bf16[16,320,128]{2,1,0:T(8,128)(2,1)} %shard_map.76), calls=%async_computation.1 | async-start | bytes 2621440 | tf_op jit(solution)/shard_map/all_to_all | solution.py:48
  73.5 0.7 copy-start.2
  74.2 0.6 copy-start.4
  74.8 0.6 copy-start.6
  75.5 0.6 copy-start.8
  94.3 3.9 %copy-start.3 = (f32[256,256]{1,0:T(8,128)S(1)}, f32[256,256]{1,0:T(8,128)}, u32[]{:S(2)}) copy-start(f32[256,256]{1,0:T(8,128)} %copy-done.2) | copy-start | bytes 786436
  94.3 3.9 %copy-start.7 = (f32[16,8,128]{2,1,0:T(8,128)S(1)}, f32[16,8,128]{2,1,0:T(8,128)}, u32[]{:S(2)}) copy-start(f32[16,8,128]{2,1,0:T(8,128)} %copy-done.6) | copy-start | bytes 196612
  94.3 38.2 %all-to-all-start.2 = ((bf16[16,320,128]{2,1,0:T(8,128)(2,1)}), bf16[16,320,128]{2,1,0:T(8,128)(2,1)S(1)}, u32[]{:S(2)}, u32[]{:S(2)}) async-start(bf16[16,320,128]{2,1,0:T(8,128)(2,1)} %get-tuple-element.37), calls=%async_computation.2 | async-start | bytes 2621440 | tf_op jit(solution)/shard_map/all_to_all | solution.py:48
  98.2 0.9 copy-start.5
  99.2 0.8 copy-start.9
  108.5 1.3 collective-permute-start.5
  109.8 4.4 %collective-permute-start.6 = (f32[16,8,128]{2,1,0:T(8,128)S(1)}, f32[16,8,128]{2,1,0:T(8,128)S(1)}, u32[]{:S(2)}, u32[]{:S(2)}) collective-permute-start(f32[16,8,128]{2,1,0:T(8,128)S(1)} %add.99), channel_id=1, source_target_pairs={{0,2},{1,3},{2,0},{3,1},{4,6},{5,7},{6,4},{7,5},{8,10},{9,11},{10,... | collective-permute-start | bytes 196616 | tf_op jit(solution)/shard_map/ppermute | solution.py:44
  114.1 5.9 %collective-permute-start.7 = (f32[16,8,128]{2,1,0:T(8,128)S(1)}, f32[16,8,128]{2,1,0:T(8,128)S(1)}, u32[]{:S(2)}, u32[]{:S(2)}) collective-permute-start(f32[16,8,128]{2,1,0:T(8,128)S(1)} %add.100), channel_id=1, source_target_pairs={{0,4},{1,5},{2,6},{3,7},{4,0},{5,1},{6,2},{7,3},{8,12},{9,13},{10,... | collective-permute-start | bytes 196616 | tf_op jit(solution)/shard_map/ppermute | solution.py:44
  116.5 16.0 %collective-permute-start.9 = (f32[128,256]{1,0:T(8,128)S(1)}, f32[128,256]{1,0:T(8,128)S(1)}, u32[]{:S(2)}, u32[]{:S(2)}) collective-permute-start(f32[128,256]{1,0:T(8,128)S(1)} %dynamic-slice_bitcast_fusion), channel_id=1, source_target_pairs={{0,16},{16,0},{32,48},{48,32},{64,80},{80,64},{96,112},{112,96},{1... | collective-permute-start | bytes 393224 | tf_op jit(solution)/shard_map/ppermute | solution.py:44
  120.0 4.5 %collective-permute-start.8 = (f32[16,8,128]{2,1,0:T(8,128)S(1)}, f32[16,8,128]{2,1,0:T(8,128)S(1)}, u32[]{:S(2)}, u32[]{:S(2)}) collective-permute-start(f32[16,8,128]{2,1,0:T(8,128)S(1)} %add.101), channel_id=1, source_target_pairs={{0,8},{1,9},{2,10},{3,11},{4,12},{5,13},{6,14},{7,15},{8,0},{9,1},... | collective-permute-start | bytes 196616 | tf_op jit(solution)/shard_map/ppermute | solution.py:44
  132.6 45.8 %all-to-all-start.3 = ((bf16[16,336,128]{2,1,0:T(8,128)(2,1)}), bf16[16,336,128]{2,1,0:T(8,128)(2,1)S(1)}, u32[]{:S(2)}, u32[]{:S(2)}) async-start(bf16[16,336,128]{2,1,0:T(8,128)(2,1)} %shard_map.82), calls=%async_computation.3 | async-start | bytes 2752512 | tf_op jit(solution)/shard_map/all_to_all | solution.py:48
  138.0 12.1 %collective-permute-start.10 = (bf16[128,256]{1,0:T(8,128)(2,1)S(1)}, bf16[128,256]{1,0:T(8,128)(2,1)S(1)}, u32[]{:S(2)}, u32[]{:S(2)}) collective-permute-start(bf16[128,256]{1,0:T(8,128)(2,1)S(1)} %fusion.4), channel_id=1, source_target_pairs={{0,128},{16,144},{32,160},{48,176},{64,192},{80,208},{96,224},{112... | collective-permute-start | bytes 196616 | tf_op jit(solution)/shard_map/ppermute | solution.py:44
  144.5 33.6 %collective-permute-start.12 = (bf16[128,256]{1,0:T(8,128)(2,1)S(1)}, bf16[128,256]{1,0:T(8,128)(2,1)S(1)}, u32[]{:S(2)}, u32[]{:S(2)}) collective-permute-start(bf16[128,256]{1,0:T(8,128)(2,1)S(1)} %fusion.4), channel_id=1, source_target_pairs={{0,192},{16,208},{32,224},{48,240},{64,128},{80,144},{96,160},{112... | collective-permute-start | bytes 196616 | tf_op jit(solution)/shard_map/ppermute | solution.py:44
  150.0 28.4 %collective-permute-start.11 = (bf16[128,256]{1,0:T(8,128)(2,1)S(1)}, bf16[128,256]{1,0:T(8,128)(2,1)S(1)}, u32[]{:S(2)}, u32[]{:S(2)}) collective-permute-start(bf16[128,256]{1,0:T(8,128)(2,1)S(1)} %fusion.4), channel_id=1, source_target_pairs={{0,64},{16,80},{32,96},{48,112},{64,0},{80,16},{96,32},{112,48},{1... | collective-permute-start | bytes 196616 | tf_op jit(solution)/shard_map/ppermute | solution.py:44
  178.4 12.6 %collective-permute-start.13 = (bf16[4,128,256]{2,1,0:T(8,128)(2,1)S(1)}, bf16[4,128,256]{2,1,0:T(8,128)(2,1)S(1)}, u32[]{:S(2)}, u32[]{:S(2)}) collective-permute-start(bf16[4,128,256]{2,1,0:T(8,128)(2,1)S(1)} %pad_maximum_fusion.refs_0_), channel_id=1, source_target_pairs={{0,16},{16,32},{32,48},{48,64},{64,80},{80,96},{96,112},{112,0},{1... | collective-permute-start | bytes 786440 | tf_op jit(solution)/shard_map/ppermute | solution.py:36
  180.3 10.7 %collective-permute-start.14 = (bf16[4,128,256]{2,1,0:T(8,128)(2,1)S(1)}, bf16[4,128,256]{2,1,0:T(8,128)(2,1)S(1)}, u32[]{:S(2)}, u32[]{:S(2)}) collective-permute-start(bf16[4,128,256]{2,1,0:T(8,128)(2,1)S(1)} %pad_maximum_fusion.refs_0_), channel_id=1, source_target_pairs={{0,112},{16,0},{32,16},{48,32},{64,48},{80,64},{96,80},{112,96},{1... | collective-permute-start | bytes 786440 | tf_op jit(solution)/shard_map/ppermute | solution.py:36
  181.7 8.1 %collective-permute-start.15 = (bf16[2,128,256]{2,1,0:T(8,128)(2,1)S(1)}, bf16[2,128,256]{2,1,0:T(8,128)(2,1)S(1)}, u32[]{:S(2)}, u32[]{:S(2)}) collective-permute-start(bf16[2,128,256]{2,1,0:T(8,128)(2,1)S(1)} %pad_maximum_fusion.1), channel_id=1, source_target_pairs={{0,32},{16,48},{32,64},{48,80},{64,96},{80,112},{96,0},{112,16},{1... | collective-permute-start | bytes 393224 | tf_op jit(solution)/shard_map/ppermute | solution.py:36
  181.8 9.1 %collective-permute-start.16 = (bf16[2,128,256]{2,1,0:T(8,128)(2,1)S(1)}, bf16[2,128,256]{2,1,0:T(8,128)(2,1)S(1)}, u32[]{:S(2)}, u32[]{:S(2)}) collective-permute-start(bf16[2,128,256]{2,1,0:T(8,128)(2,1)S(1)} %pad_maximum_fusion.1), channel_id=1, source_target_pairs={{0,96},{16,112},{32,0},{48,16},{64,32},{80,48},{96,64},{112,80},{1... | collective-permute-start | bytes 393224 | tf_op jit(solution)/shard_map/ppermute | solution.py:36

commit v6 on v5

--- a/solution.py
+++ b/solution.py
@@ -25,7 +25,7 @@
 UNITS_FLOPS = 40_000_000_000
 ALL_ROOM = 56 * 1024 * 1024
 SOME_ROOM = 12 * 1024 * 1024
-GATHERED = ((0, 4), (1, 5), (7, 3), (2,), (6,))
+GATHERED = ((0, 4), (1, 5), (7, 3), (2, 6))
 
 VMEM = pl.BlockSpec(memory_space=pltpu.VMEM)
 SMEM = pl.BlockSpec(memory_space=pltpu.SMEM)
@@ -151,8 +151,10 @@
         sources, (whole_ref, sems) = refs[: len(GATHERED)], refs[len(GATHERED) :]
         here = me_ref[0]
         copies = []
-        for source, places in zip(sources, GATHERED):
+        for n, (source, places) in enumerate(zip(sources, GATHERED)):
             for i, back in enumerate(places):
+                if n == len(GATHERED) - 1:
+                    back = back + (1 - 2 * i) * 4 * lax.rem(here, 2)
                 for side in range(2):
                     owner = lax.rem(here + RING - back, RING)
                     micro = lax.rem(here // RING + side, 2)
@@ -451,7 +453,8 @@
         cache_part, gains, gain_part,
     )
     halves = cache_part.reshape(2, LENGTH // 2, 2 * HEAD)
-    theirs = swapped(lax.dynamic_index_in_dim(halves, 1 - half, 0, keepdims=False), 1)
+    theirs = lax.dynamic_index_in_dim(halves, 1 - half, 0, keepdims=False)
+    theirs = swapped(theirs.astype(jnp.bfloat16), 1)
     for bit in (1, 2, 4, 8):
         gain_part = gain_part + swapped(gain_part, bit, "dp")
     early_grads = with_gains(early_grads, gain_part)
@@ -461,10 +464,10 @@
     mine = after(mine.astype(jnp.bfloat16), early_grads)
     came = [swapped(mine, bit) for bit in (4, 12, 8)]
     whole = unpack(late_home, True)
-    here = jnp.stack([mine, came[2]])
     both = jnp.stack([mine, came[2], came[0], came[1]])
-    both, here = lax.optimization_barrier((both, here, whole, early_home))[:2]
-    pieces = [both, turned(both, 1), turned(both, -1), turned(here, 2), turned(here, -2)]
+    both = after(both, whole, early_home)
+    inward = [(i, i // RING * RING + (i + 2 - 4 * (i % 2)) % RING) for i in range(SECTIONS)]
+    pieces = [both, turned(both, 1), turned(both, -1), moved(both, inward)]
     cache_grad = cache_whole(me, *pieces)
     layer_out, gain_sum = unpack(early_home, False, whole)
     return (layer_out[None], cache_grad, gain_sum)

time: 193 us -> 192 us (level)
  starting transfers between devices: 63.8 us -> 59 us
  waiting for transfers between devices: 86.9 us -> 90.7 us
    ppermute x9 -> x8, waiting for transfers between devices: 22.9 us -> 27.3 us  [moved(): return lax.ppermute(array, 'section', pairs)]
    ppermute x9 -> x8, starting transfers between devices: 18.7 us -> 14.7 us  [moved(): return lax.ppermute(array, 'section', pairs)]
  transfers between devices with their start and end apart: 21 -> 20, of which waited for: 13 -> 12; matrix products, arithmetic and copies ran while one was open for 2% -> 2% of each run, Pallas kernels for 15% -> 15%
where the time goes in v6:
time: 192 us; the launch traced here: 191 us
  waiting for transfers between devices  90.7 us (47%)
  starting transfers between devices  59 us (31%)
  Pallas kernels  32.6 us (17%)
  local copies, waits for them, and re-layouts  7.61 us (4%)
    ppermute x8, waiting for transfers between devices, swapped(): return lax.ppermute(array, axis, [(i, i ^ bit) for i in range(16)])  38.7 us
    all_to_all x4, starting transfers between devices, exchange(): return lax.all_to_all(array, 'section', 0, 0, tiled=True)  29.7 us
    ppermute x8, waiting for transfers between devices, moved(): return lax.ppermute(array, 'section', pairs)  27.3 us
    all_to_all x4, waiting for transfers between devices, exchange(): return lax.all_to_all(array, 'section', 0, 0, tiled=True)  24.7 us
    pallas_call x2, Pallas kernels, chain(): pl.pallas_call(kernel, out_shape=[jax.ShapeDtypeStruct(*shape) for shape...  20.7 us
    ppermute x8, starting transfers between devices, moved(): return lax.ppermute(array, 'section', pairs)  14.7 us
    ppermute x8, starting transfers between devices, swapped(): return lax.ppermute(array, axis, [(i, i ^ bit) for i in range(16)])  14.6 us
    unnamed x22, local copies, waits for them, and re-layouts  4.37 us
  transfers between devices with their start and end apart: 20, of which 12 were waited for; matrix products, arithmetic and copies ran while one was open for 2% of the time, Pallas kernels for 15%

profile of v6, /device:TPU:8, one launch (start us, length us, event | category | flops | bytes accessed | tf_op | source)
XLA Modules:
  0.0 191.2 jit_solution(6519617421360066154)
XLA Ops:
  0.6 3.0 %shard_map.77 = bf16[16,336,128]{2,1,0:T(8,128)(2,1)} custom-call(f32[1,2560]{1,0:T(1,128)} %refs_0_.1, bf16[2,256,2560]{2,1,0:T(8,128)(2,1)} %bitcast.28), custom_call_target="tpu_custom_call" | custom-call | bytes 2752512 | tf_op jit(solution)/shard_map/pallas_call | solution.py:245
  3.7 0.0 copy-start.10
  3.7 0.0 copy-start
  3.7 11.3 %all-to-all-start = ((bf16[16,336,128]{2,1,0:T(8,128)(2,1)}), bf16[16,336,128]{2,1,0:T(8,128)(2,1)}, u32[]{:S(2)}, u32[]{:S(2)}) async-start(bf16[16,336,128]{2,1,0:T(8,128)(2,1)} %shard_map.77), calls=%async_computation | async-start | bytes 2752512 | tf_op jit(solution)/shard_map/all_to_all | solution.py:48
  15.0 1.9 slice_bitcast_fusion
  16.9 6.1 %collective-permute-start = (bf16[256,1024]{1,0:T(8,128)(2,1)}, bf16[256,1024]{1,0:T(8,128)(2,1)}, u32[]{:S(2)}, u32[]{:S(2)}) collective-permute-start(bf16[256,1024]{1,0:T(8,128)(2,1)} %slice_bitcast_fusion), channel_id=1, source_target_pairs={{0,128},{1,129},{2,130},{3,131},{4,132},{5,133},{6,134},{7,135},{8... | collective-permute-start | bytes 1572872 | tf_op jit(solution)/shard_map/ppermute | solution.py:36
  23.1 0.1 dynamic-slice_bitcast_fusion.2
  23.1 0.1 eq.43
  23.2 0.1 add.88
  23.3 0.1 eq.48
  23.4 0.1 add.93
  23.5 0.9 dynamic-slice_bitcast_fusion
  24.4 0.1 fusion.3.bias_ref
  24.5 0.1 fusion.1.bias_ref
  24.7 0.0 copy-start.1
  24.7 1.6 shard_map.76
  26.2 15.5 %collective-permute-done.across_ref = bf16[256,1024]{1,0:T(8,128)(2,1)} collective-permute-done((bf16[256,1024]{1,0:T(8,128)(2,1)}, bf16[256,1024]{1,0:T(8,128)(2,1)}, u32[]{:S(2)}, u32[]{:S(2)}) %collective-permute-start) | collective-permute-done | bytes 524320 | tf_op jit(solution)/shard_map/ppermute | solution.py:36
  41.7 0.4 shard_map.78
  42.1 1.3 collective-permute-start.3
  43.4 1.3 collective-permute-start.1
  44.7 1.3 collective-permute-start.2
  46.1 2.5 %collective-permute-done.3 = bf16[256,256]{1,0:T(8,128)(2,1)S(1)} collective-permute-done((bf16[256,256]{1,0:T(8,128)(2,1)S(1)}, bf16[256,256]{1,0:T(8,128)(2,1)S(1)}, u32[]{:S(2)}, u32[]{:S(2)}) %collective-permute-start.3) | collective-permute-done | bytes 131104 | tf_op jit(solution)/shard_map/ppermute | solution.py:36
  48.5 1.7 collective-permute-done.1
  50.2 0.0 collective-permute-done.2
  50.2 1.3 collective-permute-start.4
  51.5 0.0 all-to-all-done.saved_ref
  51.5 9.7 %all-to-all-start.1 = ((bf16[16,320,128]{2,1,0:T(8,128)(2,1)}), bf16[16,320,128]{2,1,0:T(8,128)(2,1)S(1)}, u32[]{:S(2)}, u32[]{:S(2)}) async-start(bf16[16,320,128]{2,1,0:T(8,128)(2,1)} %shard_map.76), calls=%async_computation.1 | async-start | bytes 2621440 | tf_op jit(solution)/shard_map/all_to_all | solution.py:48
  61.2 0.0 collective-permute-done.4.second_ref
  61.2 12.3 %shard_map.80 = (bf16[16,320,128]{2,1,0:T(8,128)(2,1)}, f32[256,256]{1,0:T(8,128)S(1)}, f32[16,8,128]{2,1,0:T(8,128)S(1)}, f32[16,8,128]{2,1,0:T(8,128)S(1)}) custom-call(bf16[16,336,128]{2,1,0:T(8,128)(2,1)} %all-to-all-done.saved_ref, bf16[256,256]{1,0:T(8,128)(2,1)S(1)} %shard_map.79.kv_ref, f32[256,320]{1,0:T(8,128)S(1)} %fusion.1.bias_ref, ...), custom_call_target="tpu_custom_call" | custom-call | flops 1677721600 | bytes 6291456 | tf_op jit(solution)/shard_map/pallas_call | solution.py:394
  73.5 0.7 copy-done.2
  74.2 0.7 copy-done.4
  74.9 0.6 copy-done.6
  75.5 0.6 copy-done.8
  76.1 18.2 %all-to-all-done.1.saved_ref = bf16[16,320,128]{2,1,0:T(8,128)(2,1)S(1)} async-done(((bf16[16,320,128]{2,1,0:T(8,128)(2,1)}), bf16[16,320,128]{2,1,0:T(8,128)(2,1)S(1)}, u32[]{:S(2)}, u32[]{:S(2)}) %all-to-all-start.1) | async-done | bytes 1310752 | tf_op jit(solution)/shard_map/all_to_all | solution.py:48
  94.3 3.9 %all-to-all-start.2 = ((bf16[16,320,128]{2,1,0:T(8,128)(2,1)}), bf16[16,320,128]{2,1,0:T(8,128)(2,1)S(1)}, u32[]{:S(2)}, u32[]{:S(2)}) async-start(bf16[16,320,128]{2,1,0:T(8,128)(2,1)} %get-tuple-element.36), calls=%async_computation.2 | async-start | bytes 2621440 | tf_op jit(solution)/shard_map/all_to_all | solution.py:48
  98.3 0.9 copy-done.5
  99.2 0.8 copy-done.9
  100.0 8.5 %shard_map.81 = (bf16[16,336,128]{2,1,0:T(8,128)(2,1)}, f32[256,256]{1,0:T(8,128)S(1)}, f32[16,8,128]{2,1,0:T(8,128)S(1)}) custom-call(bf16[16,320,128]{2,1,0:T(8,128)(2,1)S(1)} %all-to-all-done.1.saved_ref, bf16[256,256]{1,0:T(8,128)(2,1)S(1)} %copy-done.5, f32[128,320]{1,0:T(8,128)S(1)} %fusion.3.bias_ref, bf16[64,640]{1,0:T(8,128)(2,1)S(1)} %get-tuple-element.43.top_ref, ...), custom_call_target="tpu_custom_call" | custom-call | flops 838860800 | bytes 6291456 | tf_op jit(solution)/shard_map/pallas_call | solution.py:394
  108.5 0.0 collective-permute-start.5
  108.5 1.3 collective-permute-done.5
  109.7 0.5 collective-permute-start.6
  110.3 3.8 %collective-permute-done.6 = f32[16,8,128]{2,1,0:T(8,128)S(1)} collective-permute-done((f32[16,8,128]{2,1,0:T(8,128)S(1)}, f32[16,8,128]{2,1,0:T(8,128)S(1)}, u32[]{:S(2)}, u32[]{:S(2)}) %collective-permute-start.6) | collective-permute-done | bytes 65568 | tf_op jit(solution)/shard_map/ppermute | solution.py:44
  114.1 2.4 %collective-permute-start.7 = (f32[16,8,128]{2,1,0:T(8,128)S(1)}, f32[16,8,128]{2,1,0:T(8,128)S(1)}, u32[]{:S(2)}, u32[]{:S(2)}) collective-permute-start(f32[16,8,128]{2,1,0:T(8,128)S(1)} %add.100), channel_id=1, source_target_pairs={{0,4},{1,5},{2,6},{3,7},{4,0},{5,1},{6,2},{7,3},{8,12},{9,13},{10,... | collective-permute-start | bytes 196616 | tf_op jit(solution)/shard_map/ppermute | solution.py:44
  116.5 3.5 %collective-permute-done.7 = f32[16,8,128]{2,1,0:T(8,128)S(1)} collective-permute-done((f32[16,8,128]{2,1,0:T(8,128)S(1)}, f32[16,8,128]{2,1,0:T(8,128)S(1)}, u32[]{:S(2)}, u32[]{:S(2)}) %collective-permute-start.7) | collective-permute-done | bytes 65568 | tf_op jit(solution)/shard_map/ppermute | solution.py:44
  120.0 0.7 collective-permute-start.8
  120.7 2.0 %collective-permute-start.9 = (bf16[128,256]{1,0:T(8,128)(2,1)S(1)}, bf16[128,256]{1,0:T(8,128)(2,1)S(1)}, u32[]{:S(2)}, u32[]{:S(2)}) collective-permute-start(bf16[128,256]{1,0:T(8,128)(2,1)S(1)} %fusion.5), channel_id=1, source_target_pairs={{0,16},{16,0},{32,48},{48,32},{64,80},{80,64},{96,112},{112,96},{1... | collective-permute-start | bytes 196616 | tf_op jit(solution)/shard_map/ppermute | solution.py:44
  122.7 1.8 collective-permute-done.8
  124.5 0.8 shard_map.82
  125.3 6.5 %all-to-all-done.2.came_ref = bf16[16,320,128]{2,1,0:T(8,128)(2,1)S(1)} async-done(((bf16[16,320,128]{2,1,0:T(8,128)(2,1)}), bf16[16,320,128]{2,1,0:T(8,128)(2,1)S(1)}, u32[]{:S(2)}, u32[]{:S(2)}) %all-to-all-start.2) | async-done | bytes 1310752 | tf_op jit(solution)/shard_map/all_to_all | solution.py:48
  131.8 0.0 collective-permute-done.9
  131.8 4.8 %all-to-all-start.3 = ((bf16[16,336,128]{2,1,0:T(8,128)(2,1)}), bf16[16,336,128]{2,1,0:T(8,128)(2,1)S(1)}, u32[]{:S(2)}, u32[]{:S(2)}) async-start(bf16[16,336,128]{2,1,0:T(8,128)(2,1)} %shard_map.82), calls=%async_computation.3 | async-start | bytes 2752512 | tf_op jit(solution)/shard_map/all_to_all | solution.py:48
  136.6 8.3 %collective-permute-start.12 = (bf16[128,256]{1,0:T(8,128)(2,1)S(1)}, bf16[128,256]{1,0:T(8,128)(2,1)S(1)}, u32[]{:S(2)}, u32[]{:S(2)}) collective-permute-start(bf16[128,256]{1,0:T(8,128)(2,1)S(1)} %fusion.4), channel_id=1, source_target_pairs={{0,192},{16,208},{32,224},{48,240},{64,128},{80,144},{96,160},{112... | collective-permute-start | bytes 196616 | tf_op jit(solution)/shard_map/ppermute | solution.py:44
  144.9 0.6 collective-permute-start.11
  145.5 0.1 collective-permute-start.10
  145.6 3.0 %shard_map.83.rest_0_ = bf16[2,256,2560]{2,1,0:T(8,128)(2,1)} custom-call(bf16[16,320,128]{2,1,0:T(8,128)(2,1)S(1)} %all-to-all-done.2.came_ref), custom_call_target="tpu_custom_call" | custom-call | bytes 5242880 | tf_op jit(solution)/shard_map/pallas_call | solution.py:289
  148.6 28.1 %collective-permute-done.12 = bf16[128,256]{1,0:T(8,128)(2,1)S(1)} collective-permute-done((bf16[128,256]{1,0:T(8,128)(2,1)S(1)}, bf16[128,256]{1,0:T(8,128)(2,1)S(1)}, u32[]{:S(2)}, u32[]{:S(2)}) %collective-permute-start.12) | collective-permute-done | bytes 65568 | tf_op jit(solution)/shard_map/ppermute | solution.py:44
  176.7 0.2 collective-permute-done.11
  177.0 0.0 collective-permute-done.10
  177.0 1.9 collective-permute-start.13
  178.9 1.5 collective-permute-start.14
  180.3 0.1 collective-permute-start.15
  180.4 1.8 shard_map.84
  182.2 7.7 %collective-permute-done.13.refs_1_ = bf16[4,128,256]{2,1,0:T(8,128)(2,1)S(1)} collective-permute-done((bf16[4,128,256]{2,1,0:T(8,128)(2,1)S(1)}, bf16[4,128,256]{2,1,0:T(8,128)(2,1)S(1)}, u32[]{:S(2)}, u32[]{:S(2)}) %collective-permute-start.13) | collective-permute-done | bytes 262176 | tf_op jit(solution)/shard_map/ppermute | solution.py:36
  189.9 1.2 shard_map.85
  (31 shorter events, 0.2 us)
Async XLA Ops:
  3.7 19.4 %copy-start.10 = (s32[2,256]{1,0:T(2,128)S(1)}, s32[2,256]{1,0:T(2,128)}, u32[]{:S(2)}) copy-start(s32[2,256]{1,0:T(2,128)} %param.8) | copy-start | bytes 6148
  3.7 21.0 %copy-start = (bf16[1,2,256,2560]{3,2,1,0:T(8,128)(2,1)S(1)}, bf16[1,2,256,2560]{3,2,1,0:T(8,128)(2,1)}, u32[]{:S(2)}) copy-start(bf16[1,2,256,2560]{3,2,1,0:T(8,128)(2,1)} %param.5) | copy-start | bytes 7864324
  3.7 47.8 %all-to-all-start = ((bf16[16,336,128]{2,1,0:T(8,128)(2,1)}), bf16[16,336,128]{2,1,0:T(8,128)(2,1)}, u32[]{:S(2)}, u32[]{:S(2)}) async-start(bf16[16,336,128]{2,1,0:T(8,128)(2,1)} %shard_map.77), calls=%async_computation | async-start | bytes 2752512 | tf_op jit(solution)/shard_map/all_to_all | solution.py:48
  16.9 24.8 %collective-permute-start = (bf16[256,1024]{1,0:T(8,128)(2,1)}, bf16[256,1024]{1,0:T(8,128)(2,1)}, u32[]{:S(2)}, u32[]{:S(2)}) collective-permute-start(bf16[256,1024]{1,0:T(8,128)(2,1)} %slice_bitcast_fusion), channel_id=1, source_target_pairs={{0,128},{1,129},{2,130},{3,131},{4,132},{5,133},{6,134},{7,135},{8... | collective-permute-start | bytes 1572872 | tf_op jit(solution)/shard_map/ppermute | solution.py:36
  24.7 17.1 %copy-start.1 = (bf16[1,2,256,1024]{3,2,1,0:T(8,128)(2,1)S(1)}, bf16[1,2,256,1024]{3,2,1,0:T(8,128)(2,1)}, u32[]{:S(2)}) copy-start(bf16[1,2,256,1024]{3,2,1,0:T(8,128)(2,1)} %param.7) | copy-start | bytes 3145732
  42.1 6.4 %collective-permute-start.3 = (bf16[256,256]{1,0:T(8,128)(2,1)S(1)}, bf16[256,256]{1,0:T(8,128)(2,1)S(1)}, u32[]{:S(2)}, u32[]{:S(2)}) collective-permute-start(bf16[256,256]{1,0:T(8,128)(2,1)S(1)} %get-tuple-element.28), channel_id=1, source_target_pairs={{0,112},{128,240},{1,113},{129,241},{2,114},{130,242},{3,115},{131... | collective-permute-start | bytes 393224 | tf_op jit(solution)/shard_map/ppermute | solution.py:36
  43.4 6.7 %collective-permute-start.1 = (bf16[256,256]{1,0:T(8,128)(2,1)S(1)}, bf16[256,256]{1,0:T(8,128)(2,1)S(1)}, u32[]{:S(2)}, u32[]{:S(2)}) collective-permute-start(bf16[256,256]{1,0:T(8,128)(2,1)S(1)} %get-tuple-element.26), channel_id=1, source_target_pairs={{0,80},{128,208},{1,81},{129,209},{2,82},{130,210},{3,83},{131,211... | collective-permute-start | bytes 393224 | tf_op jit(solution)/shard_map/ppermute | solution.py:36
  44.7 5.4 %collective-permute-start.2 = (bf16[256,256]{1,0:T(8,128)(2,1)S(1)}, bf16[256,256]{1,0:T(8,128)(2,1)S(1)}, u32[]{:S(2)}, u32[]{:S(2)}) collective-permute-start(bf16[256,256]{1,0:T(8,128)(2,1)S(1)} %get-tuple-element.27), channel_id=1, source_target_pairs={{0,32},{128,160},{1,33},{129,161},{2,34},{130,162},{3,35},{131,163... | collective-permute-start | bytes 393224 | tf_op jit(solution)/shard_map/ppermute | solution.py:36
  50.2 11.0 %collective-permute-start.4 = (bf16[256,256]{1,0:T(8,128)(2,1)S(1)}, bf16[256,256]{1,0:T(8,128)(2,1)S(1)}, u32[]{:S(2)}, u32[]{:S(2)}) collective-permute-start(bf16[256,256]{1,0:T(8,128)(2,1)S(1)} %add_select_fusion.first_ref), channel_id=1, source_target_pairs={{0,16},{32,48},{80,64},{112,96},{128,144},{160,176},{208,192},{240... | collective-permute-start | bytes 393224 | tf_op jit(solution)/shard_map/ppermute | solution.py:36
  51.5 42.8 %all-to-all-start.1 = ((bf16[16,320,128]{2,1,0:T(8,128)(2,1)}), bf16[16,320,128]{2,1,0:T(8,128)(2,1)S(1)}, u32[]{:S(2)}, u32[]{:S(2)}) async-start(bf16[16,320,128]{2,1,0:T(8,128)(2,1)} %shard_map.76), calls=%async_computation.1 | async-start | bytes 2621440 | tf_op jit(solution)/shard_map/all_to_all | solution.py:48
  73.5 0.7 copy-start.2
  74.2 0.7 copy-start.4
  74.9 0.6 copy-start.6
  75.5 0.6 copy-start.8
  94.3 3.9 %copy-start.3 = (f32[256,256]{1,0:T(8,128)S(1)}, f32[256,256]{1,0:T(8,128)}, u32[]{:S(2)}) copy-start(f32[256,256]{1,0:T(8,128)} %copy-done.2) | copy-start | bytes 786436
  94.3 3.9 %copy-start.7 = (f32[16,8,128]{2,1,0:T(8,128)S(1)}, f32[16,8,128]{2,1,0:T(8,128)}, u32[]{:S(2)}) copy-start(f32[16,8,128]{2,1,0:T(8,128)} %copy-done.6) | copy-start | bytes 196612
  94.3 37.5 %all-to-all-start.2 = ((bf16[16,320,128]{2,1,0:T(8,128)(2,1)}), bf16[16,320,128]{2,1,0:T(8,128)(2,1)S(1)}, u32[]{:S(2)}, u32[]{:S(2)}) async-start(bf16[16,320,128]{2,1,0:T(8,128)(2,1)} %get-tuple-element.36), calls=%async_computation.2 | async-start | bytes 2621440 | tf_op jit(solution)/shard_map/all_to_all | solution.py:48
  98.2 0.9 copy-start.5
  99.2 0.8 copy-start.9
  108.5 1.3 collective-permute-start.5
  109.7 4.4 %collective-permute-start.6 = (f32[16,8,128]{2,1,0:T(8,128)S(1)}, f32[16,8,128]{2,1,0:T(8,128)S(1)}, u32[]{:S(2)}, u32[]{:S(2)}) collective-permute-start(f32[16,8,128]{2,1,0:T(8,128)S(1)} %add.99), channel_id=1, source_target_pairs={{0,2},{1,3},{2,0},{3,1},{4,6},{5,7},{6,4},{7,5},{8,10},{9,11},{10,... | collective-permute-start | bytes 196616 | tf_op jit(solution)/shard_map/ppermute | solution.py:44
  114.1 5.9 %collective-permute-start.7 = (f32[16,8,128]{2,1,0:T(8,128)S(1)}, f32[16,8,128]{2,1,0:T(8,128)S(1)}, u32[]{:S(2)}, u32[]{:S(2)}) collective-permute-start(f32[16,8,128]{2,1,0:T(8,128)S(1)} %add.100), channel_id=1, source_target_pairs={{0,4},{1,5},{2,6},{3,7},{4,0},{5,1},{6,2},{7,3},{8,12},{9,13},{10,... | collective-permute-start | bytes 196616 | tf_op jit(solution)/shard_map/ppermute | solution.py:44
  120.0 4.5 %collective-permute-start.8 = (f32[16,8,128]{2,1,0:T(8,128)S(1)}, f32[16,8,128]{2,1,0:T(8,128)S(1)}, u32[]{:S(2)}, u32[]{:S(2)}) collective-permute-start(f32[16,8,128]{2,1,0:T(8,128)S(1)} %add.101), channel_id=1, source_target_pairs={{0,8},{1,9},{2,10},{3,11},{4,12},{5,13},{6,14},{7,15},{8,0},{9,1},... | collective-permute-start | bytes 196616 | tf_op jit(solution)/shard_map/ppermute | solution.py:44
  120.7 11.1 %collective-permute-start.9 = (bf16[128,256]{1,0:T(8,128)(2,1)S(1)}, bf16[128,256]{1,0:T(8,128)(2,1)S(1)}, u32[]{:S(2)}, u32[]{:S(2)}) collective-permute-start(bf16[128,256]{1,0:T(8,128)(2,1)S(1)} %fusion.5), channel_id=1, source_target_pairs={{0,16},{16,0},{32,48},{48,32},{64,80},{80,64},{96,112},{112,96},{1... | collective-permute-start | bytes 196616 | tf_op jit(solution)/shard_map/ppermute | solution.py:44
  131.8 45.2 %all-to-all-start.3 = ((bf16[16,336,128]{2,1,0:T(8,128)(2,1)}), bf16[16,336,128]{2,1,0:T(8,128)(2,1)S(1)}, u32[]{:S(2)}, u32[]{:S(2)}) async-start(bf16[16,336,128]{2,1,0:T(8,128)(2,1)} %shard_map.82), calls=%async_computation.3 | async-start | bytes 2752512 | tf_op jit(solution)/shard_map/all_to_all | solution.py:48
  136.6 40.1 %collective-permute-start.12 = (bf16[128,256]{1,0:T(8,128)(2,1)S(1)}, bf16[128,256]{1,0:T(8,128)(2,1)S(1)}, u32[]{:S(2)}, u32[]{:S(2)}) collective-permute-start(bf16[128,256]{1,0:T(8,128)(2,1)S(1)} %fusion.4), channel_id=1, source_target_pairs={{0,192},{16,208},{32,224},{48,240},{64,128},{80,144},{96,160},{112... | collective-permute-start | bytes 196616 | tf_op jit(solution)/shard_map/ppermute | solution.py:44
  144.9 32.0 %collective-permute-start.11 = (bf16[128,256]{1,0:T(8,128)(2,1)S(1)}, bf16[128,256]{1,0:T(8,128)(2,1)S(1)}, u32[]{:S(2)}, u32[]{:S(2)}) collective-permute-start(bf16[128,256]{1,0:T(8,128)(2,1)S(1)} %fusion.4), channel_id=1, source_target_pairs={{0,64},{16,80},{32,96},{48,112},{64,0},{80,16},{96,32},{112,48},{1... | collective-permute-start | bytes 196616 | tf_op jit(solution)/shard_map/ppermute | solution.py:44
  145.5 31.5 %collective-permute-start.10 = (bf16[128,256]{1,0:T(8,128)(2,1)S(1)}, bf16[128,256]{1,0:T(8,128)(2,1)S(1)}, u32[]{:S(2)}, u32[]{:S(2)}) collective-permute-start(bf16[128,256]{1,0:T(8,128)(2,1)S(1)} %fusion.4), channel_id=1, source_target_pairs={{0,128},{16,144},{32,160},{48,176},{64,192},{80,208},{96,224},{112... | collective-permute-start | bytes 196616 | tf_op jit(solution)/shard_map/ppermute | solution.py:44
  177.0 12.9 %collective-permute-start.13 = (bf16[4,128,256]{2,1,0:T(8,128)(2,1)S(1)}, bf16[4,128,256]{2,1,0:T(8,128)(2,1)S(1)}, u32[]{:S(2)}, u32[]{:S(2)}) collective-permute-start(bf16[4,128,256]{2,1,0:T(8,128)(2,1)S(1)} %pad_maximum_fusion.refs_0_), channel_id=1, source_target_pairs={{0,16},{16,32},{32,48},{48,64},{64,80},{80,96},{96,112},{112,0},{1... | collective-permute-start | bytes 786440 | tf_op jit(solution)/shard_map/ppermute | solution.py:36
  178.9 11.1 %collective-permute-start.14 = (bf16[4,128,256]{2,1,0:T(8,128)(2,1)S(1)}, bf16[4,128,256]{2,1,0:T(8,128)(2,1)S(1)}, u32[]{:S(2)}, u32[]{:S(2)}) collective-permute-start(bf16[4,128,256]{2,1,0:T(8,128)(2,1)S(1)} %pad_maximum_fusion.refs_0_), channel_id=1, source_target_pairs={{0,112},{16,0},{32,16},{48,32},{64,48},{80,64},{96,80},{112,96},{1... | collective-permute-start | bytes 786440 | tf_op jit(solution)/shard_map/ppermute | solution.py:36
  180.3 9.6 %collective-permute-start.15 = (bf16[4,128,256]{2,1,0:T(8,128)(2,1)S(1)}, bf16[4,128,256]{2,1,0:T(8,128)(2,1)S(1)}, u32[]{:S(2)}, u32[]{:S(2)}) collective-permute-start(bf16[4,128,256]{2,1,0:T(8,128)(2,1)S(1)} %pad_maximum_fusion.refs_0_), channel_id=1, source_target_pairs={{0,32},{16,112},{32,64},{48,16},{64,96},{80,48},{96,0},{112,80},{1... | collective-permute-start | bytes 786440 | tf_op jit(solution)/shard_map/ppermute | solution.py:36

commit v7 on v6

--- a/solution.py
+++ b/solution.py
@@ -459,7 +459,7 @@
         gain_part = gain_part + swapped(gain_part, bit, "dp")
     early_grads = with_gains(early_grads, gain_part)
 
-    early_home = exchange(after(early_grads, late_home, theirs))
+    early_home = exchange(after(early_grads, late_home))
     mine = lax.dynamic_index_in_dim(halves, half, 0, keepdims=False) + theirs
     mine = after(mine.astype(jnp.bfloat16), early_grads)
     came = [swapped(mine, bit) for bit in (4, 12, 8)]

time: 192 us -> 198 us (1.031)
  waiting for transfers between devices: 90.7 us -> 98 us
    ppermute x8, waiting for transfers between devices: 38.7 us -> 46.4 us  [swapped(): return lax.ppermute(array, axis, [(i, i ^ bit) for i in range(16)])]
  transfers between devices with their start and end apart: 20 -> 20, of which waited for: 12 -> 12; matrix products, arithmetic and copies ran while one was open for 2% -> 2% of each run, Pallas kernels for 15% -> 14%
where the time goes in v7:
time: 198 us; the launch traced here: 197 us
  waiting for transfers between devices  98 us (49%)
  starting transfers between devices  58 us (29%)
  Pallas kernels  32.6 us (16%)
  local copies, waits for them, and re-layouts  7.62 us (4%)
    ppermute x8, waiting for transfers between devices, swapped(): return lax.ppermute(array, axis, [(i, i ^ bit) for i in range(16)])  46.4 us
    all_to_all x4, starting transfers between devices, exchange(): return lax.all_to_all(array, 'section', 0, 0, tiled=True)  28.8 us
    ppermute x8, waiting for transfers between devices, moved(): return lax.ppermute(array, 'section', pairs)  27.3 us
    all_to_all x4, waiting for transfers between devices, exchange(): return lax.all_to_all(array, 'section', 0, 0, tiled=True)  24.2 us
    pallas_call x2, Pallas kernels, chain(): pl.pallas_call(kernel, out_shape=[jax.ShapeDtypeStruct(*shape) for shape...  20.7 us
    ppermute x8, starting transfers between devices, moved(): return lax.ppermute(array, 'section', pairs)  14.6 us
    ppermute x8, starting transfers between devices, swapped(): return lax.ppermute(array, axis, [(i, i ^ bit) for i in range(16)])  14.6 us
    unnamed x22, local copies, waits for them, and re-layouts  4.37 us
  transfers between devices with their start and end apart: 20, of which 12 were waited for; matrix products, arithmetic and copies ran while one was open for 2% of the time, Pallas kernels for 14%

profile of v7, /device:TPU:8, one launch (start us, length us, event | category | flops | bytes accessed | tf_op | source)
XLA Modules:
  0.0 197.4 jit_solution(18307855993911367030)
XLA Ops:
  0.6 3.0 %shard_map.77 = bf16[16,336,128]{2,1,0:T(8,128)(2,1)} custom-call(f32[1,2560]{1,0:T(1,128)} %refs_0_.1, bf16[2,256,2560]{2,1,0:T(8,128)(2,1)} %bitcast.28), custom_call_target="tpu_custom_call" | custom-call | bytes 2752512 | tf_op jit(solution)/shard_map/pallas_call | solution.py:245
  3.7 0.0 copy-start.10
  3.7 0.0 copy-start
  3.7 11.3 %all-to-all-start = ((bf16[16,336,128]{2,1,0:T(8,128)(2,1)}), bf16[16,336,128]{2,1,0:T(8,128)(2,1)}, u32[]{:S(2)}, u32[]{:S(2)}) async-start(bf16[16,336,128]{2,1,0:T(8,128)(2,1)} %shard_map.77), calls=%async_computation | async-start | bytes 2752512 | tf_op jit(solution)/shard_map/all_to_all | solution.py:48
  15.0 1.9 slice_bitcast_fusion
  16.9 6.1 %collective-permute-start = (bf16[256,1024]{1,0:T(8,128)(2,1)}, bf16[256,1024]{1,0:T(8,128)(2,1)}, u32[]{:S(2)}, u32[]{:S(2)}) collective-permute-start(bf16[256,1024]{1,0:T(8,128)(2,1)} %slice_bitcast_fusion), channel_id=1, source_target_pairs={{0,128},{1,129},{2,130},{3,131},{4,132},{5,133},{6,134},{7,135},{8... | collective-permute-start | bytes 1572872 | tf_op jit(solution)/shard_map/ppermute | solution.py:36
  23.1 0.1 dynamic-slice_bitcast_fusion.2
  23.1 0.1 eq.43
  23.2 0.1 add.88
  23.3 0.1 eq.48
  23.4 0.1 add.93
  23.5 0.9 dynamic-slice_bitcast_fusion
  24.4 0.1 fusion.3.bias_ref
  24.5 0.1 fusion.1.bias_ref
  24.7 0.0 copy-start.1
  24.7 1.6 shard_map.76
  26.2 15.5 %collective-permute-done.across_ref = bf16[256,1024]{1,0:T(8,128)(2,1)} collective-permute-done((bf16[256,1024]{1,0:T(8,128)(2,1)}, bf16[256,1024]{1,0:T(8,128)(2,1)}, u32[]{:S(2)}, u32[]{:S(2)}) %collective-permute-start) | collective-permute-done | bytes 524320 | tf_op jit(solution)/shard_map/ppermute | solution.py:36
  41.7 0.4 shard_map.78
  42.1 1.3 collective-permute-start.3
  43.4 1.3 collective-permute-start.1
  44.7 1.3 collective-permute-start.2
  46.1 2.5 %collective-permute-done.3 = bf16[256,256]{1,0:T(8,128)(2,1)S(1)} collective-permute-done((bf16[256,256]{1,0:T(8,128)(2,1)S(1)}, bf16[256,256]{1,0:T(8,128)(2,1)S(1)}, u32[]{:S(2)}, u32[]{:S(2)}) %collective-permute-start.3) | collective-permute-done | bytes 131104 | tf_op jit(solution)/shard_map/ppermute | solution.py:36
  48.5 1.7 collective-permute-done.1
  50.2 0.0 collective-permute-done.2
  50.2 1.3 collective-permute-start.4
  51.5 0.0 all-to-all-done.saved_ref
  51.5 9.7 %all-to-all-start.1 = ((bf16[16,320,128]{2,1,0:T(8,128)(2,1)}), bf16[16,320,128]{2,1,0:T(8,128)(2,1)S(1)}, u32[]{:S(2)}, u32[]{:S(2)}) async-start(bf16[16,320,128]{2,1,0:T(8,128)(2,1)} %shard_map.76), calls=%async_computation.1 | async-start | bytes 2621440 | tf_op jit(solution)/shard_map/all_to_all | solution.py:48
  61.2 0.0 collective-permute-done.4.second_ref
  61.2 12.3 %shard_map.80 = (bf16[16,320,128]{2,1,0:T(8,128)(2,1)}, f32[256,256]{1,0:T(8,128)S(1)}, f32[16,8,128]{2,1,0:T(8,128)S(1)}, f32[16,8,128]{2,1,0:T(8,128)S(1)}) custom-call(bf16[16,336,128]{2,1,0:T(8,128)(2,1)} %all-to-all-done.saved_ref, bf16[256,256]{1,0:T(8,128)(2,1)S(1)} %shard_map.79.kv_ref, f32[256,320]{1,0:T(8,128)S(1)} %fusion.1.bias_ref, ...), custom_call_target="tpu_custom_call" | custom-call | flops 1677721600 | bytes 6291456 | tf_op jit(solution)/shard_map/pallas_call | solution.py:394
  73.5 0.7 copy-done.2
  74.2 0.7 copy-done.4
  74.9 0.6 copy-done.6
  75.5 0.6 copy-done.8
  76.1 18.2 %all-to-all-done.1.saved_ref = bf16[16,320,128]{2,1,0:T(8,128)(2,1)S(1)} async-done(((bf16[16,320,128]{2,1,0:T(8,128)(2,1)}), bf16[16,320,128]{2,1,0:T(8,128)(2,1)S(1)}, u32[]{:S(2)}, u32[]{:S(2)}) %all-to-all-start.1) | async-done | bytes 1310752 | tf_op jit(solution)/shard_map/all_to_all | solution.py:48
  94.3 3.9 %all-to-all-start.2 = ((bf16[16,320,128]{2,1,0:T(8,128)(2,1)}), bf16[16,320,128]{2,1,0:T(8,128)(2,1)S(1)}, u32[]{:S(2)}, u32[]{:S(2)}) async-start(bf16[16,320,128]{2,1,0:T(8,128)(2,1)} %get-tuple-element.36), calls=%async_computation.2 | async-start | bytes 2621440 | tf_op jit(solution)/shard_map/all_to_all | solution.py:48
  98.3 0.9 copy-done.5
  99.2 0.8 copy-done.9
  100.0 8.5 %shard_map.81 = (bf16[16,336,128]{2,1,0:T(8,128)(2,1)}, f32[256,256]{1,0:T(8,128)S(1)}, f32[16,8,128]{2,1,0:T(8,128)S(1)}) custom-call(bf16[16,320,128]{2,1,0:T(8,128)(2,1)S(1)} %all-to-all-done.1.saved_ref, bf16[256,256]{1,0:T(8,128)(2,1)S(1)} %copy-done.5, f32[128,320]{1,0:T(8,128)S(1)} %fusion.3.bias_ref, bf16[64,640]{1,0:T(8,128)(2,1)S(1)} %get-tuple-element.43.top_ref, ...), custom_call_target="tpu_custom_call" | custom-call | flops 838860800 | bytes 6291456 | tf_op jit(solution)/shard_map/pallas_call | solution.py:394
  108.5 1.3 collective-permute-done.5
  109.7 0.5 collective-permute-start.6
  110.3 3.8 %collective-permute-done.6 = f32[16,8,128]{2,1,0:T(8,128)S(1)} collective-permute-done((f32[16,8,128]{2,1,0:T(8,128)S(1)}, f32[16,8,128]{2,1,0:T(8,128)S(1)}, u32[]{:S(2)}, u32[]{:S(2)}) %collective-permute-start.6) | collective-permute-done | bytes 65568 | tf_op jit(solution)/shard_map/ppermute | solution.py:44
  114.1 2.4 %collective-permute-start.7 = (f32[16,8,128]{2,1,0:T(8,128)S(1)}, f32[16,8,128]{2,1,0:T(8,128)S(1)}, u32[]{:S(2)}, u32[]{:S(2)}) collective-permute-start(f32[16,8,128]{2,1,0:T(8,128)S(1)} %add.100), channel_id=1, source_target_pairs={{0,4},{1,5},{2,6},{3,7},{4,0},{5,1},{6,2},{7,3},{8,12},{9,13},{10,... | collective-permute-start | bytes 196616 | tf_op jit(solution)/shard_map/ppermute | solution.py:44
  116.5 3.5 %collective-permute-done.7 = f32[16,8,128]{2,1,0:T(8,128)S(1)} collective-permute-done((f32[16,8,128]{2,1,0:T(8,128)S(1)}, f32[16,8,128]{2,1,0:T(8,128)S(1)}, u32[]{:S(2)}, u32[]{:S(2)}) %collective-permute-start.7) | collective-permute-done | bytes 65568 | tf_op jit(solution)/shard_map/ppermute | solution.py:44
  120.0 0.7 collective-permute-start.8
  120.7 3.8 %collective-permute-done.8 = f32[16,8,128]{2,1,0:T(8,128)S(1)} collective-permute-done((f32[16,8,128]{2,1,0:T(8,128)S(1)}, f32[16,8,128]{2,1,0:T(8,128)S(1)}, u32[]{:S(2)}, u32[]{:S(2)}) %collective-permute-start.8) | collective-permute-done | bytes 65568 | tf_op jit(solution)/shard_map/ppermute | solution.py:44
  124.5 0.8 shard_map.82
  125.3 6.1 %all-to-all-done.2.came_ref = bf16[16,320,128]{2,1,0:T(8,128)(2,1)S(1)} async-done(((bf16[16,320,128]{2,1,0:T(8,128)(2,1)}), bf16[16,320,128]{2,1,0:T(8,128)(2,1)S(1)}, u32[]{:S(2)}, u32[]{:S(2)}) %all-to-all-start.2) | async-done | bytes 1310752 | tf_op jit(solution)/shard_map/all_to_all | solution.py:48
  131.3 3.8 %all-to-all-start.3 = ((bf16[16,336,128]{2,1,0:T(8,128)(2,1)}), bf16[16,336,128]{2,1,0:T(8,128)(2,1)S(1)}, u32[]{:S(2)}, u32[]{:S(2)}) async-start(bf16[16,336,128]{2,1,0:T(8,128)(2,1)} %shard_map.82), calls=%async_computation.3 | async-start | bytes 2752512 | tf_op jit(solution)/shard_map/all_to_all | solution.py:48
  135.2 2.0 %collective-permute-start.9 = (bf16[128,256]{1,0:T(8,128)(2,1)S(1)}, bf16[128,256]{1,0:T(8,128)(2,1)S(1)}, u32[]{:S(2)}, u32[]{:S(2)}) collective-permute-start(bf16[128,256]{1,0:T(8,128)(2,1)S(1)} %fusion.5), channel_id=1, source_target_pairs={{0,16},{16,0},{32,48},{48,32},{64,80},{80,64},{96,112},{112,96},{1... | collective-permute-start | bytes 196616 | tf_op jit(solution)/shard_map/ppermute | solution.py:44
  137.2 29.5 %collective-permute-done.9 = bf16[128,256]{1,0:T(8,128)(2,1)S(1)} collective-permute-done((bf16[128,256]{1,0:T(8,128)(2,1)S(1)}, bf16[128,256]{1,0:T(8,128)(2,1)S(1)}, u32[]{:S(2)}, u32[]{:S(2)}) %collective-permute-start.9) | collective-permute-done | bytes 65568 | tf_op jit(solution)/shard_map/ppermute | solution.py:44
  166.8 7.0 %collective-permute-start.12 = (bf16[128,256]{1,0:T(8,128)(2,1)S(1)}, bf16[128,256]{1,0:T(8,128)(2,1)S(1)}, u32[]{:S(2)}, u32[]{:S(2)}) collective-permute-start(bf16[128,256]{1,0:T(8,128)(2,1)S(1)} %fusion.4), channel_id=1, source_target_pairs={{0,192},{16,208},{32,224},{48,240},{64,128},{80,144},{96,160},{112... | collective-permute-start | bytes 196616 | tf_op jit(solution)/shard_map/ppermute | solution.py:44
  173.7 1.5 collective-permute-start.11
  175.2 0.6 collective-permute-start.10
  175.7 3.0 %shard_map.83.rest_0_ = bf16[2,256,2560]{2,1,0:T(8,128)(2,1)} custom-call(bf16[16,320,128]{2,1,0:T(8,128)(2,1)S(1)} %all-to-all-done.2.came_ref), custom_call_target="tpu_custom_call" | custom-call | bytes 5242880 | tf_op jit(solution)/shard_map/pallas_call | solution.py:289
  178.8 0.0 collective-permute-done.12
  178.8 4.6 %collective-permute-done.11 = bf16[128,256]{1,0:T(8,128)(2,1)S(1)} collective-permute-done((bf16[128,256]{1,0:T(8,128)(2,1)S(1)}, bf16[128,256]{1,0:T(8,128)(2,1)S(1)}, u32[]{:S(2)}, u32[]{:S(2)}) %collective-permute-start.11) | collective-permute-done | bytes 65568 | tf_op jit(solution)/shard_map/ppermute | solution.py:44
  183.3 0.0 collective-permute-done.10
  183.4 0.0 all-to-all-done.3.came_ref
  183.4 0.3 collective-permute-start.13
  183.7 3.0 %collective-permute-start.14 = (bf16[4,128,256]{2,1,0:T(8,128)(2,1)S(1)}, bf16[4,128,256]{2,1,0:T(8,128)(2,1)S(1)}, u32[]{:S(2)}, u32[]{:S(2)}) collective-permute-start(bf16[4,128,256]{2,1,0:T(8,128)(2,1)S(1)} %pad_maximum_fusion.refs_0_), channel_id=1, source_target_pairs={{0,112},{16,0},{32,16},{48,32},{64,48},{80,64},{96,80},{112,96},{1... | collective-permute-start | bytes 786440 | tf_op jit(solution)/shard_map/ppermute | solution.py:36
  186.7 0.0 collective-permute-start.15
  186.7 1.8 shard_map.84
  188.5 7.7 %collective-permute-done.13.refs_1_ = bf16[4,128,256]{2,1,0:T(8,128)(2,1)S(1)} collective-permute-done((bf16[4,128,256]{2,1,0:T(8,128)(2,1)S(1)}, bf16[4,128,256]{2,1,0:T(8,128)(2,1)S(1)}, u32[]{:S(2)}, u32[]{:S(2)}) %collective-permute-start.13) | collective-permute-done | bytes 262176 | tf_op jit(solution)/shard_map/ppermute | solution.py:36
  196.2 1.2 shard_map.85
  (31 shorter events, 0.2 us)
Async XLA Ops:
  3.7 19.4 %copy-start.10 = (s32[2,256]{1,0:T(2,128)S(1)}, s32[2,256]{1,0:T(2,128)}, u32[]{:S(2)}) copy-start(s32[2,256]{1,0:T(2,128)} %param.8) | copy-start | bytes 6148
  3.7 21.0 %copy-start = (bf16[1,2,256,2560]{3,2,1,0:T(8,128)(2,1)S(1)}, bf16[1,2,256,2560]{3,2,1,0:T(8,128)(2,1)}, u32[]{:S(2)}) copy-start(bf16[1,2,256,2560]{3,2,1,0:T(8,128)(2,1)} %param.5) | copy-start | bytes 7864324
  3.7 47.8 %all-to-all-start = ((bf16[16,336,128]{2,1,0:T(8,128)(2,1)}), bf16[16,336,128]{2,1,0:T(8,128)(2,1)}, u32[]{:S(2)}, u32[]{:S(2)}) async-start(bf16[16,336,128]{2,1,0:T(8,128)(2,1)} %shard_map.77), calls=%async_computation | async-start | bytes 2752512 | tf_op jit(solution)/shard_map/all_to_all | solution.py:48
  16.9 24.8 %collective-permute-start = (bf16[256,1024]{1,0:T(8,128)(2,1)}, bf16[256,1024]{1,0:T(8,128)(2,1)}, u32[]{:S(2)}, u32[]{:S(2)}) collective-permute-start(bf16[256,1024]{1,0:T(8,128)(2,1)} %slice_bitcast_fusion), channel_id=1, source_target_pairs={{0,128},{1,129},{2,130},{3,131},{4,132},{5,133},{6,134},{7,135},{8... | collective-permute-start | bytes 1572872 | tf_op jit(solution)/shard_map/ppermute | solution.py:36
  24.7 17.1 %copy-start.1 = (bf16[1,2,256,1024]{3,2,1,0:T(8,128)(2,1)S(1)}, bf16[1,2,256,1024]{3,2,1,0:T(8,128)(2,1)}, u32[]{:S(2)}) copy-start(bf16[1,2,256,1024]{3,2,1,0:T(8,128)(2,1)} %param.7) | copy-start | bytes 3145732
  42.1 6.4 %collective-permute-start.3 = (bf16[256,256]{1,0:T(8,128)(2,1)S(1)}, bf16[256,256]{1,0:T(8,128)(2,1)S(1)}, u32[]{:S(2)}, u32[]{:S(2)}) collective-permute-start(bf16[256,256]{1,0:T(8,128)(2,1)S(1)} %get-tuple-element.28), channel_id=1, source_target_pairs={{0,112},{128,240},{1,113},{129,241},{2,114},{130,242},{3,115},{131... | collective-permute-start | bytes 393224 | tf_op jit(solution)/shard_map/ppermute | solution.py:36
  43.4 6.7 %collective-permute-start.1 = (bf16[256,256]{1,0:T(8,128)(2,1)S(1)}, bf16[256,256]{1,0:T(8,128)(2,1)S(1)}, u32[]{:S(2)}, u32[]{:S(2)}) collective-permute-start(bf16[256,256]{1,0:T(8,128)(2,1)S(1)} %get-tuple-element.26), channel_id=1, source_target_pairs={{0,80},{128,208},{1,81},{129,209},{2,82},{130,210},{3,83},{131,211... | collective-permute-start | bytes 393224 | tf_op jit(solution)/shard_map/ppermute | solution.py:36
  44.7 5.4 %collective-permute-start.2 = (bf16[256,256]{1,0:T(8,128)(2,1)S(1)}, bf16[256,256]{1,0:T(8,128)(2,1)S(1)}, u32[]{:S(2)}, u32[]{:S(2)}) collective-permute-start(bf16[256,256]{1,0:T(8,128)(2,1)S(1)} %get-tuple-element.27), channel_id=1, source_target_pairs={{0,32},{128,160},{1,33},{129,161},{2,34},{130,162},{3,35},{131,163... | collective-permute-start | bytes 393224 | tf_op jit(solution)/shard_map/ppermute | solution.py:36
  50.2 11.0 %collective-permute-start.4 = (bf16[256,256]{1,0:T(8,128)(2,1)S(1)}, bf16[256,256]{1,0:T(8,128)(2,1)S(1)}, u32[]{:S(2)}, u32[]{:S(2)}) collective-permute-start(bf16[256,256]{1,0:T(8,128)(2,1)S(1)} %add_select_fusion.first_ref), channel_id=1, source_target_pairs={{0,16},{32,48},{80,64},{112,96},{128,144},{160,176},{208,192},{240... | collective-permute-start | bytes 393224 | tf_op jit(solution)/shard_map/ppermute | solution.py:36
  51.5 42.8 %all-to-all-start.1 = ((bf16[16,320,128]{2,1,0:T(8,128)(2,1)}), bf16[16,320,128]{2,1,0:T(8,128)(2,1)S(1)}, u32[]{:S(2)}, u32[]{:S(2)}) async-start(bf16[16,320,128]{2,1,0:T(8,128)(2,1)} %shard_map.76), calls=%async_computation.1 | async-start | bytes 2621440 | tf_op jit(solution)/shard_map/all_to_all | solution.py:48
  73.5 0.7 copy-start.2
  74.2 0.7 copy-start.4
  74.9 0.6 copy-start.6
  75.5 0.6 copy-start.8
  94.3 3.9 %copy-start.3 = (f32[256,256]{1,0:T(8,128)S(1)}, f32[256,256]{1,0:T(8,128)}, u32[]{:S(2)}) copy-start(f32[256,256]{1,0:T(8,128)} %copy-done.2) | copy-start | bytes 786436
  94.3 3.9 %copy-start.7 = (f32[16,8,128]{2,1,0:T(8,128)S(1)}, f32[16,8,128]{2,1,0:T(8,128)}, u32[]{:S(2)}) copy-start(f32[16,8,128]{2,1,0:T(8,128)} %copy-done.6) | copy-start | bytes 196612
  94.3 37.0 %all-to-all-start.2 = ((bf16[16,320,128]{2,1,0:T(8,128)(2,1)}), bf16[16,320,128]{2,1,0:T(8,128)(2,1)S(1)}, u32[]{:S(2)}, u32[]{:S(2)}) async-start(bf16[16,320,128]{2,1,0:T(8,128)(2,1)} %get-tuple-element.36), calls=%async_computation.2 | async-start | bytes 2621440 | tf_op jit(solution)/shard_map/all_to_all | solution.py:48
  98.2 0.9 copy-start.5
  99.2 0.8 copy-start.9
  108.5 1.3 collective-permute-start.5
  109.7 4.4 %collective-permute-start.6 = (f32[16,8,128]{2,1,0:T(8,128)S(1)}, f32[16,8,128]{2,1,0:T(8,128)S(1)}, u32[]{:S(2)}, u32[]{:S(2)}) collective-permute-start(f32[16,8,128]{2,1,0:T(8,128)S(1)} %add.99), channel_id=1, source_target_pairs={{0,2},{1,3},{2,0},{3,1},{4,6},{5,7},{6,4},{7,5},{8,10},{9,11},{10,... | collective-permute-start | bytes 196616 | tf_op jit(solution)/shard_map/ppermute | solution.py:44
  114.1 5.9 %collective-permute-start.7 = (f32[16,8,128]{2,1,0:T(8,128)S(1)}, f32[16,8,128]{2,1,0:T(8,128)S(1)}, u32[]{:S(2)}, u32[]{:S(2)}) collective-permute-start(f32[16,8,128]{2,1,0:T(8,128)S(1)} %add.100), channel_id=1, source_target_pairs={{0,4},{1,5},{2,6},{3,7},{4,0},{5,1},{6,2},{7,3},{8,12},{9,13},{10,... | collective-permute-start | bytes 196616 | tf_op jit(solution)/shard_map/ppermute | solution.py:44
  120.0 4.5 %collective-permute-start.8 = (f32[16,8,128]{2,1,0:T(8,128)S(1)}, f32[16,8,128]{2,1,0:T(8,128)S(1)}, u32[]{:S(2)}, u32[]{:S(2)}) collective-permute-start(f32[16,8,128]{2,1,0:T(8,128)S(1)} %add.101), channel_id=1, source_target_pairs={{0,8},{1,9},{2,10},{3,11},{4,12},{5,13},{6,14},{7,15},{8,0},{9,1},... | collective-permute-start | bytes 196616 | tf_op jit(solution)/shard_map/ppermute | solution.py:44
  131.3 52.0 %all-to-all-start.3 = ((bf16[16,336,128]{2,1,0:T(8,128)(2,1)}), bf16[16,336,128]{2,1,0:T(8,128)(2,1)S(1)}, u32[]{:S(2)}, u32[]{:S(2)}) async-start(bf16[16,336,128]{2,1,0:T(8,128)(2,1)} %shard_map.82), calls=%async_computation.3 | async-start | bytes 2752512 | tf_op jit(solution)/shard_map/all_to_all | solution.py:48
  135.2 31.5 %collective-permute-start.9 = (bf16[128,256]{1,0:T(8,128)(2,1)S(1)}, bf16[128,256]{1,0:T(8,128)(2,1)S(1)}, u32[]{:S(2)}, u32[]{:S(2)}) collective-permute-start(bf16[128,256]{1,0:T(8,128)(2,1)S(1)} %fusion.5), channel_id=1, source_target_pairs={{0,16},{16,0},{32,48},{48,32},{64,80},{80,64},{96,112},{112,96},{1... | collective-permute-start | bytes 196616 | tf_op jit(solution)/shard_map/ppermute | solution.py:44
  166.8 12.0 %collective-permute-start.12 = (bf16[128,256]{1,0:T(8,128)(2,1)S(1)}, bf16[128,256]{1,0:T(8,128)(2,1)S(1)}, u32[]{:S(2)}, u32[]{:S(2)}) collective-permute-start(bf16[128,256]{1,0:T(8,128)(2,1)S(1)} %fusion.4), channel_id=1, source_target_pairs={{0,192},{16,208},{32,224},{48,240},{64,128},{80,144},{96,160},{112... | collective-permute-start | bytes 196616 | tf_op jit(solution)/shard_map/ppermute | solution.py:44
  173.7 9.6 %collective-permute-start.11 = (bf16[128,256]{1,0:T(8,128)(2,1)S(1)}, bf16[128,256]{1,0:T(8,128)(2,1)S(1)}, u32[]{:S(2)}, u32[]{:S(2)}) collective-permute-start(bf16[128,256]{1,0:T(8,128)(2,1)S(1)} %fusion.4), channel_id=1, source_target_pairs={{0,64},{16,80},{32,96},{48,112},{64,0},{80,16},{96,32},{112,48},{1... | collective-permute-start | bytes 196616 | tf_op jit(solution)/shard_map/ppermute | solution.py:44
  175.2 8.1 %collective-permute-start.10 = (bf16[128,256]{1,0:T(8,128)(2,1)S(1)}, bf16[128,256]{1,0:T(8,128)(2,1)S(1)}, u32[]{:S(2)}, u32[]{:S(2)}) collective-permute-start(bf16[128,256]{1,0:T(8,128)(2,1)S(1)} %fusion.4), channel_id=1, source_target_pairs={{0,128},{16,144},{32,160},{48,176},{64,192},{80,208},{96,224},{112... | collective-permute-start | bytes 196616 | tf_op jit(solution)/shard_map/ppermute | solution.py:44
  183.4 12.8 %collective-permute-start.13 = (bf16[4,128,256]{2,1,0:T(8,128)(2,1)S(1)}, bf16[4,128,256]{2,1,0:T(8,128)(2,1)S(1)}, u32[]{:S(2)}, u32[]{:S(2)}) collective-permute-start(bf16[4,128,256]{2,1,0:T(8,128)(2,1)S(1)} %pad_maximum_fusion.refs_0_), channel_id=1, source_target_pairs={{0,16},{16,32},{32,48},{48,64},{64,80},{80,96},{96,112},{112,0},{1... | collective-permute-start | bytes 786440 | tf_op jit(solution)/shard_map/ppermute | solution.py:36
  183.7 12.5 %collective-permute-start.14 = (bf16[4,128,256]{2,1,0:T(8,128)(2,1)S(1)}, bf16[4,128,256]{2,1,0:T(8,128)(2,1)S(1)}, u32[]{:S(2)}, u32[]{:S(2)}) collective-permute-start(bf16[4,128,256]{2,1,0:T(8,128)(2,1)S(1)} %pad_maximum_fusion.refs_0_), channel_id=1, source_target_pairs={{0,112},{16,0},{32,16},{48,32},{64,48},{80,64},{96,80},{112,96},{1... | collective-permute-start | bytes 786440 | tf_op jit(solution)/shard_map/ppermute | solution.py:36
  186.7 9.5 %collective-permute-start.15 = (bf16[4,128,256]{2,1,0:T(8,128)(2,1)S(1)}, bf16[4,128,256]{2,1,0:T(8,128)(2,1)S(1)}, u32[]{:S(2)}, u32[]{:S(2)}) collective-permute-start(bf16[4,128,256]{2,1,0:T(8,128)(2,1)S(1)} %pad_maximum_fusion.refs_0_), channel_id=1, source_target_pairs={{0,32},{16,112},{32,64},{48,16},{64,96},{80,48},{96,0},{112,80},{1... | collective-permute-start | bytes 786440 | tf_op jit(solution)/shard_map/ppermute | solution.py:36
